TPU v7x, 32 devices: a whole 2x2x4 slice. The times are simulated.
32 devices in a mesh: dp: 4 (over y, x), fsdp: 8 (over z, core).
Axes of the slice: x: 2, y: 2, z: 4, core: 2. Of those that a mesh axis runs over, the one named last changes fastest.
Arguments:
- tokens: bfloat16 [40960, 512], P(('dp', 'fsdp')), may hold values from -6 to 6
- features: bfloat16 [40960, 512], P(('dp', 'fsdp')), may hold values from -6 to 6
- cameras: int32 [32], P(('dp', 'fsdp')), may hold values from 2 to 4
- cotangent: bfloat16 [40960, 512], P(('dp', 'fsdp')), may hold values from -6 to 6
- w_qkv: bfloat16 [512, 1536], P(('dp', 'fsdp')), may hold values from -0.25 to 0.25
- w_out: bfloat16 [512, 512], P(('dp', 'fsdp')), may hold values from -1 to 1
- w_up: bfloat16 [512, 3200], P(('dp', 'fsdp')), may hold values from -0.25 to 0.25
- w_down: bfloat16 [512, 3200], P(('dp', 'fsdp')), may hold values from -0.109375 to 0.109375
- w_feat: bfloat16 [512, 512], P(('dp', 'fsdp')), may hold values from -0.25 to 0.25
- b_query: float32 [512], replicated, may hold values from -3 to 3
- b_value: float32 [512], replicated, may hold values from -3 to 3
- b_out: float32 [512], replicated, may hold values from -3 to 3
- gain_first: float32 [512], replicated, may hold values from 0.5 to 1.5
- shift_first: float32 [512], replicated, may hold values from -2 to 2
- b_up: float32 [3200], replicated, may hold values from -3 to 3
- b_down: float32 [512], replicated, may hold values from -3 to 3
- gain_second: float32 [512], replicated, may hold values from 0.5 to 1.5
- shift_second: float32 [512], replicated, may hold values from -2 to 2
- b_feat: float32 [512], replicated, may hold values from -3 to 3
Outputs:
- output: bfloat16 [40960, 512], P(('dp', 'fsdp'))
- grad_tokens: bfloat16 [40960, 512], P(('dp', 'fsdp'))
- grad_features: bfloat16 [40960, 512], P(('dp', 'fsdp'))
- grad_w_qkv: float32 [512, 1536], P(('dp', 'fsdp'))
- grad_w_out: float32 [512, 512], P(('dp', 'fsdp'))
- grad_w_up: float32 [512, 3200], P(('dp', 'fsdp'))
- grad_w_down: float32 [512, 3200], P(('dp', 'fsdp'))
- grad_w_feat: float32 [512, 512], P(('dp', 'fsdp'))
- grad_b_query: float32 [512], replicated
- grad_b_value: float32 [512], replicated
- grad_b_out: float32 [512], replicated
- grad_gain_first: float32 [512], replicated
- grad_shift_first: float32 [512], replicated
- grad_b_up: float32 [3200], replicated
- grad_b_down: float32 [512], replicated
- grad_gain_second: float32 [512], replicated
- grad_shift_second: float32 [512], replicated
- grad_b_feat: float32 [512], replicated
Inputs may be any that keep to these rules, and one draw needn't show every extreme that they name: Each episode's number of cameras.
All inputs are finite; a program needn't handle non-finite values.
Results may differ from a plain program's by a relative error of at most 0.018.
The roundings to bfloat16 on the way count: a program that leaves them out, or rounds other values in their place, can miss the bound.
Values may be sent and summed in bfloat16 or wider, within the bound.
A program may use at most 320 MiB of HBM per device.

v0:
```python
import jax
import jax.numpy as jnp
from jax import lax
from jax.sharding import PartitionSpec as P

HEAD = 64
SLOTS = 1280
CAM_LEN = 300


NEG_BIG = -1000000000.0
NORM_EPS = 1e-05


def layer_norm(value, gain, shift):
    average = jnp.mean(value, axis=-1, keepdims=True)
    centered = value - average
    variance = jnp.mean(centered * centered, axis=-1, keepdims=True)
    return centered * lax.rsqrt(variance + NORM_EPS) * gain + shift


def matmul(left, right):
    return jnp.dot(left, right, preferred_element_type=jnp.float32)


def matmul_tn(left, right):
    return lax.dot_general(
        left, right, (((0,), (0,)), ((), ())), preferred_element_type=jnp.float32
    )


def matmul_nt(left, right):
    return lax.dot_general(
        left, right, (((1,), (1,)), ((), ())), preferred_element_type=jnp.float32
    )


def masked_scores(queries, key_rows, valid_keys):
    scores = jnp.einsum("qhd,khd->hqk", queries, key_rows, preferred_element_type=jnp.float32)
    return jnp.where(valid_keys[None, None, :], scores, NEG_BIG)


def attend(item_tuple):
    queries, key_rows, value_rows, valid_keys = item_tuple
    scores = masked_scores(queries, key_rows, valid_keys)
    row_top = jnp.max(scores, axis=-1, keepdims=True)
    exponent = jnp.exp(scores - row_top)
    row_total = jnp.sum(exponent, axis=-1, keepdims=True)
    attn_probs = (exponent / row_total).astype(jnp.bfloat16)
    mixed_rows = jnp.einsum(
        "hqk,khd->qhd", attn_probs, value_rows, preferred_element_type=jnp.float32
    )
    return (mixed_rows, (row_top + jnp.log(row_total))[..., 0])


def attend_back(item_tuple):
    queries, key_rows, value_rows, valid_keys, grad_mixed, log_total = item_tuple
    scores = masked_scores(queries, key_rows, valid_keys)
    attn_probs = jnp.exp(scores - log_total[..., None])
    grad_probs = jnp.einsum(
        "qhd,khd->hqk", grad_mixed, value_rows, preferred_element_type=jnp.float32
    )
    grad_values = jnp.einsum(
        "hqk,qhd->khd",
        attn_probs.astype(jnp.bfloat16),
        grad_mixed,
        preferred_element_type=jnp.float32,
    ).astype(jnp.bfloat16)
    row_inner = jnp.sum(attn_probs * grad_probs, axis=-1, keepdims=True)
    grad_scores = (attn_probs * (grad_probs - row_inner)).astype(jnp.bfloat16)
    grad_queries = jnp.einsum(
        "hqk,khd->qhd", grad_scores, key_rows, preferred_element_type=jnp.float32
    ).astype(jnp.bfloat16)
    grad_keys = jnp.einsum(
        "hqk,qhd->khd", grad_scores, queries, preferred_element_type=jnp.float32
    ).astype(jnp.bfloat16)
    return (grad_queries, grad_keys, grad_values)


def on_device(
    tokens,
    features,
    cameras,
    cotangent,
    w_qkv,
    w_out,
    w_up,
    w_down,
    w_feat,
    b_query,
    b_value,
    b_out,
    gain_first,
    shift_first,
    b_up,
    b_down,
    gain_second,
    shift_second,
    b_feat,
):
    width = tokens.shape[1]
    episodes = cameras.shape[0]
    heads = width // HEAD
    gathered = (
        lax.all_gather(w_qkv, ("dp", "fsdp"), axis=0, tiled=True),
        lax.all_gather(w_out, ("dp", "fsdp"), axis=0, tiled=True),
        lax.all_gather(w_up, ("dp", "fsdp"), axis=0, tiled=True),
        lax.all_gather(w_down, ("dp", "fsdp"), axis=0, tiled=True),
        lax.all_gather(w_feat, ("dp", "fsdp"), axis=0, tiled=True),
    )
    full_qkv, full_out, full_up, full_down, full_feat = gathered
    slot_ids = lax.broadcasted_iota(jnp.int32, (episodes, SLOTS), 1)
    limits = 2 + CAM_LEN * cameras[:, None]
    valid_keys = slot_ids < limits
    camera_rows = jnp.logical_and(slot_ids >= 2, valid_keys).astype(jnp.float32).reshape(-1, 1)
    valid_rows = valid_keys.astype(jnp.float32).reshape(-1, 1)
    memory = matmul(features, full_feat) + b_feat
    start = tokens.astype(jnp.float32) + camera_rows * memory
    start_low = start.astype(jnp.bfloat16)
    joined = matmul(start_low, full_qkv)
    queries = ((joined[:, :width] + b_query) * 0.125).astype(jnp.bfloat16)
    key_rows = joined[:, width : 2 * width].astype(jnp.bfloat16)
    value_rows = (joined[:, 2 * width :] + b_value).astype(jnp.bfloat16)
    shaped = (episodes, SLOTS, heads, HEAD)
    query_eps = queries.reshape(shaped)
    key_eps = key_rows.reshape(shaped)
    value_eps = value_rows.reshape(shaped)
    mixed_eps, log_total = lax.map(attend, (query_eps, key_eps, value_eps, valid_keys))
    mixed_low = mixed_eps.reshape(-1, width).astype(jnp.bfloat16)
    attended = matmul(mixed_low, full_out) + b_out
    normed, pull_first = jax.vjp(layer_norm, start + attended, gain_first, shift_first)
    normed_low = normed.astype(jnp.bfloat16)
    inner = matmul(normed_low, full_up) + b_up
    active_full, pull_gelu = jax.vjp(jax.nn.gelu, inner)
    active = active_full.astype(jnp.bfloat16)
    branch = matmul_nt(active, full_down) + b_down
    final, pull_second = jax.vjp(layer_norm, normed + branch, gain_second, shift_second)
    output = (valid_rows * final).astype(jnp.bfloat16)
    back_qkv, back_out, back_up, back_down, back_feat = (
        lax.all_gather(w_qkv, ("dp", "fsdp"), axis=0, tiled=True),
        lax.all_gather(w_out, ("dp", "fsdp"), axis=0, tiled=True),
        lax.all_gather(w_up, ("dp", "fsdp"), axis=0, tiled=True),
        lax.all_gather(w_down, ("dp", "fsdp"), axis=0, tiled=True),
        lax.all_gather(w_feat, ("dp", "fsdp"), axis=0, tiled=True),
    )
    grad_second, grad_gain_second, grad_shift_second = pull_second(
        valid_rows * cotangent.astype(jnp.float32)
    )
    grad_branch = grad_second.astype(jnp.bfloat16)
    grad_b_down = jnp.sum(grad_branch.astype(jnp.float32), axis=0)
    grad_w_down = matmul_tn(grad_branch, active)
    grad_active = matmul(grad_branch, back_down)
    grad_inner = pull_gelu(grad_active)[0].astype(jnp.bfloat16)
    grad_b_up = jnp.sum(grad_inner.astype(jnp.float32), axis=0)
    grad_w_up = matmul_tn(normed_low, grad_inner)
    grad_normed = grad_second + matmul_nt(grad_inner, back_up)
    grad_first, grad_gain_first, grad_shift_first = pull_first(grad_normed)
    grad_attended = grad_first.astype(jnp.bfloat16)
    grad_b_out = jnp.sum(grad_attended.astype(jnp.float32), axis=0)
    grad_w_out = matmul_tn(mixed_low, grad_attended)
    grad_mixed = matmul_nt(grad_attended, back_out).astype(jnp.bfloat16)
    grad_q, grad_k, grad_v = lax.map(
        attend_back,
        (query_eps, key_eps, value_eps, valid_keys, grad_mixed.reshape(shaped), log_total),
    )
    grad_q = (grad_q.reshape(-1, width).astype(jnp.float32) * 0.125).astype(jnp.bfloat16)
    grad_k = grad_k.reshape(-1, width)
    grad_v = grad_v.reshape(-1, width)
    grad_b_query = jnp.sum(grad_q.astype(jnp.float32), axis=0)
    grad_b_value = jnp.sum(grad_v.astype(jnp.float32), axis=0)
    grad_joined = jnp.concatenate([grad_q, grad_k, grad_v], axis=1)
    grad_w_qkv = matmul_tn(start_low, grad_joined)
    grad_start = grad_first + matmul_nt(grad_joined, back_qkv)
    grad_tokens = grad_start.astype(jnp.bfloat16)
    grad_memory = (camera_rows * grad_start).astype(jnp.bfloat16)
    grad_b_feat = jnp.sum(grad_memory.astype(jnp.float32), axis=0)
    grad_w_feat = matmul_tn(features, grad_memory)
    grad_features = matmul_nt(grad_memory, back_feat).astype(jnp.bfloat16)
    sharded = (
        lax.psum_scatter(grad_w_qkv, ("dp", "fsdp"), scatter_dimension=0, tiled=True),
        lax.psum_scatter(grad_w_out, ("dp", "fsdp"), scatter_dimension=0, tiled=True),
        lax.psum_scatter(grad_w_up, ("dp", "fsdp"), scatter_dimension=0, tiled=True),
        lax.psum_scatter(grad_w_down, ("dp", "fsdp"), scatter_dimension=0, tiled=True),
        lax.psum_scatter(grad_w_feat, ("dp", "fsdp"), scatter_dimension=0, tiled=True),
    )
    summed = lax.psum(
        (
            grad_b_query,
            grad_b_value,
            grad_b_out,
            grad_gain_first,
            grad_shift_first,
            grad_b_up,
            grad_b_down,
            grad_gain_second,
            grad_shift_second,
            grad_b_feat,
        ),
        ("dp", "fsdp"),
    )
    return (
        output,
        grad_tokens,
        grad_features,
        sharded[0],
        sharded[1],
        sharded[2],
        sharded[3],
        sharded[4],
        summed[0],
        summed[1],
        summed[2],
        summed[3],
        summed[4],
        summed[5],
        summed[6],
        summed[7],
        summed[8],
        summed[9],
    )


def solution(mesh):
    placed = (
        P(("dp", "fsdp"), None),
        P(("dp", "fsdp"), None),
        P(("dp", "fsdp")),
        P(("dp", "fsdp"), None),
        P(("dp", "fsdp"), None),
        P(("dp", "fsdp"), None),
        P(("dp", "fsdp"), None),
        P(("dp", "fsdp"), None),
        P(("dp", "fsdp"), None),
        P(),
        P(),
        P(),
        P(),
        P(),
        P(),
        P(),
        P(),
        P(),
        P(),
    )
    return jax.shard_map(
        on_device,
        mesh=mesh,
        in_specs=placed,
        out_specs=(
            P(("dp", "fsdp"), None),
            P(("dp", "fsdp"), None),
            P(("dp", "fsdp"), None),
            P(("dp", "fsdp"), None),
            P(("dp", "fsdp"), None),
            P(("dp", "fsdp"), None),
            P(("dp", "fsdp"), None),
            P(("dp", "fsdp"), None),
            P(),
            P(),
            P(),
            P(),
            P(),
            P(),
            P(),
            P(),
            P(),
            P(),
        ),
        check_vma=False,
    )
```

profile of v0, /device:TPU:0, one launch (start us, length us, event | category | flops | bytes accessed | tf_op | source)
XLA Modules:
  0.0 986.3 jit_solution(8342891181858927544)
XLA Ops:
  7.2 0.7 all-gather.4.cloned.1.call-update
  7.9 0.0 all-gather.6.cloned.1.call-start
  8.0 0.7 all-gather.6.cloned.1.call-update
  8.7 0.7 all-gather.8.cloned.1.call-update
  9.4 0.0 reduce-scatter.10.cloned.1.call-start
  10.2 45.9 %all_gather.22 = bf16[512,512]{1,0:T(8,128)(2,1)S(1)} all-gather(bf16[16,512]{1,0:T(8,128)(2,1)} %param.24), channel_id=1, replica_groups=mesh['dp'=4,'fsdp'=8] {'dp','fsdp'}, dimensions={0}, use_global_device_ids=true | all-gather | bytes 540672 | tf_op jit(solution)/shard_map/all_gather | solution.py:106
  56.0 41.7 %all_gather.20 = bf16[512,512]{1,0:T(8,128)(2,1)} all-gather(bf16[16,512]{1,0:T(8,128)(2,1)} %param.27), channel_id=1, replica_groups=mesh['dp'=4,'fsdp'=8] {'dp','fsdp'}, dimensions={0}, use_global_device_ids=true | all-gather | bytes 540672 | tf_op jit(solution)/shard_map/all_gather | solution.py:109
  97.7 1.6 copy.76
  99.4 2.4 copy.70
  101.8 3.9 fusion.15
  105.7 4.4 fusion.32
  110.2 1.2 slice.25
  111.4 2.2 fusion.25
  113.6 2.5 copy.72
  116.2 2.5 copy.73
  118.6 2.4 copy.71
  121.1 22.5 %fusion.47 = (f32[8,1280]{1,0:T(8,128)S(1)}, f32[8,1280,1280]{1,2,0:T(8,128)}) fusion(bf16[1280,8,64]{0,2,1:T(8,128)(2,1)} %bitcast.54, bf16[1280,8,64]{0,2,1:T(8,128)(2,1)} %bitcast.56, pred[1280]{0:T(1024)(128)(4,1)S(1)} %iota_compare_fusion.1), kind=kOutput, calls=%fused_computation.97 | convolution fusion | flops 1703925760 | bytes 55092480 | tf_op jit(solution)/shard_map/while/body/eval_jaxpr/qhd,khd->hqk/dot_general | solution.py:39
  143.6 17.2 %fusion = f32[8,1280]{1,0:T(8,128)S(1)} fusion(f32[8,1280,1280]{1,2,0:T(8,128)} %get-tuple-element.156, f32[8,1280]{1,0:T(8,128)S(1)} %get-tuple-element.155), kind=kLoop, calls=%fused_computation.6 | loop fusion | flops 26204160 | bytes 52510720 | tf_op jit(solution)/shard_map/while/body/eval_jaxpr/reduce_sum | solution.py:48
  160.8 19.9 %fusion.23 = bf16[8,64,1280]{2,1,0:T(8,128)(2,1)S(1)} fusion(bf16[1280,8,64]{0,2,1:T(8,128)(2,1)S(1)} %bitcast.61, f32[8,1280,1280]{1,2,0:T(8,128)} %get-tuple-element.156, f32[8,1280]{1,0:T(8,128)S(1)} %fusion, f32[8,1280]{1,0:T(8,128)S(1)} %get-tuple-element.155), kind=kOutput, calls=%fused_computation.43 | convolution fusion | flops 1717698560 | bytes 55132160 | tf_op jit(solution)/shard_map/while/body/eval_jaxpr/hqk,khd->qhd/dot_general | solution.py:50
  180.7 1.0 fusion.48
  181.8 1.5 copy-done.1
  183.3 0.3 multiply_reduce_fusion.6
  183.7 13.2 %convolution_add_fusion = f32[1280,3200]{1,0:T(8,128)} fusion(bf16[512,3200]{1,0:T(8,128)(2,1)} %all-gather.6.cloned.1.call-done, f32[3200]{0:T(1024)S(1)} %copy-done.35, f32[1280,512]{0,1:T(8,128)} %copy-done.1, f32[512]{0:T(512)S(1)} %copy-done.38, f32[512]{0:T(512)S(1)} %copy-done.31, f32[1280]{0:T(1024)S(1)} %fusion.36, ...), kind=kOutput, calls=%fused_computation.13 | convolution fusion | flops 4201676800 | bytes 22309376 | tf_op jit(solution)/shard_map/dot_general | solution.py:23
  197.0 11.8 %fusion.49 = (f32[1280]{0:T(1024)S(1)}, f32[1280,512]{0,1:T(8,128)S(1)}) fusion(f32[512]{0:T(512)S(1)} %copy-done.37, bf16[512,3200]{1,0:T(8,128)(2,1)} %all-gather.8.cloned.1.call-done, f32[1280,3200]{1,0:T(8,128)} %convolution_add_fusion, f32[512]{0:T(512)S(1)} %copy-done.38, f32[512]{0:T(512)S(1)} %copy-done.31, f32[1280]{0:T(1024)S(1)} %fusion.36, ...), kind=kOutput, calls=%fused_computation.99 | convolution fusion | flops 4235754240 | bytes 24925184 | tf_op jit(solution)/shard_map/dot_general | solution.py:33
  208.8 1.5 multiply_reduce_fusion.4
  210.3 1.8 multiply_reduce_fusion.1
  212.1 3.0 convert_reduce_fusion.2
  215.1 20.7 %convert_reduce_fusion = (f32[3200]{0:T(1024)}, bf16[1280,3200]{1,0:T(8,128)(2,1)}) fusion(f32[1280,3200]{1,0:T(8,128)} %convolution_add_fusion, bf16[1280,512]{0,1:T(8,128)(2,1)S(1)} %get-tuple-element.144, bf16[512,3200]{1,0:T(8,128)(2,1)} %all-gather.8.cloned.1.call-done), kind=kOutput, calls=%fused_computation.21 | convolution fusion | flops 4284412928 | bytes 29176320 | tf_op jit(solution)/shard_map/dot_general | solution.py:23
  235.9 9.7 multiply_reduce_fusion.2
  245.6 0.7 fusion.46
  246.3 1.4 copy-done.5
  247.7 0.9 convert_reduce_fusion.3
  248.6 1.0 copy-done.15
  249.7 1.9 fusion.50
  251.5 2.2 convolution_convert_fusion
  253.7 19.3 %convert_reduce_fusion.4 = (f32[8,64]{1,0:T(8,128)S(1)}, bf16[8,64,1280]{2,1,0:T(8,128)(2,1)}) fusion(bf16[1280,8,64]{0,2,1:T(8,128)(2,1)S(1)} %bitcast.58, f32[8,1280,1280]{1,2,0:T(8,128)} %get-tuple-element.156, f32[8,1280]{1,0:T(8,128)S(1)} %log_add_fusion), kind=kOutput, calls=%fused_computation.55 | convolution fusion | flops 1705901568 | bytes 55093248 | tf_op jit(solution)/shard_map/while/body/eval_jaxpr/hqk,qhd->khd/dot_general | solution.py:63
  273.0 37.8 %multiply_reduce_fusion = (f32[8,1280]{1,0:T(8,128)S(1)}, f32[8,1280,1280]{1,2,0:T(8,128)}) fusion(f32[8,1280,1280]{1,2,0:T(8,128)} %get-tuple-element.156, f32[8,1280]{1,0:T(8,128)S(1)} %log_add_fusion, bf16[1280,8,64]{0,2,1:T(8,128)(2,1)S(1)} %bitcast.59, bf16[1280,8,64]{0,2,1:T(8,128)(2,1)} %bitcast.60), kind=kOutput, calls=%fused_computation.2 | convolution fusion | flops 1717032960 | bytes 107560960 | tf_op jit(solution)/shard_map/while/body/eval_jaxpr/qhd,khd->hqk/dot_general | solution.py:60
  310.8 0.0 reduce-scatter.16.cloned.1.call-start
  310.8 42.7 %multiply_convert_fusion = bf16[8,1280,1280]{1,2,0:T(8,128)(2,1)} fusion(f32[8,1280,1280]{1,2,0:T(8,128)} %get-tuple-element.163, f32[8,1280,1280]{1,2,0:T(8,128)} %get-tuple-element.156, f32[8,1280]{1,0:T(8,128)S(1)} %get-tuple-element.162, f32[8,1280]{1,0:T(8,128)S(1)} %log_add_fusion), kind=kLoop, calls=%fused_computation.1 | loop fusion | flops 52428800 | bytes 131153920 | tf_op jit(solution)/shard_map/while/body/eval_jaxpr/convert_element_type | solution.py:70
  353.5 14.3 %convolution_convert_fusion.2 = bf16[8,64,1280]{2,1,0:T(8,128)(2,1)} fusion(bf16[1280,8,64]{0,2,1:T(8,128)(2,1)S(1)} %bitcast.55, bf16[8,1280,1280]{1,2,0:T(8,128)(2,1)} %multiply_convert_fusion), kind=kOutput, calls=%fused_computation.38 | convolution fusion | flops 1678376960 | bytes 28835840 | tf_op jit(solution)/shard_map/while/body/eval_jaxpr/hqk,qhd->khd/dot_general | solution.py:74
  367.9 13.7 %convert_reduce_fusion.5 = (f32[8,64]{1,0:T(8,128)S(1)}, bf16[8,64,1280]{2,1,0:T(8,128)(2,1)S(1)}) fusion(bf16[1280,8,64]{0,2,1:T(8,128)(2,1)} %bitcast.57, bf16[8,1280,1280]{1,2,0:T(8,128)(2,1)} %multiply_convert_fusion), kind=kOutput, calls=%fused_computation.56 | convolution fusion | flops 1681653248 | bytes 28837888 | tf_op jit(solution)/shard_map/while/body/eval_jaxpr/hqk,khd->qhd/dot_general | solution.py:71
  381.6 3.9 convert_reduce_fusion.1
  385.5 1.1 copy-done.40
  386.6 1.8 convolution_bitcast_fusion
  388.4 2.6 copy.92
  391.0 0.0 reduce-scatter.8.cloned.1.call-start
  391.1 6.4 fusion.30
  397.5 0.3 reduce-scatter.12.cloned.1.call-start
  397.8 0.4 copy-done.39
  398.1 11.6 %fusion.41 = f32[512,3200]{1,0:T(8,128)} fusion(bf16[1280,3200]{1,0:T(8,128)(2,1)} %get-tuple-element.170, f32[1280,512]{0,1:T(8,128)} %copy-done.1, f32[512]{0:T(512)S(1)} %copy-done.39, f32[512]{0:T(512)S(1)} %copy-done.31, f32[1280]{0:T(1024)S(1)} %fusion.36, f32[1280]{0:T(1024)S(1)} %broadcast_multiply_fusion.1), kind=kOutput, calls=%fused_computation.93 | convolution fusion | flops 4197580800 | bytes 17381376 | tf_op jit(solution)/shard_map/dot_general | solution.py:27
  409.8 0.0 reduce-scatter.14.cloned.1.call-start
  409.8 1.2 copy-done.17
  411.1 11.6 %fusion.45 = f32[512,3200]{1,0:T(8,128)} fusion(bf16[1280,512]{0,1:T(8,128)(2,1)S(1)} %copy-done.17, f32[1280,3200]{1,0:T(8,128)} %convolution_add_fusion), kind=kOutput, calls=%fused_computation.95 | convolution fusion | flops 4231168000 | bytes 24248320 | tf_op jit(solution)/shard_map/dot_general | solution.py:27
  422.8 1.3 copy-done.8
  424.1 1.5 copy.82
  425.6 0.1 reduce_sum.231
  425.7 0.1 reduce_sum.229
  425.7 2.4 copy.83
  428.2 40.9 %all-reduce = (f32[512]{0:T(512)}, f32[512]{0:T(512)}, f32[512]{0:T(512)}, f32[512]{0:T(512)}, f32[512]{0:T(512)}, /*index=5*/f32[3200]{0:T(1024)}, f32[512]{0:T(512)}, f32[512]{0:T(512)}, f32[512]{0:T(512)}, f32[512]{0:T(512)}) all-reduce(f32[512]{0:T(512)S(1)} %reduce_sum.229, ...), channel_id=1, replica_groups=mesh['dp'=4,'fsdp'=8] {'dp','fsdp'}, use_global_device_ids=true, to_apply=%region_17.18 | all-reduce | flops 7808 | bytes 62464 | tf_op jit(solution)/shard_map/psum | solution.py:186
  469.1 3.3 convolution_convert_fusion.1
  472.4 105.1 %reduce-scatter.16.cloned.1.call-done = f32[16,512]{1,0:T(8,128)} async-done(((f32[512,512]{1,0:T(8,128)}), f32[16,512]{1,0:T(8,128)}) %reduce-scatter.16.cloned.1.call-update) | async-done | bytes 32784
  577.5 103.7 %reduce-scatter.8.cloned.1.call-done = f32[16,1536]{1,0:T(8,128)} async-done(((f32[512,1536]{1,0:T(8,128)}), f32[16,1536]{1,0:T(8,128)}) %reduce-scatter.8.cloned.1.call-update) | async-done | bytes 98320 | tf_op jit(solution)/shard_map/reduce_scatter | solution.py:180
  681.2 149.5 %reduce-scatter.12.cloned.1.call-done = f32[16,3200]{1,0:T(8,128)} async-done(((f32[512,3200]{1,0:T(8,128)}), f32[16,3200]{1,0:T(8,128)}) %reduce-scatter.12.cloned.1.call-update) | async-done | bytes 204816 | tf_op jit(solution)/shard_map/reduce_scatter | solution.py:182
  830.7 148.3 %reduce-scatter.14.cloned.1.call-done = f32[16,3200]{1,0:T(8,128)} async-done(((f32[512,3200]{1,0:T(8,128)}), f32[16,3200]{1,0:T(8,128)}) %reduce-scatter.14.cloned.1.call-update) | async-done | bytes 204816 | tf_op jit(solution)/shard_map/reduce_scatter | solution.py:183
  (97 shorter events, 0.5 us)
Async XLA Ops:
  7.2 94.6 %copy-start = (bf16[1280,512]{1,0:T(8,128)(2,1)S(1)}, bf16[1280,512]{1,0:T(8,128)(2,1)}, u32[]{:S(2)}) copy-start(bf16[1280,512]{1,0:T(8,128)(2,1)} %param.20) | copy-start | bytes 3932164
  7.2 98.5 %all-gather.4.cloned.1.call-start = ((), (), s32[]{:S(2)}) async-start(), calls=%async_computation.5 | async-start | bytes 1622016 | tf_op jit(solution)/shard_map/all_gather | solution.py:105
  7.9 175.8 %all-gather.6.cloned.1.call-start = ((), (), s32[]{:S(2)}) async-start(), calls=%async_computation.6 | async-start | bytes 3379200 | tf_op jit(solution)/shard_map/all_gather | solution.py:107
  8.7 188.3 %all-gather.8.cloned.1.call-start = ((), (), s32[]{:S(2)}) async-start(), calls=%async_computation.7 | async-start | bytes 3379200 | tf_op jit(solution)/shard_map/all_gather | solution.py:108
  9.4 462.9 %reduce-scatter.10.cloned.1.call-start = ((), (), s32[]{:S(2)}) async-start(), calls=%async_computation.9 | async-start | bytes 1081344 | tf_op jit(solution)/shard_map/reduce_scatter | solution.py:181
  10.2 91.6 %copy-start.25 = (f32[1280]{0:T(1024)}, f32[1280]{0:T(1024)S(1)}, u32[]{:S(2)}) copy-start(f32[1280]{0:T(1024)S(1)} %fusion.35) | copy-start | bytes 15364
  97.7 4.1 copy-start.36
  110.2 1.2 copy-start.27
  110.2 1.2 copy-start.28
  143.6 17.2 %copy-start.7 = (bf16[1280,512]{0,1:T(8,128)(2,1)S(1)}, bf16[1280,512]{0,1:T(8,128)(2,1)}, u32[]{:S(2)}) copy-start(bf16[1280,512]{0,1:T(8,128)(2,1)} %copy.71) | copy-start | bytes 3932164
  160.8 19.9 %copy-start.4 = (f32[1280,512]{0,1:T(8,128)S(1)}, f32[1280,512]{0,1:T(8,128)}, u32[]{:S(2)}) copy-start(f32[1280,512]{0,1:T(8,128)} %fusion.15) | copy-start | bytes 7864324
  160.8 19.9 %copy-start.29 = (f32[512]{0:T(512)S(1)}, f32[512]{0:T(512)}, u32[]{:S(2)}) copy-start(f32[512]{0:T(512)} %param.30) | copy-start | bytes 6148
  180.7 1.1 copy-start.13
  181.8 1.6 copy-start.1
  181.8 1.9 copy-start.31
  181.8 1.9 copy-start.35
  181.8 2.0 copy-start.38
  183.7 13.3 %copy-start.37 = (f32[512]{0:T(512)S(1)}, f32[512]{0:T(512)}, u32[]{:S(2)}) copy-start(f32[512]{0:T(512)} %param.34) | copy-start | bytes 6148
  197.0 11.8 %copy-start.19 = (f32[512]{0:T(512)S(1)}, f32[512]{0:T(512)}, u32[]{:S(2)}) copy-start(f32[512]{0:T(512)} %param.35) | copy-start | bytes 6148
  210.3 1.8 copy-start.30
  215.1 20.7 %copy-start.16 = (bf16[1280,512]{0,1:T(8,128)(2,1)}, bf16[1280,512]{0,1:T(8,128)(2,1)S(1)}, u32[]{:S(2)}) copy-start(bf16[1280,512]{0,1:T(8,128)(2,1)S(1)} %get-tuple-element.144) | copy-start | bytes 3932164
  215.1 20.7 %copy-start.2 = (f32[1280,512]{0,1:T(8,128)S(1)}, f32[1280,512]{0,1:T(8,128)}, u32[]{:S(2)}) copy-start(f32[1280,512]{0,1:T(8,128)} %copy-done.1) | copy-start | bytes 7864324
  215.1 20.7 %copy-start.34 = (bf16[512,3200]{1,0:T(8,128)(2,1)S(1)}, bf16[512,3200]{1,0:T(8,128)(2,1)}, u32[]{:S(2)}) copy-start(bf16[512,3200]{1,0:T(8,128)(2,1)} %all-gather.6.cloned.1.call-done) | copy-start | bytes 9830404
  246.3 1.5 copy-start.5
  246.3 3.4 copy-start.14
  248.6 1.0 copy-start.15
  310.8 266.7 %reduce-scatter.16.cloned.1.call-start = ((), (), s32[]{:S(2)}) async-start(), calls=%async_computation.12 | async-start | bytes 1081344
  310.8 42.7 %copy-start.3 = (bf16[1280,512]{0,1:T(8,128)(2,1)S(1)}, bf16[1280,512]{0,1:T(8,128)(2,1)}, u32[]{:S(2)}) copy-start(bf16[1280,512]{0,1:T(8,128)(2,1)} %copy.72) | copy-start | bytes 3932164
  367.9 13.7 %copy-start.6 = (f32[1280,512]{0,1:T(8,128)S(1)}, f32[1280,512]{0,1:T(8,128)}, u32[]{:S(2)}) copy-start(f32[1280,512]{0,1:T(8,128)} %copy-done.5) | copy-start | bytes 7864324
  367.9 13.7 %copy-start.9 = (bf16[8,64,1280]{2,1,0:T(8,128)(2,1)S(1)}, bf16[8,64,1280]{2,1,0:T(8,128)(2,1)}, u32[]{:S(2)}) copy-start(bf16[8,64,1280]{2,1,0:T(8,128)(2,1)} %convolution_convert_fusion.2) | copy-start | bytes 3932164
  367.9 13.7 %copy-start.10 = (bf16[8,64,1280]{2,1,0:T(8,128)(2,1)S(1)}, bf16[8,64,1280]{2,1,0:T(8,128)(2,1)}, u32[]{:S(2)}) copy-start(bf16[8,64,1280]{2,1,0:T(8,128)(2,1)} %get-tuple-element.168) | copy-start | bytes 3932164
  367.9 13.7 %copy-start.12 = (bf16[512,1536]{1,0:T(8,128)(2,1)S(1)}, bf16[512,1536]{1,0:T(8,128)(2,1)}, u32[]{:S(2)}) copy-start(bf16[512,1536]{1,0:T(8,128)(2,1)} %all-gather.4.cloned.1.call-done) | copy-start | bytes 4718596
  367.9 13.7 %copy-start.26 = (f32[1280]{0:T(1024)S(1)}, f32[1280]{0:T(1024)}, u32[]{:S(2)}) copy-start(f32[1280]{0:T(1024)} %copy-done.25) | copy-start | bytes 15364
  381.6 4.0 copy-start.11
  385.5 1.1 copy-start.40
  391.0 290.1 %reduce-scatter.8.cloned.1.call-start = ((), (), s32[]{:S(2)}) async-start(), calls=%async_computation.8 | async-start | bytes 3244032 | tf_op jit(solution)/shard_map/reduce_scatter | solution.py:180
  397.4 0.7 copy-start.39
  397.5 433.2 %reduce-scatter.12.cloned.1.call-start = ((), (), s32[]{:S(2)}) async-start(), calls=%async_computation.10 | async-start | bytes 6758400 | tf_op jit(solution)/shard_map/reduce_scatter | solution.py:182
  409.8 1.3 copy-start.17
  409.8 569.2 %reduce-scatter.14.cloned.1.call-start = ((), (), s32[]{:S(2)}) async-start(), calls=%async_computation.11 | async-start | bytes 6758400 | tf_op jit(solution)/shard_map/reduce_scatter | solution.py:183
  422.7 1.3 copy-start.8
  424.0 4.1 copy-start.20
  424.0 4.1 copy-start.21
  424.0 4.1 copy-start.22
  424.0 4.1 copy-start.23
  424.1 4.1 copy-start.24
  424.1 4.1 copy-start.32
  424.1 4.1 copy-start.33
  424.1 45.0 %copy-start.18 = (bf16[512,512]{1,0:T(8,128)(2,1)S(1)}, bf16[512,512]{1,0:T(8,128)(2,1)}, u32[]{:S(2)}) copy-start(bf16[512,512]{1,0:T(8,128)(2,1)} %all_gather.20) | copy-start | bytes 1572868
Sparse Core Ops, SparseCore 0:
  11.0 58.2 all-gather.3
  72.1 58.7 all-gather.5
  133.8 58.2 all-gather.7
  310.9 132.8 reduce-scatter.9
  446.5 130.9 reduce-scatter.15
  583.4 97.7 reduce-scatter.7
  684.0 146.5 reduce-scatter.11
  833.5 145.3 reduce-scatter.13
where the time goes:
time: 995 us; the launch traced here: 986 us
  waiting for transfers between devices  509 us (51%)
  matrix products  235 us (24%)
  blocking collectives  128 us (13%)
  other arithmetic  70.4 us (7%)
  local copies, waits for them, and re-layouts  27.5 us (3%)
  between operations  15.7 us (2%)
    reduce_scatter x1, waiting for transfers between devices, on_device(): lax.psum_scatter(grad_w_up, ('dp', 'fsdp'), scatter_dimension=0, tiled=True)  149 us
    reduce_scatter x1, waiting for transfers between devices, on_device(): lax.psum_scatter(grad_w_down, ('dp', 'fsdp'), scatter_dimension=0, tiled=...  148 us
    unnamed x9, waiting for transfers between devices  107 us
    reduce_scatter x1, waiting for transfers between devices, on_device(): lax.psum_scatter(grad_w_qkv, ('dp', 'fsdp'), scatter_dimension=0, tiled=T...  104 us
    all_gather x1, blocking collectives, on_device(): lax.all_gather(w_out, ('dp', 'fsdp'), axis=0, tiled=True)  45.9 us
    dot_general x5, matrix products, matmul(): return jnp.dot(left, right, preferred_element_type=jnp.float32)  43.3 us
    convert_element_type x1, other arithmetic, attend_back(): grad_scores = (attn_probs * (grad_probs - row_inner)).astype(jnp.bfloat16)  42.7 us
    all_gather x1, blocking collectives, on_device(): lax.all_gather(w_feat, ('dp', 'fsdp'), axis=0, tiled=True)  41.7 us
  transfers between devices with their start and end apart: 8, of which 4 were waited for; matrix products, arithmetic and copies ran while one was open for 22% of the time, Pallas kernels for 0%

commit v1 on v0

v1 whole, which is shorter than its diff:
```python
import functools

import jax
import jax.numpy as jnp
from jax import lax
from jax.experimental import pallas as pl
from jax.experimental.pallas import tpu as pltpu
from jax.sharding import PartitionSpec as P

HEAD = 64
SLOTS = 1280
CAM_LEN = 300
CAMS_MAX = 4
NORM_EPS = 1e-05
LOG2E = 1.4426950408889634
GELU_C = 0.7978845608028654
GELU_A = 0.044715

ROWS = -(-(2 + CAM_LEN * CAMS_MAX) // 64) * 64
STEP = ROWS // 4
QBLOCKS = [(at, min(256, ROWS - at)) for at in range(0, ROWS, 256)]
MIB = 2**20

bf16 = jnp.bfloat16
f32 = jnp.float32


def dg(left, right, over_left, over_right):
    return lax.dot_general(
        left, right, (((over_left,), (over_right,)), ((), ())), preferred_element_type=f32
    )


def chunks(total, width):
    return [(at, min(width, total - at)) for at in range(0, total, width)]


def norm_parts(value):
    average = jnp.mean(value, axis=-1, keepdims=True)
    centered = value - average
    variance = jnp.mean(centered * centered, axis=-1, keepdims=True)
    scale = lax.rsqrt(variance + NORM_EPS)
    return centered * scale, scale


def norm_back(grad, unit, scale, gain):
    inside = grad * gain
    one = jnp.mean(inside, axis=-1, keepdims=True)
    two = jnp.mean(inside * unit, axis=-1, keepdims=True)
    return scale * (inside - one - unit * two)


def fold(value):
    rows, width = value.shape
    return jnp.sum(value.reshape(rows // 8, 8, width), axis=0)


def split_low(value):
    high = value.astype(bf16)
    return high, (value - high.astype(f32)).astype(bf16)


def forward_kernel(
    cameras,
    tokens,
    features,
    cotangent,
    w_feat,
    w_qkv,
    w_out,
    w_up,
    w_down,
    b_query,
    b_value,
    b_out,
    gain_first,
    shift_first,
    b_up,
    b_down,
    gain_second,
    shift_second,
    b_feat,
    output,
    start_low,
    q_rows,
    k_rows,
    v_rows,
    dmix_high,
    dmix_low,
    dots,
    grad_first,
    probs,
    grad_down,
    grad_up,
    grad_out,
    sums,
    sums_up,
    first,
    act,
    gin,
    work,
    mixed,
    mixed_low,
    inverse,
    normed_low,
    grad_branch,
    grad_att,
    q_cat,
    v_cat,
    k_cat,
    stage,
    prob_sem,
    stage_sem,
    load_sem,
):
    width = tokens.shape[1]
    hidden = w_up.shape[1]
    heads = width // HEAD
    pairs = heads // 2
    limit = 2 + CAM_LEN * cameras[0]

    def rows_of(step):
        return pl.ds(pl.multiple_of(step * STEP, 16), STEP)

    def row_ids(step):
        return step * STEP + lax.broadcasted_iota(jnp.int32, (STEP, 1), 0)

    loads = [
        pltpu.make_async_copy(
            source.at[pl.ds(0, ROWS), :], act.at[:, pl.ds(i * width, width)], load_sem.at[i]
        )
        for i, source in enumerate((features, tokens))
    ]
    for load in loads:
        load.start()
    for load in loads:
        load.wait()

    def project(step, carry):
        rows = rows_of(step)
        ids = row_ids(step)
        valid = ids < limit
        camera = jnp.logical_and(ids >= 2, valid)
        memory = dg(act[rows, :width], w_feat[...], 1, 0) + b_feat[...]
        start = act[rows, width : 2 * width].astype(f32) + jnp.where(camera, memory, 0.0)
        first[rows, :] = start
        low = start.astype(bf16)
        start_low[rows, :] = low
        joined = dg(low, w_qkv[...], 1, 0)
        q_rows[rows, :] = ((joined[:, :width] + b_query[...]) * 0.125).astype(bf16)
        keys = joined[:, width : 2 * width]
        lead = k_rows[0:16, :][0:1].astype(f32)
        k_rows[rows, :] = jnp.where(valid, keys, lead).astype(bf16)
        v_rows[rows, :] = (joined[:, 2 * width :] + b_value[...]).astype(bf16)
        return carry

    lax.fori_loop(0, 4, project, 0)

    lane_valid = lax.broadcasted_iota(jnp.int32, (1, ROWS), 1) < limit

    def prob_copy(pair, side):
        source = act if side == 0 else gin
        at = pl.ds(pl.multiple_of(lax.rem(pair, 2) * 1280, 128), 1280)
        return pltpu.make_async_copy(
            source.at[:, at], probs.at[2 * pair + side], prob_sem.at[2 * lax.rem(pair, 2) + side]
        )

    def attend(pair, carry):
        lanes = pl.ds(pl.multiple_of(pair * 128, 128), 128)

        @pl.when(pair >= 2)
        def _():
            prob_copy(pair - 2, 0).wait()
            prob_copy(pair - 2, 1).wait()

        queries = q_rows[:, lanes].astype(f32).T * LOG2E
        high, low = split_low(queries)
        none = jnp.zeros((HEAD, ROWS), bf16)
        values = jnp.where(lane_valid, v_rows[:, lanes].astype(f32).T, 0.0).astype(bf16)
        ones = jnp.broadcast_to(jnp.where(lane_valid, 1.0, 0.0), (HEAD, ROWS)).astype(bf16)
        for side in range(2):
            own = slice(side * HEAD, side * HEAD + HEAD)
            other = slice((1 - side) * HEAD, (1 - side) * HEAD + HEAD)
            q_cat[side, own, :] = high[own]
            q_cat[side, other, :] = none
            q_cat[side, 128 + side * HEAD : 128 + side * HEAD + HEAD, :] = low[own]
            q_cat[side, 128 + (1 - side) * HEAD : 128 + (1 - side) * HEAD + HEAD, :] = none
            v_cat[side, :HEAD, :] = values[own]
            v_cat[side, HEAD:, :] = ones
        keys = k_rows[:, lanes]
        k_cat[:, :128] = keys
        k_cat[:, 128:] = keys
        base = lax.rem(pair, 2) * 1280
        jobs = [(side, at, size) for side in range(2) for at, size in QBLOCKS]
        peak = {}

        def score(job, at_key, keys_here):
            side, at, size = jobs[job]
            here = slice(at_key, at_key + keys_here)
            scores = dg(k_cat[here, :], q_cat[side, :, at : at + size], 1, 0)
            work[job % 3 * 4 + at_key // STEP, :, :size] = scores
            high_here = jnp.max(scores, axis=0, keepdims=True)
            peak[job] = jnp.maximum(peak[job], high_here) if job in peak else high_here

        def weigh(job, at_key, keys_here):
            side, at, size = jobs[job]
            slot = act if side == 0 else gin
            here = slice(at_key, at_key + keys_here)
            slot[here, pl.ds(pl.multiple_of(base + at, 128), size)] = jnp.exp2(
                work[job % 3 * 4 + at_key // STEP, :, :size] - peak[job]
            ).astype(bf16)

        def mix(job):
            side, at, size = jobs[job]
            slot = act if side == 0 else gin
            weight = slot[:, pl.ds(pl.multiple_of(base + at, 128), size)]
            summed = dg(v_cat[side], weight, 1, 0)
            inv = 1.0 / summed[HEAD : HEAD + 1]
            mixed[pl.ds(pl.multiple_of(pair * 128 + side * HEAD, 8), HEAD), at : at + size] = (
                summed[:HEAD] * inv
            )
            inverse[2 * pair + side, :, at : at + size] = inv

        parts = chunks(ROWS, STEP)
        for job in (0, 1):
            for part in parts:
                score(job, *part)
        for job in range(len(jobs)):
            for part in parts:
                if job + 2 < len(jobs):
                    score(job + 2, *part)
                weigh(job, *part)
            if job >= 2:
                mix(job - 2)
            if job == len(QBLOCKS) - 1:
                prob_copy(pair, 0).start()
        mix(len(jobs) - 2)
        mix(len(jobs) - 1)
        prob_copy(pair, 1).start()
        return carry

    lax.fori_loop(0, pairs, attend, 0)
    for pair in (pairs - 2, pairs - 1):
        for side in range(2):
            prob_copy(pair, side).wait()

    mixed_low[...] = mixed[...].astype(bf16)
    for at, size in chunks(width, 256):
        cols = slice(at, at + size)
        first[:, cols] += dg(mixed_low[...], w_out[:, cols], 0, 0) + b_out[:, cols]
    sums[...] = jnp.zeros_like(sums)
    sums_up[...] = jnp.zeros_like(sums_up)
    cuts = chunks(hidden, 512)

    def feed(step, carry):
        rows = rows_of(step)
        valid = row_ids(step) < limit
        unit_first, scale_first = norm_parts(first[rows, :])
        normed = unit_first * gain_first[...] + shift_first[...]
        low = normed.astype(bf16)
        normed_low[rows, :] = low
        for at, size in cuts:
            cols = slice(at, at + size)
            inner = dg(low, w_up[:, cols], 1, 0) + b_up[:, cols]
            square = inner * inner
            half = 0.5 + 0.5 * jnp.tanh(inner * (GELU_C + (GELU_C * GELU_A) * square))
            value = inner * half
            act[rows, cols] = value.astype(bf16)
            slope = half + value * (1.0 - half) * (2 * GELU_C + (6 * GELU_C * GELU_A) * square)
            for cut, wide in chunks(size, 256):
                work[(at + cut) // 256, :, :wide] = slope[:, cut : cut + wide]
        branch = dg(act[rows, :], w_down[...], 1, 1) + b_down[...]
        unit_second, scale_second = norm_parts(normed + branch)
        final = unit_second * gain_second[...] + shift_second[...]
        output[rows, :] = jnp.where(valid, final, 0.0).astype(bf16)
        grad = jnp.where(valid, cotangent[rows, :].astype(f32), 0.0)
        sums[0] += fold(grad * unit_second)
        sums[1] += fold(grad)
        grad_second = norm_back(grad, unit_second, scale_second, gain_second[...])
        low_branch = grad_second.astype(bf16)
        grad_branch[rows, :] = low_branch
        sums[2] += fold(low_branch.astype(f32))
        for at, size in cuts:
            cols = slice(at, at + size)
            slope = [work[(at + cut) // 256, :, :wide] for cut, wide in chunks(size, 256)]
            low_inner = (
                dg(low_branch, w_down[:, cols], 1, 0) * jnp.concatenate(slope, axis=1)
            ).astype(bf16)
            gin[rows, cols] = low_inner
            sums_up[:, cols] += fold(low_inner.astype(f32))
        grad_normed = grad_second + dg(gin[rows, :], w_up[...], 1, 1)
        sums[3] += fold(grad_normed * unit_first)
        sums[4] += fold(grad_normed)
        back = norm_back(grad_normed, unit_first, scale_first, gain_first[...])
        grad_first[rows, :] = back
        low_att = back.astype(bf16)
        grad_att[rows, :] = low_att
        sums[5] += fold(low_att.astype(f32))
        return carry

    lax.fori_loop(0, 4, feed, 0)
    output[ROWS:, :] = jnp.zeros((SLOTS - ROWS, width), bf16)

    for at, size in QBLOCKS:
        cols = slice(at, at + size)
        grad_mixed = dg(w_out[...], grad_att[cols, :], 1, 1).astype(bf16).astype(f32)
        scaled = grad_mixed.reshape(heads, HEAD, size) * inverse[:, :, cols]
        dots[:, :, cols] = jnp.sum(
            scaled * mixed[:, cols].reshape(heads, HEAD, size), axis=1, keepdims=True
        )
        high, low = split_low(scaled.reshape(width, size))
        dmix_high[:, cols] = high
        dmix_low[:, cols] = low

    def weight_copy(target, at, size, slot):
        return pltpu.make_async_copy(
            stage.at[slot, :, pl.ds(0, size)], target.at[:, pl.ds(at, size)], stage_sem.at[slot]
        )

    pending = {}
    for turn, (left, right, target, (at, size)) in enumerate(
        [(grad_branch, act, grad_down, cut) for cut in cuts]
        + [(normed_low, gin, grad_up, cut) for cut in cuts]
    ):
        slot = turn % 2
        if slot in pending:
            pending[slot].wait()
        stage[slot, :, 0:size] = dg(left[...], right[:, at : at + size], 0, 0).astype(bf16)
        pending[slot] = weight_copy(target, at, size, slot)
        pending[slot].start()
    grad_out[...] = dg(mixed_low[...], grad_att[...], 1, 0).astype(bf16)
    for copy in pending.values():
        copy.wait()


def shaped(shape, dtype):
    return jax.ShapeDtypeStruct(shape, dtype)


def forward_call(cameras, tokens, features, cotangent, weights, biases):
    width = tokens.shape[1]
    hidden = weights[3].shape[1]
    heads = width // HEAD
    outs = (
        shaped((SLOTS, width), bf16),
        shaped((ROWS, width), bf16),
        shaped((ROWS, width), bf16),
        shaped((ROWS, width), bf16),
        shaped((ROWS, width), bf16),
        shaped((width, ROWS), bf16),
        shaped((width, ROWS), bf16),
        shaped((heads, 1, ROWS), f32),
        shaped((ROWS, width), f32),
        shaped((heads, ROWS, 1280), bf16),
        shaped((width, hidden), bf16),
        shaped((width, hidden), bf16),
        shaped((width, width), bf16),
        shaped((6, 8, width), f32),
        shaped((8, hidden), f32),
    )
    vmem = pl.BlockSpec(memory_space=pltpu.VMEM)
    hbm = pl.BlockSpec(memory_space=pl.ANY)
    return pl.pallas_call(
        forward_kernel,
        out_shape=outs,
        in_specs=[pl.BlockSpec(memory_space=pltpu.SMEM)] + [hbm] * 2 + [vmem] * 16,
        out_specs=tuple(hbm if i in (9, 10, 11) else vmem for i in range(15)),
        scratch_shapes=[
            pltpu.VMEM((ROWS, width), f32),
            pltpu.VMEM((ROWS, hidden), bf16),
            pltpu.VMEM((ROWS, hidden), bf16),
            pltpu.VMEM((max(12, -(-hidden // 256)), STEP, 256), f32),
            pltpu.VMEM((width, ROWS), f32),
            pltpu.VMEM((width, ROWS), bf16),
            pltpu.VMEM((heads, 1, ROWS), f32),
            pltpu.VMEM((ROWS, width), bf16),
            pltpu.VMEM((ROWS, width), bf16),
            pltpu.VMEM((ROWS, width), bf16),
            pltpu.VMEM((2, 256, ROWS), bf16),
            pltpu.VMEM((2, 128, ROWS), bf16),
            pltpu.VMEM((ROWS, 256), bf16),
            pltpu.VMEM((2, width, 512), bf16),
            pltpu.SemaphoreType.DMA((4,)),
            pltpu.SemaphoreType.DMA((2,)),
            pltpu.SemaphoreType.DMA((2,)),
        ],
        compiler_params=pltpu.CompilerParams(vmem_limit_bytes=62 * MIB),
        name="layer_forward",
    )(cameras, tokens, features, cotangent, *weights, *biases)


def backward_kernel(
    cameras,
    features,
    q_rows,
    k_rows,
    v_rows,
    dmix_high,
    dmix_low,
    dots,
    start_low,
    grad_first,
    probs,
    w_qkv,
    w_feat,
    grad_tokens,
    grad_features,
    grad_qkv,
    grad_feat,
    sums,
    feats,
    weights,
    grad_scores,
    joined,
    d_cat,
    d_rows,
    v_cat,
    k_turned,
    grad_memory,
    prob_sem,
    load_sem,
):
    width = q_rows.shape[1]
    heads = width // HEAD
    pairs = heads // 2
    limit = 2 + CAM_LEN * cameras[0]

    def prob_copy(pair, side):
        slot = 2 * lax.rem(pair, 2) + side
        return pltpu.make_async_copy(
            probs.at[2 * pair + side], weights.at[slot], prob_sem.at[slot]
        )

    for side in range(2):
        prob_copy(0, side).start()
    load = pltpu.make_async_copy(features.at[pl.ds(0, ROWS), :], feats, load_sem)
    load.start()
    sums[...] = jnp.zeros_like(sums)
    lane_valid = lax.broadcasted_iota(jnp.int32, (1, ROWS), 1) < limit
    row_valid = lax.broadcasted_iota(jnp.int32, (ROWS, 1), 0) < limit

    def attend_back(pair, carry):
        lanes = pl.ds(pl.multiple_of(pair * 128, 128), 128)

        @pl.when(pair + 1 < pairs)
        def _():
            prob_copy(pair + 1, 0).start()
            prob_copy(pair + 1, 1).start()

        both = pl.ds(pl.multiple_of(pair * 128, 128), 128)
        high = dmix_high[both, :]
        low = dmix_low[both, :]
        none = jnp.zeros((HEAD, ROWS), bf16)
        for side in range(2):
            own = slice(side * HEAD, side * HEAD + HEAD)
            mine, its = side * HEAD, (1 - side) * HEAD
            d_cat[side, mine : mine + HEAD, :] = high[own]
            d_cat[side, its : its + HEAD, :] = none
            d_cat[side, 128 + mine : 128 + mine + HEAD, :] = low[own]
            d_cat[side, 128 + its : 128 + its + HEAD, :] = none
        d_rows[:, :128] = high.astype(f32).T.astype(bf16)
        d_rows[:, 128:] = low.astype(f32).T.astype(bf16)
        values = v_rows[:, lanes]
        v_cat[:, :128] = values
        v_cat[:, 128:] = values
        k_turned[...] = jnp.where(lane_valid, k_rows[:, lanes].astype(f32).T, 0.0).astype(bf16)
        base = 2 * lax.rem(pair, 2)
        jobs = [(side, at, size) for side in range(2) for at, size in QBLOCKS]
        parts = chunks(ROWS, STEP)
        turned = {0: [], 1: []}
        wide = {}

        def slope(job):
            side, at, size = jobs[job]
            offset = dots[2 * pair + side, :, at : at + size]
            for at_key, keys_here in parts:
                here = slice(at_key, at_key + keys_here)
                grad = dg(v_cat[here, :], d_cat[side, :, at : at + size], 1, 0) - offset
                weight = weights[base + side, here, at : at + size].astype(f32)
                grad_scores[side, here, at : at + size] = (weight * grad).astype(bf16)

        def queries(job):
            side, at, size = jobs[job]
            turned[side].append(
                dg(k_turned[...], grad_scores[side, :, at : at + size], 1, 0)[
                    side * HEAD : side * HEAD + HEAD
                ]
            )

        def spread(side, part):
            here = slice(part[0], part[0] + part[1])
            value = dg(weights[base + side, here, :ROWS], d_rows[...], 1, 0)
            value = value[:, :128] + value[:, 128:]
            key = dg(grad_scores[side, here, :ROWS], q_rows[:, lanes], 1, 0)
            wide[side, part] = (value, key)

        for side in range(2):
            prob_copy(pair, side).wait()
        for job in range(len(jobs)):
            slope(job)
            if job >= 1:
                queries(job - 1)
            if job > len(QBLOCKS):
                side_job = job - len(QBLOCKS) - 1
                if side_job < len(parts):
                    spread(0, parts[side_job])
        queries(len(jobs) - 1)
        first_lane = lax.broadcasted_iota(jnp.int32, (STEP, 128), 1) < HEAD
        for part in parts:
            spread(1, part)
            here = slice(part[0], part[0] + part[1])
            keep = row_valid[here]
            for which, at in ((0, 2 * width), (1, width)):
                value = jnp.where(first_lane, wide[0, part][which], wide[1, part][which])
                value = jnp.where(keep, value, 0.0).astype(bf16)
                joined[here, pl.ds(pl.multiple_of(at + pair * 128, 128), 128)] = value
        query = jnp.concatenate(
            [jnp.concatenate(turned[0], axis=1), jnp.concatenate(turned[1], axis=1)], axis=0
        )
        joined[:, lanes] = (query.astype(bf16).astype(f32).T * 0.125).astype(bf16)
        return carry

    lax.fori_loop(0, pairs, attend_back, 0)
    load.wait()

    def project_back(step, carry):
        rows = pl.ds(pl.multiple_of(step * STEP, 16), STEP)
        ids = step * STEP + lax.broadcasted_iota(jnp.int32, (STEP, 1), 0)
        camera = jnp.logical_and(ids >= 2, ids < limit)
        part = joined[rows, :]
        sums[0] += fold(part[:, :width].astype(f32))
        sums[1] += fold(part[:, 2 * width :].astype(f32))
        grad_start = grad_first[rows, :] + dg(part, w_qkv[...], 1, 1)
        grad_tokens[rows, :] = grad_start.astype(bf16)
        low = jnp.where(camera, grad_start, 0.0).astype(bf16)
        grad_memory[rows, :] = low
        sums[2] += fold(low.astype(f32))
        grad_features[rows, :] = dg(low, w_feat[...], 1, 1).astype(bf16)
        return carry

    lax.fori_loop(0, 4, project_back, 0)
    grad_tokens[ROWS:, :] = jnp.zeros((SLOTS - ROWS, width), bf16)
    grad_features[ROWS:, :] = jnp.zeros((SLOTS - ROWS, width), bf16)
    for at, size in chunks(3 * width, 512):
        cols = slice(at, at + size)
        grad_qkv[:, cols] = dg(start_low[...], joined[:, cols], 0, 0).astype(bf16)
    grad_feat[...] = dg(feats[...], grad_memory[...], 0, 0).astype(bf16)


def backward_call(cameras, features, saved, w_qkv, w_feat):
    width = features.shape[1]
    heads = width // HEAD
    outs = (
        shaped((SLOTS, width), bf16),
        shaped((SLOTS, width), bf16),
        shaped((width, 3 * width), bf16),
        shaped((width, width), bf16),
        shaped((3, 8, width), f32),
    )
    vmem = pl.BlockSpec(memory_space=pltpu.VMEM)
    hbm = pl.BlockSpec(memory_space=pl.ANY)
    return pl.pallas_call(
        backward_kernel,
        out_shape=outs,
        in_specs=[pl.BlockSpec(memory_space=pltpu.SMEM), hbm] + [vmem] * 8 + [hbm] + [vmem] * 2,
        out_specs=(vmem,) * 5,
        scratch_shapes=[
            pltpu.VMEM((ROWS, width), bf16),
            pltpu.VMEM((4, ROWS, 1280), bf16),
            pltpu.VMEM((2, ROWS, 1280), bf16),
            pltpu.VMEM((ROWS, 3 * width), bf16),
            pltpu.VMEM((2, 256, ROWS), bf16),
            pltpu.VMEM((ROWS, 256), bf16),
            pltpu.VMEM((ROWS, 256), bf16),
            pltpu.VMEM((128, ROWS), bf16),
            pltpu.VMEM((ROWS, width), bf16),
            pltpu.SemaphoreType.DMA((4,)),
            pltpu.SemaphoreType.DMA(()),
        ],
        compiler_params=pltpu.CompilerParams(vmem_limit_bytes=62 * MIB),
        name="layer_backward",
    )(cameras, features, *saved, w_qkv, w_feat)


MESH = pl.DeviceIdType.MESH
GATHER_MSGS = 11


def place():
    dp = lax.axis_index("dp")
    fs = lax.axis_index("fsdp")
    return dp // 2, dp % 2, fs // 2, fs % 2


def device(y, x, z, c):
    return (y * 2 + x, z * 2 + c)


def neighbours():
    y, x, z, c = place()
    around = [device(y, x, (z + k) % 4, c) for k in (1, 2, 3)]
    return around + [device(y, 1 - x, z, c), device(1 - y, x, z, c), device(y, x, z, 1 - c)]


def greet():
    barrier = pltpu.get_barrier_semaphore()
    peers = neighbours()
    for peer in peers:
        pl.semaphore_signal(barrier, inc=1, device_id=peer, device_id_type=MESH)
    pl.semaphore_wait(barrier, len(peers))


class Gather:
    def __init__(self, shard, whole, send, recv, local, group):
        self.shard, self.whole, self.send, self.recv = shard, whole, send, recv
        self.local, self.group = local, group
        self.sent = []

    def copy(self, msg, source, target, peer):
        return pltpu.make_async_remote_copy(
            src_ref=source,
            dst_ref=target,
            send_sem=self.send.at[self.group, msg],
            recv_sem=self.recv.at[self.group, msg],
            device_id=peer,
            device_id_type=MESH,
        )

    def push(self, msg, part, peer):
        copy = self.copy(msg, part, part, peer)
        copy.start()
        self.sent.append(copy)

    def arrived(self, msg, part):
        self.copy(msg, part, part, self.nobody).wait_recv()

    def stage(self, number):
        y, x, z, c = place()
        self.nobody = device(y, x, z, 1 - c)
        whole = self.whole
        dp, dp_x, dp_y, dp_d = y * 2 + x, y * 2 + 1 - x, (1 - y) * 2 + x, (1 - y) * 2 + 1 - x
        to_x, to_y, to_c = device(y, 1 - x, z, c), device(1 - y, x, z, c), device(y, x, z, 1 - c)
        if number == 0:
            own = whole.at[dp, z, c]
            keep = pltpu.make_async_copy(self.shard, own, self.local.at[self.group])
            keep.start()
            for k in (1, 2, 3):
                copy = self.copy(k - 1, self.shard, own, device(y, x, (z + k) % 4, c))
                copy.start()
                self.sent.append(copy)
            keep.wait()
        elif number == 1:
            for k in (1, 2, 3):
                self.arrived(k - 1, whole.at[dp, (z + 4 - k) % 4, c])
            column = whole.at[dp, :, c]
            self.push(3, column, to_x)
            self.push(4, column, to_y)
            self.push(7, column, to_c)
        elif number == 2:
            self.arrived(3, whole.at[dp_x, :, c])
            self.push(5, whole.at[dp_x, pl.ds(0, 2), c], to_y)
            self.arrived(4, whole.at[dp_y, :, c])
            self.push(6, whole.at[dp_y, pl.ds(2, 2), c], to_x)
            self.push(8, whole.at[dp_x, :, c], to_c)
            self.push(9, whole.at[dp_y, :, c], to_c)
        elif number == 3:
            self.arrived(5, whole.at[dp_d, pl.ds(0, 2), c])
            self.arrived(6, whole.at[dp_d, pl.ds(2, 2), c])
            self.push(10, whole.at[dp_d, :, c], to_c)
        elif number == 4:
            for msg, place_dp in ((7, dp), (8, dp_x), (9, dp_y), (10, dp_d)):
                self.arrived(msg, whole.at[place_dp, :, 1 - c])
        elif number == 5:
            for copy in self.sent:
                copy.wait_send()


class Reduce:
    def __init__(self, part, out, bufs, send, recv, group):
        self.part, self.out, self.send, self.recv, self.group = part, out, send, recv, group
        self.half, self.diag, self.side, self.line = bufs
        self.sent = []

    copy = Gather.copy

    def push(self, msg, source, target, peer):
        copy = self.copy(msg, source, target, peer)
        copy.start()
        self.sent.append(copy)

    def arrived(self, msg, target):
        self.copy(msg, target, target, self.nobody).wait_recv()

    def add(self, target, *sources):
        total = sources[0][...].astype(f32)
        for source in sources[1:]:
            total = total + source[...].astype(f32)
        target[...] = total.astype(target.dtype)

    def stage(self, number):
        y, x, z, c = place()
        self.nobody = device(y, x, z, 1 - c)
        dp, dp_x, dp_y, dp_d = y * 2 + x, y * 2 + 1 - x, (1 - y) * 2 + x, (1 - y) * 2 + 1 - x
        to_x, to_y, to_c = device(y, 1 - x, z, c), device(1 - y, x, z, c), device(y, x, z, 1 - c)
        part, half = self.part, self.half
        if number == 0:
            for msg, at in ((0, dp_d), (1, dp_x), (2, dp_y), (3, dp)):
                self.push(msg, part.at[at, :, 1 - c], half.at[at], to_c)
        elif number == 1:
            self.arrived(0, half.at[dp_d])
            self.add(half.at[dp_d], half.at[dp_d], part.at[dp_d, :, c])
            self.push(4, half.at[dp_d, pl.ds(0, 2)], self.diag.at[0], to_x)
            self.push(5, half.at[dp_d, pl.ds(2, 2)], self.diag.at[1], to_y)
            self.arrived(1, half.at[dp_x])
            self.add(half.at[dp_x], half.at[dp_x], part.at[dp_x, :, c])
            self.arrived(2, half.at[dp_y])
            self.add(half.at[dp_y], half.at[dp_y], part.at[dp_y, :, c])
        elif number == 2:
            self.arrived(5, self.diag.at[1])
            late = half.at[dp_x, pl.ds(2, 2)]
            self.add(late, late, self.diag.at[1])
            self.push(6, half.at[dp_x], self.side.at[0], to_x)
            self.arrived(4, self.diag.at[0])
            late = half.at[dp_y, pl.ds(0, 2)]
            self.add(late, late, self.diag.at[0])
            self.push(7, half.at[dp_y], self.side.at[1], to_y)
            self.arrived(3, half.at[dp])
            self.add(half.at[dp], half.at[dp], part.at[dp, :, c])
        elif number == 3:
            self.arrived(6, self.side.at[0])
            self.arrived(7, self.side.at[1])
            self.add(half.at[dp], half.at[dp], self.side.at[0], self.side.at[1])
            for k in (1, 2, 3):
                self.push(
                    7 + k, half.at[dp, (z + k) % 4], self.line.at[k - 1], device(y, x, (z + k) % 4, c)
                )
        elif number == 4:
            for k in (1, 2, 3):
                self.arrived(7 + k, self.line.at[k - 1])
            self.add(self.out, half.at[dp, z], self.line.at[0], self.line.at[1], self.line.at[2])
        elif number == 5:
            for copy in self.sent:
                copy.wait_send()


class Total:
    def __init__(self, value, out, bufs, send, recv, group):
        self.value, self.out, self.send, self.recv, self.group = value, out, send, recv, group
        self.mine, self.theirs = bufs
        self.sent = []

    copy = Gather.copy

    def stage(self, number):
        y, x, z, c = place()
        self.nobody = device(y, x, z, 1 - c)
        peers = [
            device(y, x, z, 1 - c),
            device(y, 1 - x, z, c),
            device(1 - y, x, z, c),
            device(y, x, z + 1 - 2 * (z % 2), c),
            device(y, x, (z + 2) % 4, c),
        ]
        mine, theirs = self.mine, self.theirs
        if number == 0:
            mine[0] = self.value[...]
        elif number <= 5:
            at = number - 1
            self.copy(at, mine.at[at], theirs.at[at], self.nobody).wait_recv()
            if number < 5:
                mine[number] = mine[at] + theirs[at]
            else:
                self.out[...] = mine[at] + theirs[at]
        if number < 5:
            copy = self.copy(number, mine.at[number], theirs.at[number], peers[number])
            copy.start()
            self.sent.append(copy)
        if number == 6:
            for copy in self.sent:
                copy.wait_send()


def in_turn(groups, last):
    for turn in range(len(groups) + last):
        for at, group in enumerate(groups):
            if 0 <= turn - at <= last:
                group.stage(turn - at)


def gather_kernel(*refs):
    shards, wholes, (send, recv, local) = refs[:5], refs[5:10], refs[10:]
    greet()
    groups = [
        Gather(shard, whole, send, recv, local, i)
        for i, (shard, whole) in enumerate(zip(shards, wholes))
    ]
    in_turn(groups, 5)


def gather_call(weights):
    vmem = pl.BlockSpec(memory_space=pltpu.VMEM)
    outs = tuple(shaped((4, 4, 2) + w.shape, bf16) for w in weights)
    wholes = pl.pallas_call(
        gather_kernel,
        out_shape=outs,
        in_specs=[vmem] * 5,
        out_specs=(vmem,) * 5,
        scratch_shapes=[
            pltpu.SemaphoreType.DMA((5, GATHER_MSGS)),
            pltpu.SemaphoreType.DMA((5, GATHER_MSGS)),
            pltpu.SemaphoreType.DMA((5,)),
        ],
        compiler_params=pltpu.CompilerParams(
            collective_id=0, has_side_effects=True, vmem_limit_bytes=62 * MIB
        ),
        name="gather_weights",
    )(*weights)
    return tuple(whole.reshape(-1, whole.shape[-1]) for whole in wholes)


def reduce_bufs(columns, rows):
    return [
        pltpu.VMEM((4, 4, rows, columns), bf16),
        pltpu.VMEM((2, 2, rows, columns), bf16),
        pltpu.VMEM((2, 4, rows, columns), bf16),
        pltpu.VMEM((3, rows, columns), bf16),
    ]


def reduce_kernel(*refs):
    parts, small, outs, small_out, bufs = refs[:5], refs[5], refs[6:11], refs[11], refs[12:-2]
    send, recv = refs[-2:]
    greet()
    groups = [
        Reduce(parts[i], outs[i], bufs[4 * i : 4 * i + 4], send, recv, i) for i in range(5)
    ]
    groups.append(Total(small, small_out, bufs[20:22], send, recv, 5))
    in_turn(groups, 6)


def reduce_call(grads, small):
    vmem = pl.BlockSpec(memory_space=pltpu.VMEM)
    rows = grads[0].shape[0] // 32
    parts = [grad.reshape(4, 4, 2, rows, grad.shape[1]) for grad in grads]
    bufs = [buf for grad in grads for buf in reduce_bufs(grad.shape[1], rows)]
    bufs += [pltpu.VMEM((5,) + small.shape, f32)] * 2
    return pl.pallas_call(
        reduce_kernel,
        out_shape=tuple(shaped((rows, grad.shape[1]), f32) for grad in grads)
        + (shaped(small.shape, f32),),
        in_specs=[vmem] * 6,
        out_specs=(vmem,) * 6,
        scratch_shapes=bufs
        + [pltpu.SemaphoreType.DMA((6, GATHER_MSGS)), pltpu.SemaphoreType.DMA((6, GATHER_MSGS))],
        compiler_params=pltpu.CompilerParams(
            collective_id=1, has_side_effects=True, vmem_limit_bytes=62 * MIB
        ),
        name="reduce_gradients",
    )(*parts, small)


AXES = ("dp", "fsdp")


def on_device(
    fast,
    tokens,
    features,
    cameras,
    cotangent,
    w_qkv,
    w_out,
    w_up,
    w_down,
    w_feat,
    *biases,
):
    width = tokens.shape[1]
    hidden = w_up.shape[1]
    biases = [bias.reshape(1, -1) for bias in biases]
    shards = (w_feat, w_qkv, w_out, w_up, w_down)
    if fast:
        weights = gather_call(shards)
    else:
        weights = tuple(lax.all_gather(w, AXES, axis=0, tiled=True) for w in shards)
    (
        output,
        start_low,
        q_rows,
        k_rows,
        v_rows,
        dmix_high,
        dmix_low,
        dots,
        grad_first,
        probs,
        grad_down,
        grad_up,
        grad_out,
        sums,
        sums_up,
    ) = forward_call(cameras, tokens, features, cotangent, weights, biases)
    saved = (q_rows, k_rows, v_rows, dmix_high, dmix_low, dots, start_low, grad_first, probs)
    grad_tokens, grad_features, grad_qkv, grad_feat, sums_back = backward_call(
        cameras, features, saved, weights[1], weights[0]
    )
    grads = (grad_down, grad_up, grad_out, grad_qkv, grad_feat)
    small = jnp.concatenate(
        [
            jnp.sum(sums, axis=1).reshape(-1),
            jnp.sum(sums_back, axis=1).reshape(-1),
            jnp.sum(sums_up, axis=0),
        ]
    )
    lines = -(-small.shape[0] // 1024) * 8
    small = jnp.pad(small, (0, lines * 128 - small.shape[0])).reshape(lines, 128)
    if fast:
        *grads, small = reduce_call(grads, small)
    else:
        grads = [
            lax.psum_scatter(
                lax.optimization_barrier(grad.astype(f32)), AXES, scatter_dimension=0, tiled=True
            )
            for grad in grads
        ]
        small = lax.psum(small, AXES)
    small = small.reshape(-1)
    rows = small[: 9 * width].reshape(9, width)
    grad_b_up = small[9 * width : 9 * width + hidden]
    grad_down, grad_up, grad_out, grad_qkv, grad_feat = grads
    return (
        output,
        grad_tokens,
        grad_features,
        grad_qkv,
        grad_out,
        grad_up,
        grad_down,
        grad_feat,
        rows[6],
        rows[7],
        rows[5],
        rows[3],
        rows[4],
        grad_b_up,
        rows[2],
        rows[0],
        rows[1],
        rows[8],
    )


def solution(mesh):
    split = P(AXES, None)
    fast = mesh.shape["dp"] == 4 and mesh.shape["fsdp"] == 8
    return jax.shard_map(
        functools.partial(on_device, fast),
        mesh=mesh,
        in_specs=(split, split, P(AXES), split) + (split,) * 5 + (P(),) * 10,
        out_specs=(split,) * 8 + (P(),) * 10,
        check_vma=False,
    )
```

time: 995 us -> 271 us (0.27)
  waiting for transfers between devices: 509 us -> 0 us
  Pallas kernels: 0 us -> 254 us
  matrix products: 235 us -> 0 us
  blocking collectives: 128 us -> 0 us
  other arithmetic: 70.4 us -> 3.3 us
  local copies, waits for them, and re-layouts: 27.5 us -> 11.6 us
  between operations: 15.7 us -> 1.35 us
    reduce_scatter x4 -> x0, waiting for transfers between devices: 401 us -> none  [the longest x1 149 us: on_device(): lax.psum_scatter(grad_w_up, ('dp', 'fsdp'), scatter_dimension=0, tiled=True)]
    pallas_call x0 -> x4, Pallas kernels: none -> 254 us  [the longest x1 76.1 us: forward_call(): pl.pallas_call(forward_kernel, out_shape=outs, in_specs=[pl.BlockSpec(mem...]
    dot_general x21 -> x0, matrix products: 235 us -> none  [the longest x5 43.3 us: matmul(): return jnp.dot(left, right, preferred_element_type=jnp.float32)]
    unnamed x9 -> x0, waiting for transfers between devices: 107 us -> none
    all_gather x2 -> x0, blocking collectives: 87.6 us -> none  [the longest x1 45.9 us: on_device(): lax.all_gather(w_out, ('dp', 'fsdp'), axis=0, tiled=True)]
    convert_element_type x4 -> x0, other arithmetic: 44.9 us -> none  [the longest x1 42.7 us: attend_back(): grad_scores = (attn_probs * (grad_probs - row_inner)).astype(jnp.bfloat16)]
    psum x1 -> x0, blocking collectives: 40.9 us -> none  [on_device(): lax.psum((grad_b_query, grad_b_value, grad_b_out, grad_gain_first, grad_s...]
    reduce_sum x7 -> x3, other arithmetic: 25.4 us -> 2.68 us  [the longest x1 0.93 us: on_device(): jnp.sum(sums_up, axis=0)]
  transfers between devices with their start and end apart: 8 -> 0, of which waited for: 4 -> 0; matrix products, arithmetic and copies ran while one was open for 22% -> 0% of each run, Pallas kernels for 0% -> 0%
where the time goes in v1:
time: 271 us; the launch traced here: 270 us
  Pallas kernels  254 us (94%)
  local copies, waits for them, and re-layouts  11.6 us (4%)
  other arithmetic  3.3 us (1%)
    pallas_call x1, Pallas kernels, forward_call(): pl.pallas_call(forward_kernel, out_shape=outs, in_specs=[pl.BlockSpec(mem...  76.1 us
    pallas_call x1, Pallas kernels, reduce_call(): pl.pallas_call(reduce_kernel, out_shape=tuple((shaped((rows, grad.shape[1...  73.4 us
    pallas_call x1, Pallas kernels, gather_call(): pl.pallas_call(gather_kernel, out_shape=outs, in_specs=[vmem] * 5, out_sp...  62.8 us
    pallas_call x1, Pallas kernels, backward_call(): pl.pallas_call(backward_kernel, out_shape=outs, in_specs=[pl.BlockSpec(me...  41.5 us
    unnamed x5, local copies, waits for them, and re-layouts  7.53 us

profile of v1, /device:TPU:0, one launch (start us, length us, event | category | flops | bytes accessed | tf_op | source)
XLA Modules:
  0.0 270.0 jit_solution(12528349208869228747)
XLA Ops:
  1.3 1.3 reshape.138.b_up
  2.6 62.8 %gather_weights.1 = (bf16[4,4,2,16,512]{4,3,2,1,0:T(8,128)(2,1)}, bf16[4,4,2,16,1536]{4,3,2,1,0:T(8,128)(2,1)}, bf16[4,4,2,16,512]{4,3,2,1,0:T(8,128)(2,1)}, bf1...) custom-call(bf16[16,512]{1,0:T(8,128)(2,1)} %refs_0_.1, bf16[16,1536]{1,0:T(8,128)(2,1)} %refs_1_.1, ...), custom_call_target="tpu_custom_call" | custom-call | tf_op jit(solution)/shard_map/gather_weights/pallas_call | solution.py:803
  65.4 76.1 %layer_forward.1 = (bf16[1280,512]{1,0:T(8,128)(2,1)}, bf16[1216,512]{1,0:T(8,128)(2,1)}, bf16[1216,512]{1,0:T(8,128)(2,1)}, bf16[1216,512]{1,0:T(8,128)(2,1)}, ...) custom-call(s32[1]{0:T(128)S(6)} %copy.42.cameras, ...), custom_call_target="tpu_custom_call" | custom-call | tf_op jit(solution)/shard_map/layer_forward/pallas_call | solution.py:363
  141.5 0.9 reduce_sum.27
  142.5 0.9 reduce_sum.29
  143.4 41.5 %layer_backward.1 = (bf16[1280,512]{1,0:T(8,128)(2,1)}, bf16[1280,512]{1,0:T(8,128)(2,1)}, bf16[512,1536]{1,0:T(8,128)(2,1)}, bf16[512,512]{1,0:T(8,128)(2,1)}, f32[3,8,512]{2,1,0:T(8,128)}) custom-call(s32[1]{0:T(128)S(6)} %copy.42.cameras, bf16[1280,512]{1,0:T(8,128)(2,1)} %features.3, bf16[1216,512]{1,0:T(8,128)(2,1)} %get-tuple-element.55.q_rows, ...), custom_call_target="tpu_custom_call" | custom-call | tf_op jit(solution)/shard_map/layer_backward/pallas_call | solution.py:562
  184.9 0.8 reduce_sum.28
  185.7 0.6 fusion.refs_5_
  186.3 73.4 %reduce_gradients.1 = (f32[16,3200]{1,0:T(8,128)}, f32[16,3200]{1,0:T(8,128)}, f32[16,512]{1,0:T(8,128)}, f32[16,1536]{1,0:T(8,128)}, f32[16,512]{1,0:T(8,128)}, /*index=5*/f32[64,128]{1,0:T(8,128)}) custom-call(bf16[4,4,2,16,3200]{4,3,2,1,0:T(8,128)(2,1)} %bitcast.43, bf16[4,4,2,16,3200]{4,3,2,1,0:T(8,128)(2,1)} %bitcast.44, ...), custom_call_target="tpu_custom_call" | custom-call | tf_op jit(solution)/shard_map/reduce_gradients/pallas_call | solution.py:847
  259.7 1.3 slice_bitcast_fusion
  261.0 1.4 slice_bitcast_fusion.1
  262.4 1.5 copy.43
  264.0 1.4 copy.44
  265.3 1.6 copy.45
  267.0 1.6 copy.46
  268.6 1.4 copy.47
  (2 shorter events, 0.0 us)

commit v2 on v1

v2 whole, which is shorter than its diff:
```python
import functools

import jax
import jax.numpy as jnp
from jax import lax
from jax.experimental import pallas as pl
from jax.experimental.pallas import tpu as pltpu
from jax.sharding import PartitionSpec as P

HEAD = 64
SLOTS = 1280
CAM_LEN = 300
CAMS_MAX = 4
NORM_EPS = 1e-05
LOG2E = 1.4426950408889634
GELU_C = 0.7978845608028654
GELU_A = 0.044715

ROWS = -(-(2 + CAM_LEN * CAMS_MAX) // 64) * 64
STEP = ROWS // 4
QBLOCKS = [(at, min(256, ROWS - at)) for at in range(0, ROWS, 256)]
MIB = 2**20

bf16 = jnp.bfloat16
f32 = jnp.float32


def dg(left, right, over_left, over_right):
    return lax.dot_general(
        left, right, (((over_left,), (over_right,)), ((), ())), preferred_element_type=f32
    )


def chunks(total, width):
    return [(at, min(width, total - at)) for at in range(0, total, width)]


def norm_parts(value):
    average = jnp.mean(value, axis=-1, keepdims=True)
    centered = value - average
    variance = jnp.mean(centered * centered, axis=-1, keepdims=True)
    scale = lax.rsqrt(variance + NORM_EPS)
    return centered * scale, scale


def norm_back(grad, unit, scale, gain):
    inside = grad * gain
    one = jnp.mean(inside, axis=-1, keepdims=True)
    two = jnp.mean(inside * unit, axis=-1, keepdims=True)
    return scale * (inside - one - unit * two)


def fold(value):
    rows, width = value.shape
    return jnp.sum(value.reshape(rows // 8, 8, width), axis=0)


def split_low(value):
    high = value.astype(bf16)
    return high, (value - high.astype(f32)).astype(bf16)


MESH = pl.DeviceIdType.MESH
GATHER_MSGS = 11


def place():
    dp = lax.axis_index("dp")
    fs = lax.axis_index("fsdp")
    return dp // 2, dp % 2, fs // 2, fs % 2


def device(y, x, z, c):
    return (y * 2 + x, z * 2 + c)


def neighbours():
    y, x, z, c = place()
    around = [device(y, x, (z + k) % 4, c) for k in (1, 2, 3)]
    return around + [device(y, 1 - x, z, c), device(1 - y, x, z, c), device(y, x, z, 1 - c)]


def greet():
    barrier = pltpu.get_barrier_semaphore()
    peers = neighbours()
    for peer in peers:
        pl.semaphore_signal(barrier, inc=1, device_id=peer, device_id_type=MESH)
    pl.semaphore_wait(barrier, len(peers))


class Gather:
    def __init__(self, shard, whole, cols, send, recv, local, group):
        self.shard, self.whole, self.cols, self.send, self.recv = shard, whole, cols, send, recv
        self.local, self.group = local, group

    def copy(self, msg, source, target, peer):
        return pltpu.make_async_remote_copy(
            src_ref=source,
            dst_ref=target,
            send_sem=self.send.at[self.group, msg],
            recv_sem=self.recv.at[self.group, msg],
            device_id=peer,
            device_id_type=MESH,
        )

    def stage(self, number):
        y, x, z, c = place()
        at_x, at_y, at_d, at = y * 2 + 1 - x, (1 - y) * 2 + x, (1 - y) * 2 + 1 - x, y * 2 + x
        to_x, to_y, to_c = device(y, 1 - x, z, c), device(1 - y, x, z, c), device(y, x, z, 1 - c)
        cols = pl.ds(*self.cols)
        whole = lambda dp, line, core: self.whole.at[dp, line, core, :, cols]
        own = whole(at, z, c)
        shard = self.shard.at[:, cols]
        every, low, high = slice(None), pl.ds(0, 2), pl.ds(2, 2)
        out = [(shard, own, device(y, x, (z + k) % 4, c)) for k in (1, 2, 3)] + [
            (part, part, peer)
            for part, peer in (
                (whole(at, every, c), to_x),
                (whole(at, every, c), to_y),
                (whole(at_x, low, c), to_y),
                (whole(at_y, high, c), to_x),
                (whole(at, every, c), to_c),
                (whole(at_x, every, c), to_c),
                (whole(at_y, every, c), to_c),
                (whole(at_d, every, c), to_c),
            )
        ]
        arrived = lambda msg, part: self.copy(msg, part, part, to_c).wait_recv()
        start = lambda msg: self.copy(msg, *out[msg]).start()
        if number == 0:
            keep = pltpu.make_async_copy(shard, own, self.local.at[self.group])
            keep.start()
            for msg in (0, 1, 2):
                start(msg)
            keep.wait()
        elif number == 1:
            for k in (1, 2, 3):
                arrived(k - 1, whole(at, (z + 4 - k) % 4, c))
            for msg in (3, 4, 7):
                start(msg)
        elif number == 2:
            arrived(3, whole(at_x, every, c))
            start(5)
            arrived(4, whole(at_y, every, c))
            for msg in (6, 8, 9):
                start(msg)
        elif number == 3:
            arrived(5, whole(at_d, low, c))
            arrived(6, whole(at_d, high, c))
            start(10)
        elif number == 4:
            for msg, dp in ((7, at), (8, at_x), (9, at_y), (10, at_d)):
                arrived(msg, whole(dp, every, 1 - c))
        elif number == 5:
            for msg, ends in enumerate(out):
                self.copy(msg, *ends).wait_send()


def turns(groups, *list_of):
    for stage, group in list_of:
        groups[group].stage(stage)


def matrix(ref, cols=slice(None)):
    value = ref[(slice(None),) * (len(ref.shape) - 1) + (cols,)]
    return value.reshape(-1, value.shape[-1])


class Reduce:
    def __init__(self, part, out, bufs, send, recv, group):
        self.part, self.out, self.send, self.recv, self.group = part, out, send, recv, group
        self.half, self.diag, self.side, self.line = bufs
        self.sent = []

    copy = Gather.copy

    def push(self, msg, source, target, peer):
        copy = self.copy(msg, source, target, peer)
        copy.start()
        self.sent.append(copy)

    def arrived(self, msg, target):
        self.copy(msg, target, target, self.nobody).wait_recv()

    def add(self, target, *sources):
        total = sources[0][...].astype(f32)
        for source in sources[1:]:
            total = total + source[...].astype(f32)
        target[...] = total.astype(target.dtype)

    def stage(self, number):
        y, x, z, c = place()
        self.nobody = device(y, x, z, 1 - c)
        dp, dp_x, dp_y, dp_d = y * 2 + x, y * 2 + 1 - x, (1 - y) * 2 + x, (1 - y) * 2 + 1 - x
        to_x, to_y, to_c = device(y, 1 - x, z, c), device(1 - y, x, z, c), device(y, x, z, 1 - c)
        part, half = self.part, self.half
        if number == 0:
            for msg, at in ((0, dp_d), (1, dp_x), (2, dp_y), (3, dp)):
                self.push(msg, part.at[at, :, 1 - c], half.at[at], to_c)
        elif number == 1:
            self.arrived(0, half.at[dp_d])
            self.add(half.at[dp_d], half.at[dp_d], part.at[dp_d, :, c])
            self.push(4, half.at[dp_d, pl.ds(0, 2)], self.diag.at[0], to_x)
            self.push(5, half.at[dp_d, pl.ds(2, 2)], self.diag.at[1], to_y)
            self.arrived(1, half.at[dp_x])
            self.add(half.at[dp_x], half.at[dp_x], part.at[dp_x, :, c])
            self.arrived(2, half.at[dp_y])
            self.add(half.at[dp_y], half.at[dp_y], part.at[dp_y, :, c])
        elif number == 2:
            self.arrived(5, self.diag.at[1])
            late = half.at[dp_x, pl.ds(2, 2)]
            self.add(late, late, self.diag.at[1])
            self.push(6, half.at[dp_x], self.side.at[0], to_x)
            self.arrived(4, self.diag.at[0])
            late = half.at[dp_y, pl.ds(0, 2)]
            self.add(late, late, self.diag.at[0])
            self.push(7, half.at[dp_y], self.side.at[1], to_y)
            self.arrived(3, half.at[dp])
            self.add(half.at[dp], half.at[dp], part.at[dp, :, c])
        elif number == 3:
            self.arrived(6, self.side.at[0])
            self.arrived(7, self.side.at[1])
            self.add(half.at[dp], half.at[dp], self.side.at[0], self.side.at[1])
            for k in (1, 2, 3):
                self.push(
                    7 + k, half.at[dp, (z + k) % 4], self.line.at[k - 1], device(y, x, (z + k) % 4, c)
                )
        elif number == 4:
            for k in (1, 2, 3):
                self.arrived(7 + k, self.line.at[k - 1])
            self.add(self.out, half.at[dp, z], self.line.at[0], self.line.at[1], self.line.at[2])
        elif number == 5:
            for copy in self.sent:
                copy.wait_send()


class Total:
    def __init__(self, value, out, bufs, send, recv, group):
        self.value, self.out, self.send, self.recv, self.group = value, out, send, recv, group
        self.mine, self.theirs = bufs
        self.sent = []

    copy = Gather.copy

    def stage(self, number):
        y, x, z, c = place()
        self.nobody = device(y, x, z, 1 - c)
        peers = [
            device(y, x, z, 1 - c),
            device(y, 1 - x, z, c),
            device(1 - y, x, z, c),
            device(y, x, z + 1 - 2 * (z % 2), c),
            device(y, x, (z + 2) % 4, c),
        ]
        mine, theirs = self.mine, self.theirs
        if number == 0:
            mine[0] = self.value[...]
        elif number <= 5:
            at = number - 1
            self.copy(at, mine.at[at], theirs.at[at], self.nobody).wait_recv()
            if number < 5:
                mine[number] = mine[at] + theirs[at]
            else:
                self.out[...] = mine[at] + theirs[at]
        if number < 5:
            copy = self.copy(number, mine.at[number], theirs.at[number], peers[number])
            copy.start()
            self.sent.append(copy)
        if number == 6:
            for copy in self.sent:
                copy.wait_send()


def in_turn(groups, last):
    for turn in range(len(groups) + last):
        for at, group in enumerate(groups):
            if 0 <= turn - at <= last:
                group.stage(turn - at)


def forward_kernel(fast, *refs):
    refs = list(refs)
    take = lambda count: [refs.pop(0) for _ in range(count)]
    cameras, tokens, features, cotangent = take(4)
    shards = take(5)
    b_query, b_value, b_out, gain_first, shift_first = take(5)
    b_up, b_down, gain_second, shift_second, b_feat = take(5)
    output, start_low, q_rows, k_rows, v_rows, dmix_high, dmix_low, dots = take(8)
    grad_first, probs, grad_down, grad_up, grad_out, sums, sums_up = take(7)
    w_feat, w_qkv = take(2) if fast else shards[:2]
    first, act, gin, work, mixed, mixed_low, inverse = take(7)
    normed_low, grad_branch, grad_att, q_cat, v_cat, k_cat, stage = take(7)
    prob_sem, stage_sem, load_sem = take(3)
    w_out, w_up, w_down = take(3) if fast else shards[2:]
    width = tokens.shape[1]
    hidden = w_up.shape[-1]
    if fast:
        send, recv, local = take(3)
        half = hidden // 256 * 128
        wholes = (w_feat, w_qkv, w_out, w_up, w_up, w_down, w_down)
        pieces = ((0, width), (0, 3 * width), (0, width)) + ((0, half), (half, hidden - half)) * 2
        gather = [
            Gather(shards[which], whole, cols, send, recv, local, i)
            for i, (which, whole, cols) in enumerate(zip((0, 1, 2, 3, 3, 4, 4), wholes, pieces))
        ]
        greet()
        turns(gather, (0, 0), (0, 1))
    heads = width // HEAD
    pairs = heads // 2
    limit = 2 + CAM_LEN * cameras[0]

    def rows_of(step):
        return pl.ds(pl.multiple_of(step * STEP, 16), STEP)

    def row_ids(step):
        return step * STEP + lax.broadcasted_iota(jnp.int32, (STEP, 1), 0)

    loads = [
        pltpu.make_async_copy(
            source.at[pl.ds(0, ROWS), :], act.at[:, pl.ds(i * width, width)], load_sem.at[i]
        )
        for i, source in enumerate((features, tokens))
    ]
    for load in loads:
        load.start()
    if fast:
        turns(gather, (1, 0), (1, 1), (0, 2), (0, 3), (0, 4), (0, 5), (0, 6), (2, 0), (2, 1))
        turns(gather, (3, 0), (3, 1), (4, 0), (4, 1), (1, 2))
    for load in loads:
        load.wait()

    def project(step, carry):
        rows = rows_of(step)
        ids = row_ids(step)
        valid = ids < limit
        camera = jnp.logical_and(ids >= 2, valid)
        memory = dg(act[rows, :width], matrix(w_feat), 1, 0) + b_feat[...]
        start = act[rows, width : 2 * width].astype(f32) + jnp.where(camera, memory, 0.0)
        first[rows, :] = start
        low = start.astype(bf16)
        start_low[rows, :] = low
        joined = dg(low, matrix(w_qkv), 1, 0)
        q_rows[rows, :] = ((joined[:, :width] + b_query[...]) * 0.125).astype(bf16)
        keys = joined[:, width : 2 * width]
        lead = k_rows[0:16, :][0:1].astype(f32)
        k_rows[rows, :] = jnp.where(valid, keys, lead).astype(bf16)
        v_rows[rows, :] = (joined[:, 2 * width :] + b_value[...]).astype(bf16)
        return carry

    lax.fori_loop(0, 4, project, 0)

    lane_valid = lax.broadcasted_iota(jnp.int32, (1, ROWS), 1) < limit

    def prob_copy(pair, side):
        source = act if side == 0 else gin
        at = pl.ds(pl.multiple_of(lax.rem(pair, 2) * 1280, 128), 1280)
        return pltpu.make_async_copy(
            source.at[:, at], probs.at[2 * pair + side], prob_sem.at[2 * lax.rem(pair, 2) + side]
        )

    def attend(pair, carry):
        lanes = pl.ds(pl.multiple_of(pair * 128, 128), 128)
        if fast:
            for at_pair in range(pairs):

                @pl.when(pair == at_pair)
                def _():
                    turns(gather, (1, at_pair + 3), (2, at_pair + 2))
                    if at_pair:
                        turns(gather, (3, at_pair + 1))

        @pl.when(pair >= 2)
        def _():
            prob_copy(pair - 2, 0).wait()
            prob_copy(pair - 2, 1).wait()

        queries = q_rows[:, lanes].astype(f32).T * LOG2E
        high, low = split_low(queries)
        none = jnp.zeros((HEAD, ROWS), bf16)
        values = jnp.where(lane_valid, v_rows[:, lanes].astype(f32).T, 0.0).astype(bf16)
        ones = jnp.broadcast_to(jnp.where(lane_valid, 1.0, 0.0), (HEAD, ROWS)).astype(bf16)
        for side in range(2):
            own = slice(side * HEAD, side * HEAD + HEAD)
            other = slice((1 - side) * HEAD, (1 - side) * HEAD + HEAD)
            q_cat[side, own, :] = high[own]
            q_cat[side, other, :] = none
            q_cat[side, 128 + side * HEAD : 128 + side * HEAD + HEAD, :] = low[own]
            q_cat[side, 128 + (1 - side) * HEAD : 128 + (1 - side) * HEAD + HEAD, :] = none
            v_cat[side, :HEAD, :] = values[own]
            v_cat[side, HEAD:, :] = ones
        keys = k_rows[:, lanes]
        k_cat[:, :128] = keys
        k_cat[:, 128:] = keys
        base = lax.rem(pair, 2) * 1280
        jobs = [(side, at, size) for side in range(2) for at, size in QBLOCKS]
        peak = {}

        def score(job, at_key, keys_here):
            side, at, size = jobs[job]
            here = slice(at_key, at_key + keys_here)
            scores = dg(k_cat[here, :], q_cat[side, :, at : at + size], 1, 0)
            work[job % 3 * 4 + at_key // STEP, :, :size] = scores
            high_here = jnp.max(scores, axis=0, keepdims=True)
            peak[job] = jnp.maximum(peak[job], high_here) if job in peak else high_here

        def weigh(job, at_key, keys_here):
            side, at, size = jobs[job]
            slot = act if side == 0 else gin
            here = slice(at_key, at_key + keys_here)
            slot[here, pl.ds(pl.multiple_of(base + at, 128), size)] = jnp.exp2(
                work[job % 3 * 4 + at_key // STEP, :, :size] - peak[job]
            ).astype(bf16)

        def mix(job):
            side, at, size = jobs[job]
            slot = act if side == 0 else gin
            weight = slot[:, pl.ds(pl.multiple_of(base + at, 128), size)]
            summed = dg(v_cat[side], weight, 1, 0)
            inv = 1.0 / summed[HEAD : HEAD + 1]
            mixed[pl.ds(pl.multiple_of(pair * 128 + side * HEAD, 8), HEAD), at : at + size] = (
                summed[:HEAD] * inv
            )
            inverse[2 * pair + side, :, at : at + size] = inv

        parts = chunks(ROWS, STEP)
        for job in (0, 1):
            for part in parts:
                score(job, *part)
        for job in range(len(jobs)):
            for part in parts:
                if job + 2 < len(jobs):
                    score(job + 2, *part)
                weigh(job, *part)
            if job >= 2:
                mix(job - 2)
            if job == len(QBLOCKS) - 1:
                prob_copy(pair, 0).start()
        mix(len(jobs) - 2)
        mix(len(jobs) - 1)
        prob_copy(pair, 1).start()
        return carry

    lax.fori_loop(0, pairs, attend, 0)
    for pair in (pairs - 2, pairs - 1):
        for side in range(2):
            prob_copy(pair, side).wait()

    if fast:
        turns(gather, (2, 6), (3, 5), (4, 2))
    mixed_low[...] = mixed[...].astype(bf16)
    for at, size in chunks(width, 256):
        cols = slice(at, at + size)
        first[:, cols] += dg(mixed_low[...], matrix(w_out, cols), 0, 0) + b_out[:, cols]
    sums[...] = jnp.zeros_like(sums)
    sums_up[...] = jnp.zeros_like(sums_up)
    cuts = chunks(hidden, 512)
    if fast:
        turns(gather, (3, 6), (4, 3), (4, 4), (4, 5), (4, 6), *[(5, i) for i in range(7)])

    def feed(step, carry):
        rows = rows_of(step)
        valid = row_ids(step) < limit
        unit_first, scale_first = norm_parts(first[rows, :])
        normed = unit_first * gain_first[...] + shift_first[...]
        low = normed.astype(bf16)
        normed_low[rows, :] = low
        for at, size in cuts:
            cols = slice(at, at + size)
            inner = dg(low, matrix(w_up, cols), 1, 0) + b_up[:, cols]
            square = inner * inner
            half = 0.5 + 0.5 * jnp.tanh(inner * (GELU_C + (GELU_C * GELU_A) * square))
            value = inner * half
            act[rows, cols] = value.astype(bf16)
            slope = half + value * (1.0 - half) * (2 * GELU_C + (6 * GELU_C * GELU_A) * square)
            for cut, wide in chunks(size, 256):
                work[(at + cut) // 256, :, :wide] = slope[:, cut : cut + wide]
        branch = dg(act[rows, :], matrix(w_down), 1, 1) + b_down[...]
        unit_second, scale_second = norm_parts(normed + branch)
        final = unit_second * gain_second[...] + shift_second[...]
        output[rows, :] = jnp.where(valid, final, 0.0).astype(bf16)
        grad = jnp.where(valid, cotangent[rows, :].astype(f32), 0.0)
        sums[0] += fold(grad * unit_second)
        sums[1] += fold(grad)
        grad_second = norm_back(grad, unit_second, scale_second, gain_second[...])
        low_branch = grad_second.astype(bf16)
        grad_branch[rows, :] = low_branch
        sums[2] += fold(low_branch.astype(f32))
        for at, size in cuts:
            cols = slice(at, at + size)
            slope = [work[(at + cut) // 256, :, :wide] for cut, wide in chunks(size, 256)]
            low_inner = (
                dg(low_branch, matrix(w_down, cols), 1, 0) * jnp.concatenate(slope, axis=1)
            ).astype(bf16)
            gin[rows, cols] = low_inner
            sums_up[:, cols] += fold(low_inner.astype(f32))
        grad_normed = grad_second + dg(gin[rows, :], matrix(w_up), 1, 1)
        sums[3] += fold(grad_normed * unit_first)
        sums[4] += fold(grad_normed)
        back = norm_back(grad_normed, unit_first, scale_first, gain_first[...])
        grad_first[rows, :] = back
        low_att = back.astype(bf16)
        grad_att[rows, :] = low_att
        sums[5] += fold(low_att.astype(f32))
        return carry

    lax.fori_loop(0, 4, feed, 0)
    output[ROWS:, :] = jnp.zeros((SLOTS - ROWS, width), bf16)

    for at, size in QBLOCKS:
        cols = slice(at, at + size)
        grad_mixed = dg(matrix(w_out), grad_att[cols, :], 1, 1).astype(bf16).astype(f32)
        scaled = grad_mixed.reshape(heads, HEAD, size) * inverse[:, :, cols]
        dots[:, :, cols] = jnp.sum(
            scaled * mixed[:, cols].reshape(heads, HEAD, size), axis=1, keepdims=True
        )
        high, low = split_low(scaled.reshape(width, size))
        dmix_high[:, cols] = high
        dmix_low[:, cols] = low

    def weight_copy(target, at, size, slot):
        return pltpu.make_async_copy(
            stage.at[slot, :, pl.ds(0, size)], target.at[:, pl.ds(at, size)], stage_sem.at[slot]
        )

    pending = {}
    for turn, (left, right, target, (at, size)) in enumerate(
        [(grad_branch, act, grad_down, cut) for cut in cuts]
        + [(normed_low, gin, grad_up, cut) for cut in cuts]
    ):
        slot = turn % 2
        if slot in pending:
            pending[slot].wait()
        stage[slot, :, 0:size] = dg(left[...], right[:, at : at + size], 0, 0).astype(bf16)
        pending[slot] = weight_copy(target, at, size, slot)
        pending[slot].start()
    grad_out[...] = dg(mixed_low[...], grad_att[...], 1, 0).astype(bf16)
    for copy in pending.values():
        copy.wait()


def shaped(shape, dtype):
    return jax.ShapeDtypeStruct(shape, dtype)


def forward_call(fast, cameras, tokens, features, cotangent, weights, biases):
    width = tokens.shape[1]
    hidden = weights[3].shape[1]
    heads = width // HEAD
    outs = (
        shaped((SLOTS, width), bf16),
        shaped((ROWS, width), bf16),
        shaped((ROWS, width), bf16),
        shaped((ROWS, width), bf16),
        shaped((ROWS, width), bf16),
        shaped((width, ROWS), bf16),
        shaped((width, ROWS), bf16),
        shaped((heads, 1, ROWS), f32),
        shaped((ROWS, width), f32),
        shaped((heads, ROWS, 1280), bf16),
        shaped((width, hidden), bf16),
        shaped((width, hidden), bf16),
        shaped((width, width), bf16),
        shaped((6, 8, width), f32),
        shaped((8, hidden), f32),
    )
    wholes = [(4, 4, 2) + w.shape for w in weights]
    if fast:
        outs += tuple(shaped(whole, bf16) for whole in wholes[:2])
    vmem = pl.BlockSpec(memory_space=pltpu.VMEM)
    hbm = pl.BlockSpec(memory_space=pl.ANY)
    return pl.pallas_call(
        functools.partial(forward_kernel, fast),
        out_shape=outs,
        in_specs=[pl.BlockSpec(memory_space=pltpu.SMEM)] + [hbm] * 2 + [vmem] * 16,
        out_specs=tuple(hbm if i in (9, 10, 11) else vmem for i in range(len(outs))),
        scratch_shapes=[
            pltpu.VMEM((ROWS, width), f32),
            pltpu.VMEM((ROWS, hidden), bf16),
            pltpu.VMEM((ROWS, hidden), bf16),
            pltpu.VMEM((max(12, -(-hidden // 256)), STEP, 256), f32),
            pltpu.VMEM((width, ROWS), f32),
            pltpu.VMEM((width, ROWS), bf16),
            pltpu.VMEM((heads, 1, ROWS), f32),
            pltpu.VMEM((ROWS, width), bf16),
            pltpu.VMEM((ROWS, width), bf16),
            pltpu.VMEM((ROWS, width), bf16),
            pltpu.VMEM((2, 256, ROWS), bf16),
            pltpu.VMEM((2, 128, ROWS), bf16),
            pltpu.VMEM((ROWS, 256), bf16),
            pltpu.VMEM((2, width, 512), bf16),
            pltpu.SemaphoreType.DMA((4,)),
            pltpu.SemaphoreType.DMA((2,)),
            pltpu.SemaphoreType.DMA((2,)),
        ]
        + fast
        * (
            [pltpu.VMEM(whole, bf16) for whole in wholes[2:]]
            + [
                pltpu.SemaphoreType.DMA((7, GATHER_MSGS)),
                pltpu.SemaphoreType.DMA((7, GATHER_MSGS)),
                pltpu.SemaphoreType.DMA((7,)),
            ]
        ),
        compiler_params=pltpu.CompilerParams(
            vmem_limit_bytes=62 * MIB,
            collective_id=0 if fast else None,
            has_side_effects=fast,
        ),
        name="layer_forward",
    )(cameras, tokens, features, cotangent, *weights, *biases)


def backward_kernel(
    cameras,
    features,
    q_rows,
    k_rows,
    v_rows,
    dmix_high,
    dmix_low,
    dots,
    start_low,
    grad_first,
    probs,
    w_qkv,
    w_feat,
    grad_tokens,
    grad_features,
    grad_qkv,
    grad_feat,
    sums,
    feats,
    weights,
    grad_scores,
    joined,
    d_cat,
    d_rows,
    v_cat,
    k_turned,
    grad_memory,
    prob_sem,
    load_sem,
):
    width = q_rows.shape[1]
    heads = width // HEAD
    pairs = heads // 2
    limit = 2 + CAM_LEN * cameras[0]

    def prob_copy(pair, side):
        slot = 2 * lax.rem(pair, 2) + side
        return pltpu.make_async_copy(
            probs.at[2 * pair + side], weights.at[slot], prob_sem.at[slot]
        )

    for side in range(2):
        prob_copy(0, side).start()
    load = pltpu.make_async_copy(features.at[pl.ds(0, ROWS), :], feats, load_sem)
    load.start()
    sums[...] = jnp.zeros_like(sums)
    lane_valid = lax.broadcasted_iota(jnp.int32, (1, ROWS), 1) < limit
    row_valid = lax.broadcasted_iota(jnp.int32, (ROWS, 1), 0) < limit

    def attend_back(pair, carry):
        lanes = pl.ds(pl.multiple_of(pair * 128, 128), 128)

        @pl.when(pair + 1 < pairs)
        def _():
            prob_copy(pair + 1, 0).start()
            prob_copy(pair + 1, 1).start()

        both = pl.ds(pl.multiple_of(pair * 128, 128), 128)
        high = dmix_high[both, :]
        low = dmix_low[both, :]
        none = jnp.zeros((HEAD, ROWS), bf16)
        for side in range(2):
            own = slice(side * HEAD, side * HEAD + HEAD)
            mine, its = side * HEAD, (1 - side) * HEAD
            d_cat[side, mine : mine + HEAD, :] = high[own]
            d_cat[side, its : its + HEAD, :] = none
            d_cat[side, 128 + mine : 128 + mine + HEAD, :] = low[own]
            d_cat[side, 128 + its : 128 + its + HEAD, :] = none
        d_rows[:, :128] = high.astype(f32).T.astype(bf16)
        d_rows[:, 128:] = low.astype(f32).T.astype(bf16)
        values = v_rows[:, lanes]
        v_cat[:, :128] = values
        v_cat[:, 128:] = values
        k_turned[...] = jnp.where(lane_valid, k_rows[:, lanes].astype(f32).T, 0.0).astype(bf16)
        base = 2 * lax.rem(pair, 2)
        jobs = [(side, at, size) for side in range(2) for at, size in QBLOCKS]
        parts = chunks(ROWS, STEP)
        turned = {0: [], 1: []}
        wide = {}

        def slope(job):
            side, at, size = jobs[job]
            offset = dots[2 * pair + side, :, at : at + size]
            for at_key, keys_here in parts:
                here = slice(at_key, at_key + keys_here)
                grad = dg(v_cat[here, :], d_cat[side, :, at : at + size], 1, 0) - offset
                weight = weights[base + side, here, at : at + size].astype(f32)
                grad_scores[side, here, at : at + size] = (weight * grad).astype(bf16)

        def queries(job):
            side, at, size = jobs[job]
            turned[side].append(
                dg(k_turned[...], grad_scores[side, :, at : at + size], 1, 0)[
                    side * HEAD : side * HEAD + HEAD
                ]
            )

        def spread(side, part):
            here = slice(part[0], part[0] + part[1])
            value = dg(weights[base + side, here, :ROWS], d_rows[...], 1, 0)
            value = value[:, :128] + value[:, 128:]
            key = dg(grad_scores[side, here, :ROWS], q_rows[:, lanes], 1, 0)
            wide[side, part] = (value, key)

        for side in range(2):
            prob_copy(pair, side).wait()
        for job in range(len(jobs)):
            slope(job)
            if job >= 1:
                queries(job - 1)
            if job > len(QBLOCKS):
                side_job = job - len(QBLOCKS) - 1
                if side_job < len(parts):
                    spread(0, parts[side_job])
        queries(len(jobs) - 1)
        first_lane = lax.broadcasted_iota(jnp.int32, (STEP, 128), 1) < HEAD
        for part in parts:
            spread(1, part)
            here = slice(part[0], part[0] + part[1])
            keep = row_valid[here]
            for which, at in ((0, 2 * width), (1, width)):
                value = jnp.where(first_lane, wide[0, part][which], wide[1, part][which])
                value = jnp.where(keep, value, 0.0).astype(bf16)
                joined[here, pl.ds(pl.multiple_of(at + pair * 128, 128), 128)] = value
        query = jnp.concatenate(
            [jnp.concatenate(turned[0], axis=1), jnp.concatenate(turned[1], axis=1)], axis=0
        )
        joined[:, lanes] = (query.astype(bf16).astype(f32).T * 0.125).astype(bf16)
        return carry

    lax.fori_loop(0, pairs, attend_back, 0)
    load.wait()

    def project_back(step, carry):
        rows = pl.ds(pl.multiple_of(step * STEP, 16), STEP)
        ids = step * STEP + lax.broadcasted_iota(jnp.int32, (STEP, 1), 0)
        camera = jnp.logical_and(ids >= 2, ids < limit)
        part = joined[rows, :]
        sums[0] += fold(part[:, :width].astype(f32))
        sums[1] += fold(part[:, 2 * width :].astype(f32))
        grad_start = grad_first[rows, :] + dg(part, w_qkv[...], 1, 1)
        grad_tokens[rows, :] = grad_start.astype(bf16)
        low = jnp.where(camera, grad_start, 0.0).astype(bf16)
        grad_memory[rows, :] = low
        sums[2] += fold(low.astype(f32))
        grad_features[rows, :] = dg(low, w_feat[...], 1, 1).astype(bf16)
        return carry

    lax.fori_loop(0, 4, project_back, 0)
    grad_tokens[ROWS:, :] = jnp.zeros((SLOTS - ROWS, width), bf16)
    grad_features[ROWS:, :] = jnp.zeros((SLOTS - ROWS, width), bf16)
    for at, size in chunks(3 * width, 512):
        cols = slice(at, at + size)
        grad_qkv[:, cols] = dg(start_low[...], joined[:, cols], 0, 0).astype(bf16)
    grad_feat[...] = dg(feats[...], grad_memory[...], 0, 0).astype(bf16)


def backward_call(cameras, features, saved, w_qkv, w_feat):
    width = features.shape[1]
    heads = width // HEAD
    outs = (
        shaped((SLOTS, width), bf16),
        shaped((SLOTS, width), bf16),
        shaped((width, 3 * width), bf16),
        shaped((width, width), bf16),
        shaped((3, 8, width), f32),
    )
    vmem = pl.BlockSpec(memory_space=pltpu.VMEM)
    hbm = pl.BlockSpec(memory_space=pl.ANY)
    return pl.pallas_call(
        backward_kernel,
        out_shape=outs,
        in_specs=[pl.BlockSpec(memory_space=pltpu.SMEM), hbm] + [vmem] * 8 + [hbm] + [vmem] * 2,
        out_specs=(vmem,) * 5,
        scratch_shapes=[
            pltpu.VMEM((ROWS, width), bf16),
            pltpu.VMEM((4, ROWS, 1280), bf16),
            pltpu.VMEM((2, ROWS, 1280), bf16),
            pltpu.VMEM((ROWS, 3 * width), bf16),
            pltpu.VMEM((2, 256, ROWS), bf16),
            pltpu.VMEM((ROWS, 256), bf16),
            pltpu.VMEM((ROWS, 256), bf16),
            pltpu.VMEM((128, ROWS), bf16),
            pltpu.VMEM((ROWS, width), bf16),
            pltpu.SemaphoreType.DMA((4,)),
            pltpu.SemaphoreType.DMA(()),
        ],
        compiler_params=pltpu.CompilerParams(vmem_limit_bytes=62 * MIB),
        name="layer_backward",
    )(cameras, features, *saved, w_qkv, w_feat)


def reduce_bufs(columns, rows):
    return [
        pltpu.VMEM((4, 4, rows, columns), bf16),
        pltpu.VMEM((2, 2, rows, columns), bf16),
        pltpu.VMEM((2, 4, rows, columns), bf16),
        pltpu.VMEM((3, rows, columns), bf16),
    ]


def reduce_kernel(*refs):
    parts, small, outs, small_out, bufs = refs[:5], refs[5], refs[6:11], refs[11], refs[12:-2]
    send, recv = refs[-2:]
    greet()
    groups = [
        Reduce(parts[i], outs[i], bufs[4 * i : 4 * i + 4], send, recv, i) for i in range(5)
    ]
    groups.append(Total(small, small_out, bufs[20:22], send, recv, 5))
    in_turn(groups, 6)


def reduce_call(grads, small):
    vmem = pl.BlockSpec(memory_space=pltpu.VMEM)
    rows = grads[0].shape[0] // 32
    parts = [grad.reshape(4, 4, 2, rows, grad.shape[1]) for grad in grads]
    bufs = [buf for grad in grads for buf in reduce_bufs(grad.shape[1], rows)]
    bufs += [pltpu.VMEM((5,) + small.shape, f32)] * 2
    return pl.pallas_call(
        reduce_kernel,
        out_shape=tuple(shaped((rows, grad.shape[1]), f32) for grad in grads)
        + (shaped(small.shape, f32),),
        in_specs=[vmem] * 6,
        out_specs=(vmem,) * 6,
        scratch_shapes=bufs
        + [pltpu.SemaphoreType.DMA((6, GATHER_MSGS)), pltpu.SemaphoreType.DMA((6, GATHER_MSGS))],
        compiler_params=pltpu.CompilerParams(
            collective_id=1, has_side_effects=True, vmem_limit_bytes=62 * MIB
        ),
        name="reduce_gradients",
    )(*parts, small)


AXES = ("dp", "fsdp")


def on_device(
    fast,
    tokens,
    features,
    cameras,
    cotangent,
    w_qkv,
    w_out,
    w_up,
    w_down,
    w_feat,
    *biases,
):
    width = tokens.shape[1]
    hidden = w_up.shape[1]
    biases = [bias.reshape(1, -1) for bias in biases]
    shards = (w_feat, w_qkv, w_out, w_up, w_down)
    weights = shards
    if not fast:
        weights = tuple(lax.all_gather(w, AXES, axis=0, tiled=True) for w in shards)
    (
        output,
        start_low,
        q_rows,
        k_rows,
        v_rows,
        dmix_high,
        dmix_low,
        dots,
        grad_first,
        probs,
        grad_down,
        grad_up,
        grad_out,
        sums,
        sums_up,
        *wholes,
    ) = forward_call(fast, cameras, tokens, features, cotangent, weights, biases)
    if fast:
        weights = [whole.reshape(width, -1) for whole in wholes]
    saved = (q_rows, k_rows, v_rows, dmix_high, dmix_low, dots, start_low, grad_first, probs)
    grad_tokens, grad_features, grad_qkv, grad_feat, sums_back = backward_call(
        cameras, features, saved, weights[1], weights[0]
    )
    grads = (grad_down, grad_up, grad_out, grad_qkv, grad_feat)
    small = jnp.concatenate(
        [
            jnp.sum(sums, axis=1).reshape(-1),
            jnp.sum(sums_back, axis=1).reshape(-1),
            jnp.sum(sums_up, axis=0),
        ]
    )
    lines = -(-small.shape[0] // 1024) * 8
    small = jnp.pad(small, (0, lines * 128 - small.shape[0])).reshape(lines, 128)
    if fast:
        *grads, small = reduce_call(grads, small)
    else:
        grads = [
            lax.psum_scatter(
                lax.optimization_barrier(grad.astype(f32)), AXES, scatter_dimension=0, tiled=True
            )
            for grad in grads
        ]
        small = lax.psum(small, AXES)
    small = small.reshape(-1)
    rows = small[: 9 * width].reshape(9, width)
    grad_b_up = small[9 * width : 9 * width + hidden]
    grad_down, grad_up, grad_out, grad_qkv, grad_feat = grads
    return (
        output,
        grad_tokens,
        grad_features,
        grad_qkv,
        grad_out,
        grad_up,
        grad_down,
        grad_feat,
        rows[6],
        rows[7],
        rows[5],
        rows[3],
        rows[4],
        grad_b_up,
        rows[2],
        rows[0],
        rows[1],
        rows[8],
    )


def solution(mesh):
    split = P(AXES, None)
    fast = mesh.shape["dp"] == 4 and mesh.shape["fsdp"] == 8
    return jax.shard_map(
        functools.partial(on_device, fast),
        mesh=mesh,
        in_specs=(split, split, P(AXES), split) + (split,) * 5 + (P(),) * 10,
        out_specs=(split,) * 8 + (P(),) * 10,
        check_vma=False,
    )
```

time: 271 us -> 232 us (0.86)
  Pallas kernels: 254 us -> 218 us
  local copies, waits for them, and re-layouts: 11.6 us -> 8.36 us
    pallas_call x2 -> x1, Pallas kernels: 139 us -> 106 us  [forward_call(): pl.pallas_call(functools.partial(forward_kernel, fast), out_shape=outs, i...]
    unnamed x5 -> x18, local copies, waits for them, and re-layouts: 7.53 us -> 4.31 us
where the time goes in v2:
time: 232 us; the launch traced here: 231 us
  Pallas kernels  218 us (94%)
  local copies, waits for them, and re-layouts  8.36 us (4%)
  other arithmetic  3.3 us (1%)
    pallas_call x1, Pallas kernels, forward_call(): pl.pallas_call(functools.partial(forward_kernel, fast), out_shape=outs, i...  106 us
    pallas_call x1, Pallas kernels, reduce_call(): pl.pallas_call(reduce_kernel, out_shape=tuple((shaped((rows, grad.shape[1...  70.8 us
    pallas_call x1, Pallas kernels, backward_call(): pl.pallas_call(backward_kernel, out_shape=outs, in_specs=[pl.BlockSpec(me...  41.5 us

profile of v2, /device:TPU:0, one launch (start us, length us, event | category | flops | bytes accessed | tf_op | source)
XLA Modules:
  0.0 231.3 jit_solution(6068087780591716928)
XLA Ops:
  1.3 1.3 reshape.124.refs_14_
  2.6 106.0 %layer_forward.1 = (bf16[1280,512]{1,0:T(8,128)(2,1)}, bf16[1216,512]{1,0:T(8,128)(2,1)}, bf16[1216,512]{1,0:T(8,128)(2,1)}, bf16[1216,512]{1,0:T(8,128)(2,1)}, ...) custom-call(s32[1]{0:T(128)S(6)} %copy.43.refs_0_.cameras, ...), custom_call_target="tpu_custom_call" | custom-call | tf_op jit(solution)/shard_map/layer_forward/pallas_call | solution.py:571
  108.6 0.9 reduce_sum.27
  109.6 0.9 reduce_sum.29
  110.5 41.5 %layer_backward.1 = (bf16[1280,512]{1,0:T(8,128)(2,1)}, bf16[1280,512]{1,0:T(8,128)(2,1)}, bf16[512,1536]{1,0:T(8,128)(2,1)}, bf16[512,512]{1,0:T(8,128)(2,1)}, f32[3,8,512]{2,1,0:T(8,128)}) custom-call(s32[1]{0:T(128)S(6)} %copy.43.refs_0_.cameras, bf16[1280,512]{1,0:T(8,128)(2,1)} %features.1, bf16[1216,512]{1,0:T(8,128)(2,1)} %get-tuple-element.47.q_rows, ...), custom_call_target="tpu_custom_call" | custom-call | tf_op jit(solution)/shard_map/layer_backward/pallas_call | solution.py:783
  152.0 0.8 reduce_sum.28
  152.8 0.6 fusion.refs_5_
  153.4 0.0 copy-start
  153.4 70.8 %reduce_gradients.1 = (f32[16,3200]{1,0:T(8,128)}, f32[16,3200]{1,0:T(8,128)}, f32[16,512]{1,0:T(8,128)}, f32[16,1536]{1,0:T(8,128)}, f32[16,512]{1,0:T(8,128)}, /*index=5*/f32[64,128]{1,0:T(8,128)}) custom-call(bf16[4,4,2,16,3200]{4,3,2,1,0:T(8,128)(2,1)} %bitcast.38, bf16[4,4,2,16,3200]{4,3,2,1,0:T(8,128)(2,1)} %bitcast.39, ...), custom_call_target="tpu_custom_call" | custom-call | tf_op jit(solution)/shard_map/reduce_gradients/pallas_call | solution.py:832
  224.2 1.3 slice_bitcast_fusion
  225.6 1.4 slice_bitcast_fusion.1
  226.9 0.0 copy-done
  226.9 0.0 copy-start.3
  226.9 0.0 copy-start.5
  227.0 0.0 copy-start.2
  227.0 0.0 copy-start.1
  227.0 0.0 copy-start.4
  227.0 1.1 copy.44
  228.0 0.0 copy-done.3
  228.0 0.6 copy.45
  228.7 0.0 copy-done.5
  228.7 0.6 copy.46
  229.3 0.0 copy-done.2
  229.3 0.7 copy.47
  230.0 0.0 copy-done.1
  230.0 0.7 copy.48
  230.7 0.0 copy-done.4
  230.7 0.6 copy.49
  (2 shorter events, 0.0 us)
Async XLA Ops:
  153.4 73.5 %copy-start = (bf16[1280,512]{1,0:T(8,128)(2,1)S(1)}, bf16[1280,512]{1,0:T(8,128)(2,1)}, u32[]{:S(2)}) copy-start(bf16[1280,512]{1,0:T(8,128)(2,1)} %get-tuple-element.101) | copy-start | bytes 3932164
  226.9 1.1 copy-start.3
  226.9 1.7 copy-start.5
  227.0 2.4 %copy-start.2 = (f32[16,3200]{1,0:T(8,128)S(1)}, f32[16,3200]{1,0:T(8,128)}, u32[]{:S(2)}) copy-start(f32[16,3200]{1,0:T(8,128)} %get-tuple-element.106) | copy-start | bytes 614404
  227.0 3.0 %copy-start.1 = (f32[16,3200]{1,0:T(8,128)S(1)}, f32[16,3200]{1,0:T(8,128)}, u32[]{:S(2)}) copy-start(f32[16,3200]{1,0:T(8,128)} %get-tuple-element.107) | copy-start | bytes 614404
  227.0 3.7 %copy-start.4 = (f32[16,512]{1,0:T(8,128)S(1)}, f32[16,512]{1,0:T(8,128)}, u32[]{:S(2)}) copy-start(f32[16,512]{1,0:T(8,128)} %get-tuple-element.108) | copy-start | bytes 98308

commit v3 on v2

--- a/solution.py
+++ b/solution.py
@@ -50,6 +50,10 @@
     return scale * (inside - one - unit * two)
 
 
+def line_of(ref, cols=slice(None)):
+    return ref[cols].reshape(1, -1)
+
+
 def fold(value):
     rows, width = value.shape
     return jnp.sum(value.reshape(rows // 8, 8, width), axis=0)
@@ -61,7 +65,7 @@
 
 
 MESH = pl.DeviceIdType.MESH
-GATHER_MSGS = 11
+MESSAGES = 11
 
 
 def place():
@@ -77,7 +81,12 @@
 def neighbours():
     y, x, z, c = place()
     around = [device(y, x, (z + k) % 4, c) for k in (1, 2, 3)]
-    return around + [device(y, 1 - x, z, c), device(1 - y, x, z, c), device(y, x, z, 1 - c)]
+    return around + [
+        device(y, 1 - x, z, c),
+        device(1 - y, x, z, c),
+        device(1 - y, 1 - x, z, c),
+        device(y, x, z, 1 - c),
+    ]
 
 
 def greet():
@@ -167,22 +176,17 @@
 
 
 class Reduce:
-    def __init__(self, part, out, bufs, send, recv, group):
-        self.part, self.out, self.send, self.recv, self.group = part, out, send, recv, group
+    def __init__(self, part, cols, write, bufs, mine, direct, send, recv, local, group):
+        self.part, self.cols, self.write, self.mine, self.direct = part, cols, write, mine, direct
+        self.send, self.recv, self.local, self.group = send, recv, local, group
         self.half, self.diag, self.side, self.line = bufs
-        self.sent = []
 
     copy = Gather.copy
 
-    def push(self, msg, source, target, peer):
-        copy = self.copy(msg, source, target, peer)
-        copy.start()
-        self.sent.append(copy)
-
-    def arrived(self, msg, target):
-        self.copy(msg, target, target, self.nobody).wait_recv()
-
     def add(self, target, *sources):
+        if len(sources) == 2:
+            target[...] = sources[0][...] + sources[1][...]
+            return
         total = sources[0][...].astype(f32)
         for source in sources[1:]:
             total = total + source[...].astype(f32)
@@ -190,92 +194,142 @@
 
     def stage(self, number):
         y, x, z, c = place()
-        self.nobody = device(y, x, z, 1 - c)
-        dp, dp_x, dp_y, dp_d = y * 2 + x, y * 2 + 1 - x, (1 - y) * 2 + x, (1 - y) * 2 + 1 - x
+        at_x, at_y, at_d, at = y * 2 + 1 - x, (1 - y) * 2 + x, (1 - y) * 2 + 1 - x, y * 2 + x
         to_x, to_y, to_c = device(y, 1 - x, z, c), device(1 - y, x, z, c), device(y, x, z, 1 - c)
-        part, half = self.part, self.half
+        to_d = device(1 - y, 1 - x, z, c)
+        cols = pl.ds(*self.cols)
+        half, diag, side, line = self.half, self.diag, self.side, self.line
+        if self.mine is None:
+            mine = lambda dp: self.part.at[dp, :, c, :, cols]
+        else:
+            mine = lambda dp: self.mine.at[dp]
+            fetch = lambda: pltpu.make_async_copy(
+                self.part.at[:, :, c, :, cols], self.mine, self.local.at[self.group]
+            )
+        low, high = pl.ds(0, 2), pl.ds(2, 2)
+        blocks = (at_d, at_x, at_y, at)
+        out = [(self.part.at[dp, :, 1 - c, :, cols], half.at[dp], to_c) for dp in blocks]
+        if self.direct:
+            out += [
+                (half.at[at_d], diag, to_d),
+                None,
+                (half.at[at_x], side.at[0], to_x),
+                (half.at[at_y], side.at[1], to_y),
+            ]
+        else:
+            out += [
+                (half.at[at_d, low], diag.at[0], to_x),
+                (half.at[at_d, high], diag.at[1], to_y),
+                (half.at[at_x], side.at[0], to_x),
+                (half.at[at_y], side.at[1], to_y),
+            ]
+        out += [
+            (half.at[at, (z + k) % 4], line.at[k - 1], device(y, x, (z + k) % 4, c))
+            for k in (1, 2, 3)
+        ]
+        arrived = lambda msg: self.copy(msg, *out[msg][1:2] * 2, to_c).wait_recv()
+        start = lambda msg: self.copy(msg, *out[msg]).start()
+
+        def halve(msg):
+            self.copy(msg, half.at[blocks[msg]], half.at[blocks[msg]], to_c).wait_recv()
+            self.add(half.at[blocks[msg]], half.at[blocks[msg]], mine(blocks[msg]))
+
         if number == 0:
-            for msg, at in ((0, dp_d), (1, dp_x), (2, dp_y), (3, dp)):
-                self.push(msg, part.at[at, :, 1 - c], half.at[at], to_c)
+            for msg in range(4):
+                start(msg)
+            if self.mine is not None:
+                fetch().start()
         elif number == 1:
-            self.arrived(0, half.at[dp_d])
-            self.add(half.at[dp_d], half.at[dp_d], part.at[dp_d, :, c])
-            self.push(4, half.at[dp_d, pl.ds(0, 2)], self.diag.at[0], to_x)
-            self.push(5, half.at[dp_d, pl.ds(2, 2)], self.diag.at[1], to_y)
-            self.arrived(1, half.at[dp_x])
-            self.add(half.at[dp_x], half.at[dp_x], part.at[dp_x, :, c])
-            self.arrived(2, half.at[dp_y])
-            self.add(half.at[dp_y], half.at[dp_y], part.at[dp_y, :, c])
-        elif number == 2:
-            self.arrived(5, self.diag.at[1])
-            late = half.at[dp_x, pl.ds(2, 2)]
-            self.add(late, late, self.diag.at[1])
-            self.push(6, half.at[dp_x], self.side.at[0], to_x)
-            self.arrived(4, self.diag.at[0])
-            late = half.at[dp_y, pl.ds(0, 2)]
-            self.add(late, late, self.diag.at[0])
-            self.push(7, half.at[dp_y], self.side.at[1], to_y)
-            self.arrived(3, half.at[dp])
-            self.add(half.at[dp], half.at[dp], part.at[dp, :, c])
+            if self.mine is not None:
+                fetch().wait()
+            halve(0)
+            start(4)
+            if not self.direct:
+                start(5)
+            halve(1)
+            if self.direct:
+                start(6)
+            halve(2)
+            if self.direct:
+                start(7)
+            halve(3)
+        elif number == 2 and not self.direct:
+            arrived(5)
+            late = half.at[at_x, high]
+            self.add(late, late, diag.at[1])
+            start(6)
+            arrived(4)
+            late = half.at[at_y, low]
+            self.add(late, late, diag.at[0])
+            start(7)
         elif number == 3:
-            self.arrived(6, self.side.at[0])
-            self.arrived(7, self.side.at[1])
-            self.add(half.at[dp], half.at[dp], self.side.at[0], self.side.at[1])
+            own = half.at[at]
+            if self.direct:
+                arrived(4)
+            arrived(6)
+            arrived(7)
+            self.add(own, own, side.at[0], side.at[1], *((diag,) if self.direct else ()))
             for k in (1, 2, 3):
-                self.push(
-                    7 + k, half.at[dp, (z + k) % 4], self.line.at[k - 1], device(y, x, (z + k) % 4, c)
-                )
+                start(7 + k)
         elif number == 4:
             for k in (1, 2, 3):
-                self.arrived(7 + k, self.line.at[k - 1])
-            self.add(self.out, half.at[dp, z], self.line.at[0], self.line.at[1], self.line.at[2])
+                arrived(7 + k)
+            total = half[at, z].astype(f32) + line[0].astype(f32)
+            self.write(total + line[1].astype(f32) + line[2].astype(f32))
         elif number == 5:
-            for copy in self.sent:
-                copy.wait_send()
+            for msg, ends in enumerate(out):
+                if ends is not None:
+                    self.copy(msg, *ends).wait_send()
 
 
 class Total:
     def __init__(self, value, out, bufs, send, recv, group):
         self.value, self.out, self.send, self.recv, self.group = value, out, send, recv, group
-        self.mine, self.theirs = bufs
-        self.sent = []
+        self.line, self.plane, self.pair = bufs
 
     copy = Gather.copy
 
     def stage(self, number):
         y, x, z, c = place()
-        self.nobody = device(y, x, z, 1 - c)
-        peers = [
-            device(y, x, z, 1 - c),
-            device(y, 1 - x, z, c),
-            device(1 - y, x, z, c),
-            device(y, x, z + 1 - 2 * (z % 2), c),
-            device(y, x, (z + 2) % 4, c),
+        at_x, at_y, at_d, at = y * 2 + 1 - x, (1 - y) * 2 + x, (1 - y) * 2 + 1 - x, y * 2 + x
+        to_c = device(y, x, z, 1 - c)
+        line, plane, pair = self.line, self.plane, self.pair
+        out = [(line.at[z], device(y, x, (z + k) % 4, c)) for k in (1, 2, 3)] + [
+            (plane.at[at], device(y, 1 - x, z, c)),
+            (plane.at[at], device(1 - y, x, z, c)),
+            (plane.at[at], device(1 - y, 1 - x, z, c)),
+            (pair.at[c], to_c),
         ]
-        mine, theirs = self.mine, self.theirs
+        came = [line.at[(z + 4 - k) % 4] for k in (1, 2, 3)]
+        came += [plane.at[dp] for dp in (at_x, at_y, at_d)] + [pair.at[1 - c]]
+
+        def start(msg):
+            self.copy(msg, out[msg][0], out[msg][0], out[msg][1]).start()
+
+        def arrived(msg):
+            self.copy(msg, came[msg], came[msg], to_c).wait_recv()
+
         if number == 0:
-            mine[0] = self.value[...]
-        elif number <= 5:
-            at = number - 1
-            self.copy(at, mine.at[at], theirs.at[at], self.nobody).wait_recv()
-            if number < 5:
-                mine[number] = mine[at] + theirs[at]
-            else:
-                self.out[...] = mine[at] + theirs[at]
-        if number < 5:
-            copy = self.copy(number, mine.at[number], theirs.at[number], peers[number])
-            copy.start()
-            self.sent.append(copy)
-        if number == 6:
-            for copy in self.sent:
-                copy.wait_send()
-
-
-def in_turn(groups, last):
-    for turn in range(len(groups) + last):
-        for at, group in enumerate(groups):
-            if 0 <= turn - at <= last:
-                group.stage(turn - at)
+            line[z] = self.value[...]
+            for msg in (0, 1, 2):
+                start(msg)
+        elif number == 1:
+            for msg in (0, 1, 2):
+                arrived(msg)
+            plane[at] = line[0] + line[1] + line[2] + line[3]
+            for msg in (3, 4, 5):
+                start(msg)
+        elif number == 2:
+            for msg in (3, 4, 5):
+                arrived(msg)
+            pair[c] = plane[0] + plane[1] + plane[2] + plane[3]
+            start(6)
+        elif number == 3:
+            arrived(6)
+            self.out[...] = pair[0] + pair[1]
+        elif number == 5:
+            for msg in range(7):
+                self.copy(msg, out[msg][0], out[msg][0], out[msg][1]).wait_send()
 
 
 def forward_kernel(fast, *refs):
@@ -286,10 +340,10 @@
     b_query, b_value, b_out, gain_first, shift_first = take(5)
     b_up, b_down, gain_second, shift_second, b_feat = take(5)
     output, start_low, q_rows, k_rows, v_rows, dmix_high, dmix_low, dots = take(8)
-    grad_first, probs, grad_down, grad_up, grad_out, sums, sums_up = take(7)
+    grad_first, probs, grad_down, grad_up, grad_out, small = take(6)
     w_feat, w_qkv = take(2) if fast else shards[:2]
     first, act, gin, work, mixed, mixed_low, inverse = take(7)
-    normed_low, grad_branch, grad_att, q_cat, v_cat, k_cat, stage = take(7)
+    normed_low, grad_branch, grad_att, q_cat, v_cat, k_cat, stage, sums, sums_up = take(9)
     prob_sem, stage_sem, load_sem = take(3)
     w_out, w_up, w_down = take(3) if fast else shards[2:]
     width = tokens.shape[1]
@@ -334,17 +388,17 @@
         ids = row_ids(step)
         valid = ids < limit
         camera = jnp.logical_and(ids >= 2, valid)
-        memory = dg(act[rows, :width], matrix(w_feat), 1, 0) + b_feat[...]
+        memory = dg(act[rows, :width], matrix(w_feat), 1, 0) + line_of(b_feat)
         start = act[rows, width : 2 * width].astype(f32) + jnp.where(camera, memory, 0.0)
         first[rows, :] = start
         low = start.astype(bf16)
         start_low[rows, :] = low
         joined = dg(low, matrix(w_qkv), 1, 0)
-        q_rows[rows, :] = ((joined[:, :width] + b_query[...]) * 0.125).astype(bf16)
+        q_rows[rows, :] = ((joined[:, :width] + line_of(b_query)) * 0.125).astype(bf16)
         keys = joined[:, width : 2 * width]
         lead = k_rows[0:16, :][0:1].astype(f32)
         k_rows[rows, :] = jnp.where(valid, keys, lead).astype(bf16)
-        v_rows[rows, :] = (joined[:, 2 * width :] + b_value[...]).astype(bf16)
+        v_rows[rows, :] = (joined[:, 2 * width :] + line_of(b_value)).astype(bf16)
         return carry
 
     lax.fori_loop(0, 4, project, 0)
@@ -450,7 +504,7 @@
     mixed_low[...] = mixed[...].astype(bf16)
     for at, size in chunks(width, 256):
         cols = slice(at, at + size)
-        first[:, cols] += dg(mixed_low[...], matrix(w_out, cols), 0, 0) + b_out[:, cols]
+        first[:, cols] += dg(mixed_low[...], matrix(w_out, cols), 0, 0) + line_of(b_out, cols)
     sums[...] = jnp.zeros_like(sums)
     sums_up[...] = jnp.zeros_like(sums_up)
     cuts = chunks(hidden, 512)
@@ -461,12 +515,12 @@
         rows = rows_of(step)
         valid = row_ids(step) < limit
         unit_first, scale_first = norm_parts(first[rows, :])
-        normed = unit_first * gain_first[...] + shift_first[...]
+        normed = unit_first * line_of(gain_first) + line_of(shift_first)
         low = normed.astype(bf16)
         normed_low[rows, :] = low
         for at, size in cuts:
             cols = slice(at, at + size)
-            inner = dg(low, matrix(w_up, cols), 1, 0) + b_up[:, cols]
+            inner = dg(low, matrix(w_up, cols), 1, 0) + line_of(b_up, cols)
             square = inner * inner
             half = 0.5 + 0.5 * jnp.tanh(inner * (GELU_C + (GELU_C * GELU_A) * square))
             value = inner * half
@@ -474,14 +528,14 @@
             slope = half + value * (1.0 - half) * (2 * GELU_C + (6 * GELU_C * GELU_A) * square)
             for cut, wide in chunks(size, 256):
                 work[(at + cut) // 256, :, :wide] = slope[:, cut : cut + wide]
-        branch = dg(act[rows, :], matrix(w_down), 1, 1) + b_down[...]
+        branch = dg(act[rows, :], matrix(w_down), 1, 1) + line_of(b_down)
         unit_second, scale_second = norm_parts(normed + branch)
-        final = unit_second * gain_second[...] + shift_second[...]
+        final = unit_second * line_of(gain_second) + line_of(shift_second)
         output[rows, :] = jnp.where(valid, final, 0.0).astype(bf16)
         grad = jnp.where(valid, cotangent[rows, :].astype(f32), 0.0)
         sums[0] += fold(grad * unit_second)
         sums[1] += fold(grad)
-        grad_second = norm_back(grad, unit_second, scale_second, gain_second[...])
+        grad_second = norm_back(grad, unit_second, scale_second, line_of(gain_second))
         low_branch = grad_second.astype(bf16)
         grad_branch[rows, :] = low_branch
         sums[2] += fold(low_branch.astype(f32))
@@ -496,7 +550,7 @@
         grad_normed = grad_second + dg(gin[rows, :], matrix(w_up), 1, 1)
         sums[3] += fold(grad_normed * unit_first)
         sums[4] += fold(grad_normed)
-        back = norm_back(grad_normed, unit_first, scale_first, gain_first[...])
+        back = norm_back(grad_normed, unit_first, scale_first, line_of(gain_first))
         grad_first[rows, :] = back
         low_att = back.astype(bf16)
         grad_att[rows, :] = low_att
@@ -504,6 +558,11 @@
         return carry
 
     lax.fori_loop(0, 4, feed, 0)
+    small[...] = jnp.zeros_like(small)
+    for i in range(6):
+        small[i : i + 1, :] = jnp.sum(sums[i], axis=0, keepdims=True)
+    for i, (at, size) in enumerate(chunks(hidden, width)):
+        small[6 + i : 7 + i, :size] = jnp.sum(sums_up[:, at : at + size], axis=0, keepdims=True)
     output[ROWS:, :] = jnp.zeros((SLOTS - ROWS, width), bf16)
 
     for at, size in QBLOCKS:
@@ -523,17 +582,17 @@
         )
 
     pending = {}
-    for turn, (left, right, target, (at, size)) in enumerate(
-        [(grad_branch, act, grad_down, cut) for cut in cuts]
-        + [(normed_low, gin, grad_up, cut) for cut in cuts]
+    for turn, (left, over, right, target, (at, size)) in enumerate(
+        [(grad_branch, 0, act, grad_down, cut) for cut in cuts]
+        + [(normed_low, 0, gin, grad_up, cut) for cut in cuts]
+        + [(mixed_low, 1, grad_att, grad_out, (0, width))]
     ):
         slot = turn % 2
         if slot in pending:
             pending[slot].wait()
-        stage[slot, :, 0:size] = dg(left[...], right[:, at : at + size], 0, 0).astype(bf16)
+        stage[slot, :, 0:size] = dg(left[...], right[:, at : at + size], over, 0).astype(bf16)
         pending[slot] = weight_copy(target, at, size, slot)
         pending[slot].start()
-    grad_out[...] = dg(mixed_low[...], grad_att[...], 1, 0).astype(bf16)
     for copy in pending.values():
         copy.wait()
 
@@ -560,8 +619,7 @@
         shaped((width, hidden), bf16),
         shaped((width, hidden), bf16),
         shaped((width, width), bf16),
-        shaped((6, 8, width), f32),
-        shaped((8, hidden), f32),
+        shaped((-(-(6 + -(-hidden // width)) // 8) * 8, width), f32),
     )
     wholes = [(4, 4, 2) + w.shape for w in weights]
     if fast:
@@ -572,7 +630,7 @@
         functools.partial(forward_kernel, fast),
         out_shape=outs,
         in_specs=[pl.BlockSpec(memory_space=pltpu.SMEM)] + [hbm] * 2 + [vmem] * 16,
-        out_specs=tuple(hbm if i in (9, 10, 11) else vmem for i in range(len(outs))),
+        out_specs=tuple(hbm if i in (9, 10, 11, 12) else vmem for i in range(len(outs))),
         scratch_shapes=[
             pltpu.VMEM((ROWS, width), f32),
             pltpu.VMEM((ROWS, hidden), bf16),
@@ -588,6 +646,8 @@
             pltpu.VMEM((2, 128, ROWS), bf16),
             pltpu.VMEM((ROWS, 256), bf16),
             pltpu.VMEM((2, width, 512), bf16),
+            pltpu.VMEM((6, 8, width), f32),
+            pltpu.VMEM((8, hidden), f32),
             pltpu.SemaphoreType.DMA((4,)),
             pltpu.SemaphoreType.DMA((2,)),
             pltpu.SemaphoreType.DMA((2,)),
@@ -596,8 +656,8 @@
         * (
             [pltpu.VMEM(whole, bf16) for whole in wholes[2:]]
             + [
-                pltpu.SemaphoreType.DMA((7, GATHER_MSGS)),
-                pltpu.SemaphoreType.DMA((7, GATHER_MSGS)),
+                pltpu.SemaphoreType.DMA((7, MESSAGES)),
+                pltpu.SemaphoreType.DMA((7, MESSAGES)),
                 pltpu.SemaphoreType.DMA((7,)),
             ]
         ),
@@ -610,41 +670,97 @@
     )(cameras, tokens, features, cotangent, *weights, *biases)
 
 
-def backward_kernel(
-    cameras,
-    features,
-    q_rows,
-    k_rows,
-    v_rows,
-    dmix_high,
-    dmix_low,
-    dots,
-    start_low,
-    grad_first,
-    probs,
-    w_qkv,
-    w_feat,
-    grad_tokens,
-    grad_features,
-    grad_qkv,
-    grad_feat,
-    sums,
-    feats,
-    weights,
-    grad_scores,
-    joined,
-    d_cat,
-    d_rows,
-    v_cat,
-    k_turned,
-    grad_memory,
-    prob_sem,
-    load_sem,
-):
+def reduce_plan(width, hidden):
+    half = hidden // 256 * 128
+    plan = [(which, cols, False) for which in (0, 1) for cols in ((0, half), (half, hidden - half))]
+    plan += [(2, (0, width), False)]
+    plan += [(3, (pair * 384, 384), False) for pair in range(width // 128)]
+    return plan + [(4, (0, width), True)]
+
+
+HOOKS = {
+    (0, 0): ((1, 0), (1, 10)),
+    (0, 1): ((1, 1),),
+    (0, 2): ((2, 0), (2, 10)),
+    (1, 0): ((1, 2), (0, 5), (3, 10)),
+    (1, 1): ((2, 1), (1, 5)),
+    (1, 2): ((3, 0), (1, 3)),
+    (2, 0): ((2, 2), (0, 6), (2, 5)),
+    (2, 1): ((3, 1), (1, 4), (1, 6)),
+    (2, 2): ((2, 3), (4, 0), (3, 5)),
+    (3, 0): ((3, 2), (0, 7), (2, 6)),
+    (3, 1): ((2, 4), (1, 7), (4, 1), (4, 5)),
+    (3, 2): ((3, 3), (3, 6)),
+    "pairs": ((0, 8), (2, 7), (4, 2)),
+    "rows0": ((1, 8), (3, 4), (4, 3)),
+    "rows1": ((3, 7), (4, 6)),
+    "rows2": ((2, 8),),
+    "feat": ((0, 9), (4, 4), (0, 11)),
+    "half": ((3, 8), (1, 9), (1, 11), (4, 7)),
+    "end": ((4, 8), (2, 11), (3, 9), (3, 11), (4, 9)),
+}
+
+
+def backward_kernel(fast, *refs):
+    refs = list(refs)
+    take = lambda count: [refs.pop(0) for _ in range(count)]
+    cameras, features, q_rows, k_rows, v_rows, dmix_high, dmix_low, dots = take(8)
+    start_low, grad_first, probs, w_qkv, w_feat = take(5)
+    if fast:
+        grad_down, grad_up, grad_out, small = take(4)
+        grad_tokens, grad_features, *summed = take(7)
+        total, total_late = take(2)
+    else:
+        grad_tokens, grad_features, grad_qkv, grad_feat, small_late = take(5)
+    feats, weights, grad_scores, joined, d_cat, d_rows, v_cat = take(7)
+    k_turned, grad_memory, pair_rows, sums, prob_sem, load_sem = take(6)
     width = q_rows.shape[1]
     heads = width // HEAD
     pairs = heads // 2
     limit = 2 + CAM_LEN * cameras[0]
+    if fast:
+        small_late, part_qkv, part_feat = take(3)
+        send, recv, local = refs[-3:]
+        plan = reduce_plan(width, grad_up.shape[-1])
+        parts_of = (grad_down, grad_up, grad_out, part_qkv, part_feat)
+
+        def writer(which, cols):
+            def write(value):
+                if which == 3:
+                    pair = cols[0] // 384
+                    for i in range(3):
+                        at = i * width + pair * 128
+                        summed[3][:, at : at + 128] = value[:, i * 128 : i * 128 + 128]
+                else:
+                    summed[which][:, cols[0] : cols[0] + cols[1]] = value
+
+            return write
+
+        groups = []
+        for i, (which, cols, direct) in enumerate(plan):
+            bufs = take(4)
+            mine = take(1)[0] if which < 3 else None
+            groups.append(
+                Reduce(
+                    parts_of[which], cols, writer(which, cols), bufs, mine, direct, send, recv, local, i
+                )
+            )
+        groups.append(Total(small, total, take(3), send, recv, len(plan)))
+        groups.append(Total(small_late, total_late, take(3), send, recv, len(plan) + 1))
+        greet()
+        turns(groups, *[(0, i) for i in range(5)], (0, 10))
+
+    def hook(where):
+        if fast:
+            turns(groups, *HOOKS[where])
+
+    def pair_hook(pair, spot):
+        if fast:
+            for at_pair in range(pairs):
+
+                @pl.when(pair == at_pair)
+                def _():
+                    hook((at_pair, spot))
 
     def prob_copy(pair, side):
         slot = 2 * lax.rem(pair, 2) + side
@@ -659,6 +775,7 @@
     sums[...] = jnp.zeros_like(sums)
     lane_valid = lax.broadcasted_iota(jnp.int32, (1, ROWS), 1) < limit
     row_valid = lax.broadcasted_iota(jnp.int32, (ROWS, 1), 0) < limit
+    none = jnp.zeros((HEAD, ROWS), bf16)
 
     def attend_back(pair, carry):
         lanes = pl.ds(pl.multiple_of(pair * 128, 128), 128)
@@ -668,10 +785,9 @@
             prob_copy(pair + 1, 0).start()
             prob_copy(pair + 1, 1).start()
 
-        both = pl.ds(pl.multiple_of(pair * 128, 128), 128)
-        high = dmix_high[both, :]
-        low = dmix_low[both, :]
-        none = jnp.zeros((HEAD, ROWS), bf16)
+        pair_hook(pair, 0)
+        high = dmix_high[lanes, :]
+        low = dmix_low[lanes, :]
         for side in range(2):
             own = slice(side * HEAD, side * HEAD + HEAD)
             mine, its = side * HEAD, (1 - side) * HEAD
@@ -718,6 +834,8 @@
         for side in range(2):
             prob_copy(pair, side).wait()
         for job in range(len(jobs)):
+            if job == len(QBLOCKS):
+                pair_hook(pair, 1)
             slope(job)
             if job >= 1:
                 queries(job - 1)
@@ -726,26 +844,39 @@
                 if side_job < len(parts):
                     spread(0, parts[side_job])
         queries(len(jobs) - 1)
+        pair_hook(pair, 2)
         first_lane = lax.broadcasted_iota(jnp.int32, (STEP, 128), 1) < HEAD
         for part in parts:
             spread(1, part)
             here = slice(part[0], part[0] + part[1])
             keep = row_valid[here]
-            for which, at in ((0, 2 * width), (1, width)):
+            for which, at in ((0, 2), (1, 1)):
                 value = jnp.where(first_lane, wide[0, part][which], wide[1, part][which])
                 value = jnp.where(keep, value, 0.0).astype(bf16)
-                joined[here, pl.ds(pl.multiple_of(at + pair * 128, 128), 128)] = value
+                joined[here, pl.ds(pl.multiple_of(at * width + pair * 128, 128), 128)] = value
+                pair_rows[here, at * 128 : at * 128 + 128] = value
         query = jnp.concatenate(
             [jnp.concatenate(turned[0], axis=1), jnp.concatenate(turned[1], axis=1)], axis=0
         )
-        joined[:, lanes] = (query.astype(bf16).astype(f32).T * 0.125).astype(bf16)
+        query = (query.astype(bf16).astype(f32).T * 0.125).astype(bf16)
+        joined[:, lanes] = query
+        pair_rows[:, :128] = query
+        grad = dg(start_low[...], pair_rows[...], 0, 0).astype(bf16)
+        if fast:
+            at = pl.ds(pl.multiple_of(pair * 384, 128), 384)
+            part_qkv[:, :, :, :, at] = grad.reshape(part_qkv.shape[:4] + (384,))
+        else:
+            for i in range(3):
+                at = pl.ds(pl.multiple_of(i * width + pair * 128, 128), 128)
+                grad_qkv[:, at] = grad[:, i * 128 : i * 128 + 128]
         return carry
 
     lax.fori_loop(0, pairs, attend_back, 0)
     load.wait()
-
-    def project_back(step, carry):
-        rows = pl.ds(pl.multiple_of(step * STEP, 16), STEP)
+    hook("pairs")
+
+    for step in range(4):
+        rows = slice(step * STEP, step * STEP + STEP)
         ids = step * STEP + lax.broadcasted_iota(jnp.int32, (STEP, 1), 0)
         camera = jnp.logical_and(ids >= 2, ids < limit)
         part = joined[rows, :]
@@ -756,92 +887,139 @@
         low = jnp.where(camera, grad_start, 0.0).astype(bf16)
         grad_memory[rows, :] = low
         sums[2] += fold(low.astype(f32))
-        grad_features[rows, :] = dg(low, w_feat[...], 1, 1).astype(bf16)
-        return carry
-
-    lax.fori_loop(0, 4, project_back, 0)
+        if step < 3:
+            hook(f"rows{step}")
+    grad = dg(feats[...], grad_memory[...], 0, 0).astype(bf16)
+    small_late[...] = jnp.zeros_like(small_late)
+    for i in range(3):
+        small_late[i : i + 1, :] = jnp.sum(sums[i], axis=0, keepdims=True)
+    if fast:
+        part_feat[...] = grad.reshape(part_feat.shape)
+    else:
+        grad_feat[...] = grad
+    hook("feat")
+    for step in range(4):
+        rows = slice(step * STEP, step * STEP + STEP)
+        grad_features[rows, :] = dg(grad_memory[rows, :], w_feat[...], 1, 1).astype(bf16)
+        if step == 1:
+            hook("half")
     grad_tokens[ROWS:, :] = jnp.zeros((SLOTS - ROWS, width), bf16)
     grad_features[ROWS:, :] = jnp.zeros((SLOTS - ROWS, width), bf16)
-    for at, size in chunks(3 * width, 512):
-        cols = slice(at, at + size)
-        grad_qkv[:, cols] = dg(start_low[...], joined[:, cols], 0, 0).astype(bf16)
-    grad_feat[...] = dg(feats[...], grad_memory[...], 0, 0).astype(bf16)
-
-
-def backward_call(cameras, features, saved, w_qkv, w_feat):
+    hook("end")
+    if fast:
+        turns(groups, *[(5, i) for i in range(len(groups))])
+
+
+def backward_call(fast, cameras, features, saved, w_qkv, w_feat, grads, small):
     width = features.shape[1]
     heads = width // HEAD
-    outs = (
-        shaped((SLOTS, width), bf16),
-        shaped((SLOTS, width), bf16),
-        shaped((width, 3 * width), bf16),
-        shaped((width, width), bf16),
-        shaped((3, 8, width), f32),
-    )
+    vmem = pl.BlockSpec(memory_space=pltpu.VMEM)
+    hbm = pl.BlockSpec(memory_space=pl.ANY)
+    scratch = [
+        pltpu.VMEM((ROWS, width), bf16),
+        pltpu.VMEM((4, ROWS, 1280), bf16),
+        pltpu.VMEM((2, ROWS, 1280), bf16),
+        pltpu.VMEM((ROWS, 3 * width), bf16),
+        pltpu.VMEM((2, 256, ROWS), bf16),
+        pltpu.VMEM((ROWS, 256), bf16),
+        pltpu.VMEM((ROWS, 256), bf16),
+        pltpu.VMEM((128, ROWS), bf16),
+        pltpu.VMEM((ROWS, width), bf16),
+        pltpu.VMEM((ROWS, 384), bf16),
+        pltpu.VMEM((3, 8, width), f32),
+        pltpu.SemaphoreType.DMA((4,)),
+        pltpu.SemaphoreType.DMA(()),
+    ]
+    outs = (shaped((SLOTS, width), bf16),) * 2
+    inputs = [cameras, features, *saved, w_qkv, w_feat]
+    specs = [pl.BlockSpec(memory_space=pltpu.SMEM), hbm] + [vmem] * 8 + [hbm] + [vmem] * 2
+    if fast:
+        hidden = grads[0].shape[1]
+        rows = width // 32
+        late = (8, width)
+        outs += tuple(shaped((rows, n), f32) for n in (hidden, hidden, width, 3 * width, width))
+        outs += (shaped(small.shape, f32), shaped(late, f32))
+        inputs += [grad.reshape(4, 4, 2, rows, -1) for grad in grads] + [small]
+        specs += [hbm] * 3 + [vmem]
+        scratch += [
+            pltpu.VMEM(late, f32),
+            pltpu.VMEM((4, 4, 2, rows, 3 * width), bf16),
+            pltpu.VMEM((4, 4, 2, rows, width), bf16),
+        ]
+        plan = reduce_plan(width, hidden)
+        for which, (_, size), direct in plan:
+            scratch += [
+                pltpu.VMEM((4, 4, rows, size), bf16),
+                pltpu.VMEM((4, rows, size) if direct else (2, 2, rows, size), bf16),
+                pltpu.VMEM((2, 4, rows, size), bf16),
+                pltpu.VMEM((3, rows, size), bf16),
+            ]
+            if which < 3:
+                scratch += [pltpu.VMEM((4, 4, rows, size), bf16)]
+        for shape in (small.shape, late):
+            scratch += [pltpu.VMEM((count,) + shape, f32) for count in (4, 4, 2)]
+        scratch += [
+            pltpu.SemaphoreType.DMA((len(plan) + 2, MESSAGES)),
+            pltpu.SemaphoreType.DMA((len(plan) + 2, MESSAGES)),
+            pltpu.SemaphoreType.DMA((len(plan),)),
+        ]
+    else:
+        outs += (
+            shaped((width, 3 * width), bf16),
+            shaped((width, width), bf16),
+            shaped((8, width), f32),
+        )
+    return pl.pallas_call(
+        functools.partial(backward_kernel, fast),
+        out_shape=outs,
+        in_specs=specs,
+        out_specs=(vmem,) * len(outs),
+        scratch_shapes=scratch,
+        compiler_params=pltpu.CompilerParams(
+            vmem_limit_bytes=62 * MIB,
+            collective_id=1 if fast else None,
+            has_side_effects=fast,
+        ),
+        name="layer_backward",
+    )(*inputs)
+
+
+def finish_kernel(*refs):
+    refs = list(refs)
+    take = lambda count: [refs.pop(0) for _ in range(count)]
+    sources, (small, late), targets = take(8), take(2), take(8)
+    vectors, sem = take(10), refs[0]
+    copies = [
+        pltpu.make_async_copy(source, target, sem.at[i])
+        for i, (source, target) in enumerate(zip(sources, targets))
+    ]
+    for copy in copies:
+        copy.start()
+    places = ((late, 0), (late, 1), (small, 5), (small, 3), (small, 4), None)
+    places += ((small, 2), (small, 0), (small, 1), (late, 2))
+    for vector, spot in zip(vectors, places):
+        if spot is None:
+            for i, (at, size) in enumerate(chunks(vector.shape[0], small.shape[1])):
+                vector[at : at + size] = small[6 + i, :size]
+        else:
+            vector[...] = spot[0][spot[1]]
+    for copy in copies:
+        copy.wait()
+
+
+def finish_call(large, small, late, hidden):
+    width = small.shape[1]
     vmem = pl.BlockSpec(memory_space=pltpu.VMEM)
     hbm = pl.BlockSpec(memory_space=pl.ANY)
     return pl.pallas_call(
-        backward_kernel,
-        out_shape=outs,
-        in_specs=[pl.BlockSpec(memory_space=pltpu.SMEM), hbm] + [vmem] * 8 + [hbm] + [vmem] * 2,
-        out_specs=(vmem,) * 5,
-        scratch_shapes=[
-            pltpu.VMEM((ROWS, width), bf16),
-            pltpu.VMEM((4, ROWS, 1280), bf16),
-            pltpu.VMEM((2, ROWS, 1280), bf16),
-            pltpu.VMEM((ROWS, 3 * width), bf16),
-            pltpu.VMEM((2, 256, ROWS), bf16),
-            pltpu.VMEM((ROWS, 256), bf16),
-            pltpu.VMEM((ROWS, 256), bf16),
-            pltpu.VMEM((128, ROWS), bf16),
-            pltpu.VMEM((ROWS, width), bf16),
-            pltpu.SemaphoreType.DMA((4,)),
-            pltpu.SemaphoreType.DMA(()),
-        ],
-        compiler_params=pltpu.CompilerParams(vmem_limit_bytes=62 * MIB),
-        name="layer_backward",
-    )(cameras, features, *saved, w_qkv, w_feat)
-
-
-def reduce_bufs(columns, rows):
-    return [
-        pltpu.VMEM((4, 4, rows, columns), bf16),
-        pltpu.VMEM((2, 2, rows, columns), bf16),
-        pltpu.VMEM((2, 4, rows, columns), bf16),
-        pltpu.VMEM((3, rows, columns), bf16),
-    ]
-
-
-def reduce_kernel(*refs):
-    parts, small, outs, small_out, bufs = refs[:5], refs[5], refs[6:11], refs[11], refs[12:-2]
-    send, recv = refs[-2:]
-    greet()
-    groups = [
-        Reduce(parts[i], outs[i], bufs[4 * i : 4 * i + 4], send, recv, i) for i in range(5)
-    ]
-    groups.append(Total(small, small_out, bufs[20:22], send, recv, 5))
-    in_turn(groups, 6)
-
-
-def reduce_call(grads, small):
-    vmem = pl.BlockSpec(memory_space=pltpu.VMEM)
-    rows = grads[0].shape[0] // 32
-    parts = [grad.reshape(4, 4, 2, rows, grad.shape[1]) for grad in grads]
-    bufs = [buf for grad in grads for buf in reduce_bufs(grad.shape[1], rows)]
-    bufs += [pltpu.VMEM((5,) + small.shape, f32)] * 2
-    return pl.pallas_call(
-        reduce_kernel,
-        out_shape=tuple(shaped((rows, grad.shape[1]), f32) for grad in grads)
-        + (shaped(small.shape, f32),),
-        in_specs=[vmem] * 6,
-        out_specs=(vmem,) * 6,
-        scratch_shapes=bufs
-        + [pltpu.SemaphoreType.DMA((6, GATHER_MSGS)), pltpu.SemaphoreType.DMA((6, GATHER_MSGS))],
-        compiler_params=pltpu.CompilerParams(
-            collective_id=1, has_side_effects=True, vmem_limit_bytes=62 * MIB
-        ),
-        name="reduce_gradients",
-    )(*parts, small)
+        finish_kernel,
+        out_shape=tuple(shaped(a.shape, a.dtype) for a in large)
+        + tuple(shaped((hidden if i == 5 else width,), f32) for i in range(10)),
+        in_specs=[vmem] * 10,
+        out_specs=(hbm,) * 8 + (vmem,) * 10,
+        scratch_shapes=[pltpu.SemaphoreType.DMA((8,))],
+        name="place_outputs",
+    )(*large, small, late)
 
 
 AXES = ("dp", "fsdp")
@@ -862,79 +1040,33 @@
 ):
     width = tokens.shape[1]
     hidden = w_up.shape[1]
-    biases = [bias.reshape(1, -1) for bias in biases]
-    shards = (w_feat, w_qkv, w_out, w_up, w_down)
-    weights = shards
+    weights = (w_feat, w_qkv, w_out, w_up, w_down)
     if not fast:
-        weights = tuple(lax.all_gather(w, AXES, axis=0, tiled=True) for w in shards)
-    (
-        output,
-        start_low,
-        q_rows,
-        k_rows,
-        v_rows,
-        dmix_high,
-        dmix_low,
-        dots,
-        grad_first,
-        probs,
-        grad_down,
-        grad_up,
-        grad_out,
-        sums,
-        sums_up,
-        *wholes,
-    ) = forward_call(fast, cameras, tokens, features, cotangent, weights, biases)
+        weights = tuple(lax.all_gather(w, AXES, axis=0, tiled=True) for w in weights)
+    output, start_low, *rest = forward_call(fast, cameras, tokens, features, cotangent, weights, biases)
+    q_rows, k_rows, v_rows, dmix_high, dmix_low, dots, grad_first, probs, *rest = rest
+    grad_down, grad_up, grad_out, small, *wholes = rest
     if fast:
         weights = [whole.reshape(width, -1) for whole in wholes]
     saved = (q_rows, k_rows, v_rows, dmix_high, dmix_low, dots, start_low, grad_first, probs)
-    grad_tokens, grad_features, grad_qkv, grad_feat, sums_back = backward_call(
-        cameras, features, saved, weights[1], weights[0]
+    grads = (grad_down, grad_up, grad_out)
+    grad_tokens, grad_features, *rest = backward_call(
+        fast, cameras, features, saved, weights[1], weights[0], grads, small
     )
-    grads = (grad_down, grad_up, grad_out, grad_qkv, grad_feat)
-    small = jnp.concatenate(
-        [
-            jnp.sum(sums, axis=1).reshape(-1),
-            jnp.sum(sums_back, axis=1).reshape(-1),
-            jnp.sum(sums_up, axis=0),
-        ]
-    )
-    lines = -(-small.shape[0] // 1024) * 8
-    small = jnp.pad(small, (0, lines * 128 - small.shape[0])).reshape(lines, 128)
-    if fast:
-        *grads, small = reduce_call(grads, small)
+    if fast:
+        *grads, small, late = rest
     else:
+        grads += tuple(rest[:2])
         grads = [
             lax.psum_scatter(
                 lax.optimization_barrier(grad.astype(f32)), AXES, scatter_dimension=0, tiled=True
             )
             for grad in grads
         ]
-        small = lax.psum(small, AXES)
-    small = small.reshape(-1)
-    rows = small[: 9 * width].reshape(9, width)
-    grad_b_up = small[9 * width : 9 * width + hidden]
+        small, late = lax.psum((small, rest[2]), AXES)
     grad_down, grad_up, grad_out, grad_qkv, grad_feat = grads
-    return (
-        output,
-        grad_tokens,
-        grad_features,
-        grad_qkv,
-        grad_out,
-        grad_up,
-        grad_down,
-        grad_feat,
-        rows[6],
-        rows[7],
-        rows[5],
-        rows[3],
-        rows[4],
-        grad_b_up,
-        rows[2],
-        rows[0],
-        rows[1],
-        rows[8],
-    )
+    large = (output, grad_tokens, grad_features, grad_qkv, grad_out, grad_up, grad_down, grad_feat)
+    return finish_call(large, small, late, hidden)
 
 
 def solution(mesh):

time: 232 us -> 186 us (0.80)
  Pallas kernels: 218 us -> 184 us
  local copies, waits for them, and re-layouts: 8.36 us -> 0 us
  other arithmetic: 3.3 us -> 0 us
    pallas_call x2, Pallas kernels: 112 us -> 77.4 us  [the longest x1 72.4 us: backward_call(): pl.pallas_call(functools.partial(backward_kernel, fast), out_shape=outs,...]
    unnamed x18 -> x0, local copies, waits for them, and re-layouts: 4.31 us -> none
    reduce_sum x3 -> x0, other arithmetic: 2.68 us -> none  [the longest x1 0.93 us: on_device(): jnp.sum(sums_up, axis=0)]
where the time goes in v3:
time: 186 us
  Pallas kernels  184 us (99%)
    pallas_call x1, Pallas kernels, forward_call(): pl.pallas_call(functools.partial(forward_kernel, fast), out_shape=outs, i...  107 us
    pallas_call x1, Pallas kernels, backward_call(): pl.pallas_call(functools.partial(backward_kernel, fast), out_shape=outs,...  72.4 us
    pallas_call x1, Pallas kernels, finish_call(): pl.pallas_call(finish_kernel, out_shape=tuple((shaped(a.shape, a.dtype) f...  5.02 us

profile of v3, /device:TPU:0, one launch (start us, length us, event | category | flops | bytes accessed | tf_op | source)
XLA Modules:
  0.0 185.8 jit_solution(13390383583227082166)
XLA Ops:
  1.3 106.8 %layer_forward.1 = (bf16[1280,512]{1,0:T(8,128)(2,1)}, bf16[1216,512]{1,0:T(8,128)(2,1)}, bf16[1216,512]{1,0:T(8,128)(2,1)}, bf16[1216,512]{1,0:T(8,128)(2,1)}, ...) custom-call(s32[1]{0:T(128)S(6)} %copy.37.refs_0_, ...), custom_call_target="tpu_custom_call" | custom-call | tf_op jit(solution)/shard_map/layer_forward/pallas_call | solution.py:629
  108.2 72.4 %layer_backward.1 = (bf16[1280,512]{1,0:T(8,128)(2,1)}, bf16[1280,512]{1,0:T(8,128)(2,1)}, f32[16,3200]{1,0:T(8,128)}, f32[16,3200]{1,0:T(8,128)}, f32[16,512]{1...) custom-call(s32[1]{0:T(128)S(6)} %copy.37.refs_0_, ...), custom_call_target="tpu_custom_call" | custom-call | tf_op jit(solution)/shard_map/layer_backward/pallas_call | solution.py:972
  180.6 5.0 %place_outputs.1 = (bf16[1280,512]{1,0:T(8,128)(2,1)}, bf16[1280,512]{1,0:T(8,128)(2,1)}, bf16[1280,512]{1,0:T(8,128)(2,1)}, f32[16,1536]{1,0:T(8,128)}, f32[16,...) custom-call(bf16[1280,512]{1,0:T(8,128)(2,1)} %get-tuple-element.43., ...), custom_call_target="tpu_custom_call" | custom-call | tf_op jit(solution)/shard_map/place_outputs/pallas_call | solution.py:1014

commit v4 on v3

--- a/solution.py
+++ b/solution.py
@@ -176,9 +176,9 @@
 
 
 class Reduce:
-    def __init__(self, part, cols, write, bufs, mine, direct, send, recv, local, group):
-        self.part, self.cols, self.write, self.mine, self.direct = part, cols, write, mine, direct
-        self.send, self.recv, self.local, self.group = send, recv, local, group
+    def __init__(self, part, cols, write, bufs, direct, send, recv, group):
+        self.part, self.cols, self.write, self.direct = part, cols, write, direct
+        self.send, self.recv, self.group = send, recv, group
         self.half, self.diag, self.side, self.line = bufs
 
     copy = Gather.copy
@@ -199,13 +199,7 @@
         to_d = device(1 - y, 1 - x, z, c)
         cols = pl.ds(*self.cols)
         half, diag, side, line = self.half, self.diag, self.side, self.line
-        if self.mine is None:
-            mine = lambda dp: self.part.at[dp, :, c, :, cols]
-        else:
-            mine = lambda dp: self.mine.at[dp]
-            fetch = lambda: pltpu.make_async_copy(
-                self.part.at[:, :, c, :, cols], self.mine, self.local.at[self.group]
-            )
+        mine = lambda dp: self.part.at[dp, :, c, :, cols]
         low, high = pl.ds(0, 2), pl.ds(2, 2)
         blocks = (at_d, at_x, at_y, at)
         out = [(self.part.at[dp, :, 1 - c, :, cols], half.at[dp], to_c) for dp in blocks]
@@ -237,11 +231,7 @@
         if number == 0:
             for msg in range(4):
                 start(msg)
-            if self.mine is not None:
-                fetch().start()
         elif number == 1:
-            if self.mine is not None:
-                fetch().wait()
             halve(0)
             start(4)
             if not self.direct:
@@ -332,36 +322,76 @@
                 self.copy(msg, out[msg][0], out[msg][0], out[msg][1]).wait_send()
 
 
+GATHER_HOOKS = {
+    "start": ((0, 0), (0, 1)) + tuple((0, i) for i in range(2, 10)),
+    "first": ((1, 0), (1, 1), (1, 2), (2, 0), (2, 1), (1, 3), (3, 0), (3, 1), (4, 0)),
+    0: ((1, 4), (2, 2), (1, 5), (4, 1)),
+    1: ((3, 2), (2, 3), (1, 6), (4, 2)),
+    2: ((3, 3), (2, 4), (2, 5), (1, 7), (4, 3)),
+    3: ((3, 4), (3, 5), (2, 6), (1, 8), (4, 4)),
+    "out": ((2, 7), (3, 6), (1, 9), (4, 5)),
+    "up": ((3, 7), (4, 6), (4, 7)),
+    "up1": ((2, 8),),
+    "up2": ((3, 8), (2, 9)),
+    "down": ((3, 9), (4, 8), (4, 9)) + tuple((5, i) for i in range(10)),
+}
+
+
+def gather_plan(width, hidden):
+    half = hidden // 256 * 128
+    plan = [(0, (0, width))] + [(1, (pair * 384, 384)) for pair in range(width // 128)]
+    plan += [(2, (0, width))]
+    return plan + [(which, cols) for which in (3, 4) for cols in ((0, half), (half, hidden - half))]
+
+
 def forward_kernel(fast, *refs):
     refs = list(refs)
     take = lambda count: [refs.pop(0) for _ in range(count)]
-    cameras, tokens, features, cotangent = take(4)
+    cameras, tokens, features, cotangent_in = take(4)
     shards = take(5)
     b_query, b_value, b_out, gain_first, shift_first = take(5)
     b_up, b_down, gain_second, shift_second, b_feat = take(5)
-    output, start_low, q_rows, k_rows, v_rows, dmix_high, dmix_low, dots = take(8)
-    grad_first, probs, grad_down, grad_up, grad_out, small = take(6)
-    w_feat, w_qkv = take(2) if fast else shards[:2]
-    first, act, gin, work, mixed, mixed_low, inverse = take(7)
-    normed_low, grad_branch, grad_att, q_cat, v_cat, k_cat, stage, sums, sums_up = take(9)
-    prob_sem, stage_sem, load_sem = take(3)
-    w_out, w_up, w_down = take(3) if fast else shards[2:]
+    stored = take(14)
+    probs, dots, small = take(3)
+    wholes_out = take(2) if fast else []
+    kept = take(14)
+    output, start_low, q_rows, k_rows, v_rows, dmix_high, dmix_low = kept[:7]
+    grad_first, act, gin, normed_low, grad_branch, grad_att, mixed_low = kept[7:]
+    first, work, mixed, inverse, q_cat, v_cat, k_cat, cotangent, sums, sums_up = take(10)
+    prob_sem, load_sem, store_sem, step_sem = take(4)
+    w_feat, w_qkv, w_out, w_up, w_down = take(5) if fast else shards
     width = tokens.shape[1]
     hidden = w_up.shape[-1]
-    if fast:
-        send, recv, local = take(3)
-        half = hidden // 256 * 128
-        wholes = (w_feat, w_qkv, w_out, w_up, w_up, w_down, w_down)
-        pieces = ((0, width), (0, 3 * width), (0, width)) + ((0, half), (half, hidden - half)) * 2
-        gather = [
-            Gather(shards[which], whole, cols, send, recv, local, i)
-            for i, (which, whole, cols) in enumerate(zip((0, 1, 2, 3, 3, 4, 4), wholes, pieces))
-        ]
-        greet()
-        turns(gather, (0, 0), (0, 1))
     heads = width // HEAD
     pairs = heads // 2
     limit = 2 + CAM_LEN * cameras[0]
+    if fast:
+        turned_shard, send, recv, local = take(4)
+        for pair in range(pairs):
+            for i in range(3):
+                at = i * width + pair * 128
+                turned_shard[:, pair * 384 + i * 128 : pair * 384 + i * 128 + 128] = shards[1][
+                    :, at : at + 128
+                ]
+        shards[1] = turned_shard
+        wholes = (w_feat, w_qkv, w_out, w_up, w_down)
+        gather = [
+            Gather(shards[which], wholes[which], cols, send, recv, local, i)
+            for i, (which, cols) in enumerate(gather_plan(width, hidden))
+        ]
+        greet()
+
+    def hook(where):
+        if fast:
+            turns(gather, *GATHER_HOOKS[where])
+
+    def hooks(step, where):
+        if fast:
+            for at_step, name in where:
+
+                @pl.when(step == at_step)
+                def _():
+                    hook(name)
 
     def rows_of(step):
         return pl.ds(pl.multiple_of(step * STEP, 16), STEP)
@@ -369,39 +399,48 @@
     def row_ids(step):
         return step * STEP + lax.broadcasted_iota(jnp.int32, (STEP, 1), 0)
 
+    def store(i, source=None, target=None):
+        return pltpu.make_async_copy(
+            kept[i] if source is None else source,
+            stored[i] if target is None else target,
+            store_sem.at[i],
+        )
+
+    def store_step(i, step):
+        which = 0 if i == 8 else 1
+        rows = rows_of(step)
+        return pltpu.make_async_copy(
+            kept[i].at[rows, :], stored[i].at[rows, :], step_sem.at[4 * which + step]
+        )
+
+    hook("start")
     loads = [
         pltpu.make_async_copy(
             source.at[pl.ds(0, ROWS), :], act.at[:, pl.ds(i * width, width)], load_sem.at[i]
         )
         for i, source in enumerate((features, tokens))
     ]
+    loads.append(
+        pltpu.make_async_copy(cotangent_in.at[pl.ds(0, ROWS), :], cotangent, load_sem.at[2])
+    )
     for load in loads:
         load.start()
-    if fast:
-        turns(gather, (1, 0), (1, 1), (0, 2), (0, 3), (0, 4), (0, 5), (0, 6), (2, 0), (2, 1))
-        turns(gather, (3, 0), (3, 1), (4, 0), (4, 1), (1, 2))
+    hook("first")
     for load in loads:
         load.wait()
 
     def project(step, carry):
         rows = rows_of(step)
         ids = row_ids(step)
-        valid = ids < limit
-        camera = jnp.logical_and(ids >= 2, valid)
+        camera = jnp.logical_and(ids >= 2, ids < limit)
         memory = dg(act[rows, :width], matrix(w_feat), 1, 0) + line_of(b_feat)
         start = act[rows, width : 2 * width].astype(f32) + jnp.where(camera, memory, 0.0)
         first[rows, :] = start
-        low = start.astype(bf16)
-        start_low[rows, :] = low
-        joined = dg(low, matrix(w_qkv), 1, 0)
-        q_rows[rows, :] = ((joined[:, :width] + line_of(b_query)) * 0.125).astype(bf16)
-        keys = joined[:, width : 2 * width]
-        lead = k_rows[0:16, :][0:1].astype(f32)
-        k_rows[rows, :] = jnp.where(valid, keys, lead).astype(bf16)
-        v_rows[rows, :] = (joined[:, 2 * width :] + line_of(b_value)).astype(bf16)
+        start_low[rows, :] = start.astype(bf16)
         return carry
 
     lax.fori_loop(0, 4, project, 0)
+    store(1).start()
 
     lane_valid = lax.broadcasted_iota(jnp.int32, (1, ROWS), 1) < limit
 
@@ -414,20 +453,26 @@
 
     def attend(pair, carry):
         lanes = pl.ds(pl.multiple_of(pair * 128, 128), 128)
-        if fast:
-            for at_pair in range(pairs):
-
-                @pl.when(pair == at_pair)
-                def _():
-                    turns(gather, (1, at_pair + 3), (2, at_pair + 2))
-                    if at_pair:
-                        turns(gather, (3, at_pair + 1))
+        hooks(pair, [(i, i) for i in range(pairs)])
 
         @pl.when(pair >= 2)
         def _():
             prob_copy(pair - 2, 0).wait()
             prob_copy(pair - 2, 1).wait()
 
+        w_pair = matrix(w_qkv, pl.ds(pl.multiple_of(pair * 384, 128), 384))
+        for step in range(4):
+            rows = slice(step * STEP, step * STEP + STEP)
+            part = dg(start_low[rows, :], w_pair, 1, 0)
+            q_rows[rows, lanes] = ((part[:, :128] + line_of(b_query, lanes)) * 0.125).astype(bf16)
+            keys = part[:, 128:256]
+            if step == 0:
+                lead = keys[0:1]
+            keys = jnp.where(row_ids(step) < limit, keys, lead).astype(bf16)
+            k_rows[rows, lanes] = keys
+            k_cat[rows, :128] = keys
+            k_cat[rows, 128:] = keys
+            v_rows[rows, lanes] = (part[:, 256:] + line_of(b_value, lanes)).astype(bf16)
         queries = q_rows[:, lanes].astype(f32).T * LOG2E
         high, low = split_low(queries)
         none = jnp.zeros((HEAD, ROWS), bf16)
@@ -442,9 +487,6 @@
             q_cat[side, 128 + (1 - side) * HEAD : 128 + (1 - side) * HEAD + HEAD, :] = none
             v_cat[side, :HEAD, :] = values[own]
             v_cat[side, HEAD:, :] = ones
-        keys = k_rows[:, lanes]
-        k_cat[:, :128] = keys
-        k_cat[:, 128:] = keys
         base = lax.rem(pair, 2) * 1280
         jobs = [(side, at, size) for side in range(2) for at, size in QBLOCKS]
         peak = {}
@@ -499,24 +541,24 @@
         for side in range(2):
             prob_copy(pair, side).wait()
 
-    if fast:
-        turns(gather, (2, 6), (3, 5), (4, 2))
+    for i in (2, 3, 4):
+        store(i).start()
+    hook("out")
     mixed_low[...] = mixed[...].astype(bf16)
+    store(13).start()
     for at, size in chunks(width, 256):
         cols = slice(at, at + size)
         first[:, cols] += dg(mixed_low[...], matrix(w_out, cols), 0, 0) + line_of(b_out, cols)
     sums[...] = jnp.zeros_like(sums)
     sums_up[...] = jnp.zeros_like(sums_up)
     cuts = chunks(hidden, 512)
-    if fast:
-        turns(gather, (3, 6), (4, 3), (4, 4), (4, 5), (4, 6), *[(5, i) for i in range(7)])
-
-    def feed(step, carry):
+    hook("up")
+
+    def widen(step, carry):
+        hooks(step, [(1, "up1"), (2, "up2")])
         rows = rows_of(step)
-        valid = row_ids(step) < limit
         unit_first, scale_first = norm_parts(first[rows, :])
-        normed = unit_first * line_of(gain_first) + line_of(shift_first)
-        low = normed.astype(bf16)
+        low = (unit_first * line_of(gain_first) + line_of(shift_first)).astype(bf16)
         normed_low[rows, :] = low
         for at, size in cuts:
             cols = slice(at, at + size)
@@ -526,8 +568,19 @@
             value = inner * half
             act[rows, cols] = value.astype(bf16)
             slope = half + value * (1.0 - half) * (2 * GELU_C + (6 * GELU_C * GELU_A) * square)
-            for cut, wide in chunks(size, 256):
-                work[(at + cut) // 256, :, :wide] = slope[:, cut : cut + wide]
+            gin[rows, cols] = slope.astype(bf16)
+        store_step(8, step).start()
+        return carry
+
+    lax.fori_loop(0, 4, widen, 0)
+    store(10).start()
+    hook("down")
+
+    def feed(step, carry):
+        rows = rows_of(step)
+        valid = row_ids(step) < limit
+        unit_first, scale_first = norm_parts(first[rows, :])
+        normed = unit_first * line_of(gain_first) + line_of(shift_first)
         branch = dg(act[rows, :], matrix(w_down), 1, 1) + line_of(b_down)
         unit_second, scale_second = norm_parts(normed + branch)
         final = unit_second * line_of(gain_second) + line_of(shift_second)
@@ -541,12 +594,12 @@
         sums[2] += fold(low_branch.astype(f32))
         for at, size in cuts:
             cols = slice(at, at + size)
-            slope = [work[(at + cut) // 256, :, :wide] for cut, wide in chunks(size, 256)]
             low_inner = (
-                dg(low_branch, matrix(w_down, cols), 1, 0) * jnp.concatenate(slope, axis=1)
+                dg(low_branch, matrix(w_down, cols), 1, 0) * gin[rows, cols].astype(f32)
             ).astype(bf16)
             gin[rows, cols] = low_inner
             sums_up[:, cols] += fold(low_inner.astype(f32))
+        store_step(9, step).start()
         grad_normed = grad_second + dg(gin[rows, :], matrix(w_up), 1, 1)
         sums[3] += fold(grad_normed * unit_first)
         sums[4] += fold(grad_normed)
@@ -558,12 +611,21 @@
         return carry
 
     lax.fori_loop(0, 4, feed, 0)
+    output[ROWS:, :] = jnp.zeros((SLOTS - ROWS, width), bf16)
+    for i in (0, 7, 11, 12):
+        store(i).start()
     small[...] = jnp.zeros_like(small)
     for i in range(6):
         small[i : i + 1, :] = jnp.sum(sums[i], axis=0, keepdims=True)
     for i, (at, size) in enumerate(chunks(hidden, width)):
         small[6 + i : 7 + i, :size] = jnp.sum(sums_up[:, at : at + size], axis=0, keepdims=True)
-    output[ROWS:, :] = jnp.zeros((SLOTS - ROWS, width), bf16)
+    if fast:
+        whole_copies = [
+            store(14 + i, source, target)
+            for i, (source, target) in enumerate(zip((w_feat, w_qkv), wholes_out))
+        ]
+        for copy in whole_copies:
+            copy.start()
 
     for at, size in QBLOCKS:
         cols = slice(at, at + size)
@@ -575,26 +637,16 @@
         high, low = split_low(scaled.reshape(width, size))
         dmix_high[:, cols] = high
         dmix_low[:, cols] = low
-
-    def weight_copy(target, at, size, slot):
-        return pltpu.make_async_copy(
-            stage.at[slot, :, pl.ds(0, size)], target.at[:, pl.ds(at, size)], stage_sem.at[slot]
-        )
-
-    pending = {}
-    for turn, (left, over, right, target, (at, size)) in enumerate(
-        [(grad_branch, 0, act, grad_down, cut) for cut in cuts]
-        + [(normed_low, 0, gin, grad_up, cut) for cut in cuts]
-        + [(mixed_low, 1, grad_att, grad_out, (0, width))]
-    ):
-        slot = turn % 2
-        if slot in pending:
-            pending[slot].wait()
-        stage[slot, :, 0:size] = dg(left[...], right[:, at : at + size], over, 0).astype(bf16)
-        pending[slot] = weight_copy(target, at, size, slot)
-        pending[slot].start()
-    for copy in pending.values():
-        copy.wait()
+    for i in (5, 6):
+        store(i).start()
+    for step in range(4):
+        store_step(8, step).wait()
+        store_step(9, step).wait()
+    for i in (0, 1, 2, 3, 4, 5, 6, 7, 10, 11, 12, 13):
+        store(i).wait()
+    if fast:
+        for copy in whole_copies:
+            copy.wait()
 
 
 def shaped(shape, dtype):
@@ -605,60 +657,51 @@
     width = tokens.shape[1]
     hidden = weights[3].shape[1]
     heads = width // HEAD
-    outs = (
-        shaped((SLOTS, width), bf16),
-        shaped((ROWS, width), bf16),
-        shaped((ROWS, width), bf16),
-        shaped((ROWS, width), bf16),
-        shaped((ROWS, width), bf16),
-        shaped((width, ROWS), bf16),
-        shaped((width, ROWS), bf16),
+    token_rows = shaped((ROWS, width), bf16)
+    kept = (shaped((SLOTS, width), bf16),) + (token_rows,) * 4 + (shaped((width, ROWS), bf16),) * 2
+    kept += (shaped((ROWS, width), f32),) + (shaped((ROWS, hidden), bf16),) * 2
+    kept += (token_rows,) * 3 + (shaped((width, ROWS), bf16),)
+    wholes = [(4, 4, 2) + w.shape for w in weights]
+    outs = kept + (
+        shaped((heads, ROWS, 1280), bf16),
         shaped((heads, 1, ROWS), f32),
-        shaped((ROWS, width), f32),
-        shaped((heads, ROWS, 1280), bf16),
-        shaped((width, hidden), bf16),
-        shaped((width, hidden), bf16),
-        shaped((width, width), bf16),
         shaped((-(-(6 + -(-hidden // width)) // 8) * 8, width), f32),
     )
-    wholes = [(4, 4, 2) + w.shape for w in weights]
     if fast:
         outs += tuple(shaped(whole, bf16) for whole in wholes[:2])
     vmem = pl.BlockSpec(memory_space=pltpu.VMEM)
     hbm = pl.BlockSpec(memory_space=pl.ANY)
+    groups = len(gather_plan(width, hidden))
     return pl.pallas_call(
         functools.partial(forward_kernel, fast),
         out_shape=outs,
-        in_specs=[pl.BlockSpec(memory_space=pltpu.SMEM)] + [hbm] * 2 + [vmem] * 16,
-        out_specs=tuple(hbm if i in (9, 10, 11, 12) else vmem for i in range(len(outs))),
-        scratch_shapes=[
+        in_specs=[pl.BlockSpec(memory_space=pltpu.SMEM)] + [hbm] * 3 + [vmem] * 15,
+        out_specs=tuple(vmem if i in (15, 16) else hbm for i in range(len(outs))),
+        scratch_shapes=[pltpu.VMEM(k.shape, k.dtype) for k in kept]
+        + [
             pltpu.VMEM((ROWS, width), f32),
-            pltpu.VMEM((ROWS, hidden), bf16),
-            pltpu.VMEM((ROWS, hidden), bf16),
-            pltpu.VMEM((max(12, -(-hidden // 256)), STEP, 256), f32),
+            pltpu.VMEM((12, STEP, 256), f32),
             pltpu.VMEM((width, ROWS), f32),
-            pltpu.VMEM((width, ROWS), bf16),
             pltpu.VMEM((heads, 1, ROWS), f32),
-            pltpu.VMEM((ROWS, width), bf16),
-            pltpu.VMEM((ROWS, width), bf16),
-            pltpu.VMEM((ROWS, width), bf16),
             pltpu.VMEM((2, 256, ROWS), bf16),
             pltpu.VMEM((2, 128, ROWS), bf16),
             pltpu.VMEM((ROWS, 256), bf16),
-            pltpu.VMEM((2, width, 512), bf16),
+            pltpu.VMEM((ROWS, width), bf16),
             pltpu.VMEM((6, 8, width), f32),
             pltpu.VMEM((8, hidden), f32),
             pltpu.SemaphoreType.DMA((4,)),
-            pltpu.SemaphoreType.DMA((2,)),
-            pltpu.SemaphoreType.DMA((2,)),
+            pltpu.SemaphoreType.DMA((3,)),
+            pltpu.SemaphoreType.DMA((16,)),
+            pltpu.SemaphoreType.DMA((8,)),
         ]
         + fast
         * (
-            [pltpu.VMEM(whole, bf16) for whole in wholes[2:]]
+            [pltpu.VMEM(whole, bf16) for whole in wholes]
             + [
-                pltpu.SemaphoreType.DMA((7, MESSAGES)),
-                pltpu.SemaphoreType.DMA((7, MESSAGES)),
-                pltpu.SemaphoreType.DMA((7,)),
+                pltpu.VMEM(weights[1].shape, bf16),
+                pltpu.SemaphoreType.DMA((groups, MESSAGES)),
+                pltpu.SemaphoreType.DMA((groups, MESSAGES)),
+                pltpu.SemaphoreType.DMA((groups,)),
             ]
         ),
         compiler_params=pltpu.CompilerParams(
@@ -670,59 +713,82 @@
     )(cameras, tokens, features, cotangent, *weights, *biases)
 
 
+TAIL = 1280
+
+
 def reduce_plan(width, hidden):
-    half = hidden // 256 * 128
-    plan = [(which, cols, False) for which in (0, 1) for cols in ((0, half), (half, hidden - half))]
+    cuts = ((0, TAIL), (TAIL, TAIL), (2 * TAIL, hidden - 2 * TAIL))
+    plan = [(which, cols, False) for which in (0, 1) for cols in cuts]
     plan += [(2, (0, width), False)]
-    plan += [(3, (pair * 384, 384), False) for pair in range(width // 128)]
+    pairs = width // 128
+    plan += [(3, (pair * 384, 384), pair == pairs - 1) for pair in range(pairs)]
     return plan + [(4, (0, width), True)]
 
 
-HOOKS = {
-    (0, 0): ((1, 0), (1, 10)),
-    (0, 1): ((1, 1),),
-    (0, 2): ((2, 0), (2, 10)),
-    (1, 0): ((1, 2), (0, 5), (3, 10)),
-    (1, 1): ((2, 1), (1, 5)),
-    (1, 2): ((3, 0), (1, 3)),
-    (2, 0): ((2, 2), (0, 6), (2, 5)),
-    (2, 1): ((3, 1), (1, 4), (1, 6)),
-    (2, 2): ((2, 3), (4, 0), (3, 5)),
-    (3, 0): ((3, 2), (0, 7), (2, 6)),
-    (3, 1): ((2, 4), (1, 7), (4, 1), (4, 5)),
-    (3, 2): ((3, 3), (3, 6)),
-    "pairs": ((0, 8), (2, 7), (4, 2)),
-    "rows0": ((1, 8), (3, 4), (4, 3)),
-    "rows1": ((3, 7), (4, 6)),
-    "rows2": ((2, 8),),
-    "feat": ((0, 9), (4, 4), (0, 11)),
-    "half": ((3, 8), (1, 9), (1, 11), (4, 7)),
-    "end": ((4, 8), (2, 11), (3, 9), (3, 11), (4, 9)),
+REDUCE_HOOKS = {
+    "start": ((0, 12),),
+    "out": ((0, 6),),
+    "tails": ((0, 5), (0, 2), (1, 6)),
+    "up0": ((0, 3), (1, 5), (1, 12)),
+    "up1": ((0, 4), (1, 2)),
+    "down0": ((0, 0), (1, 3), (2, 6)),
+    "down1": ((0, 1), (1, 4), (2, 5)),
+    (0, 0): ((2, 2), (2, 12)),
+    (0, 1): ((1, 0),),
+    (0, 2): ((2, 3), (1, 1), (3, 12)),
+    (1, 0): ((2, 4), (0, 7), (3, 6)),
+    (1, 1): ((1, 7), (3, 5)),
+    (1, 2): ((2, 0), (3, 2)),
+    (2, 0): ((0, 8), (2, 1)),
+    (2, 1): ((1, 8), (2, 7), (3, 3)),
+    (2, 2): ((3, 4),),
+    (3, 0): ((0, 9), (2, 8)),
+    (3, 1): ((1, 9), (3, 0)),
+    (3, 2): ((3, 1),),
+    "pairs": ((0, 10), (2, 9), (3, 7)),
+    "rows0": ((1, 10),),
+    "rows1": ((3, 8),),
+    "rows2": ((4, 6), (4, 5), (4, 2), (3, 9)),
+    "feat": ((0, 11), (0, 13), (4, 3)),
+    "half": ((1, 11), (1, 13), (3, 10), (4, 4)),
+    "end": ((4, 0), (4, 1), (4, 7), (4, 8), (2, 13), (4, 9), (3, 11), (4, 10), (3, 13), (4, 11))
+    + tuple((5, i) for i in range(14)),
 }
+
+
+def put(target, cols, value):
+    if len(target.shape) == 2:
+        target[:, cols] = value
+    else:
+        target[:, :, :, :, cols] = value.reshape(target.shape[:4] + value.shape[1:])
 
 
 def backward_kernel(fast, *refs):
     refs = list(refs)
     take = lambda count: [refs.pop(0) for _ in range(count)]
-    cameras, features, q_rows, k_rows, v_rows, dmix_high, dmix_low, dots = take(8)
-    start_low, grad_first, probs, w_qkv, w_feat = take(5)
+    cameras, features, probs, dots, act, gin, *wgrad_in = take(10)
+    inputs = take(9)
+    small = take(1)[0] if fast else None
+    grad_tokens, grad_features = take(2)
     if fast:
-        grad_down, grad_up, grad_out, small = take(4)
-        grad_tokens, grad_features, *summed = take(7)
-        total, total_late = take(2)
+        summed, (total, total_late) = take(5), take(2)
+        parts_of = take(5)
+        small_late = take(1)[0]
     else:
-        grad_tokens, grad_features, grad_qkv, grad_feat, small_late = take(5)
-    feats, weights, grad_scores, joined, d_cat, d_rows, v_cat = take(7)
-    k_turned, grad_memory, pair_rows, sums, prob_sem, load_sem = take(6)
+        parts_of = take(5)
+        small_late = take(1)[0]
+    loaded = take(9)
+    q_rows, k_rows, v_rows, dmix_high, dmix_low, start_low, grad_first, w_qkv, w_feat = loaded
+    weights, grad_scores, joined, d_cat, d_rows, v_cat, k_turned, blank, sums = take(9)
+    prob_sem, load_sem, wgrad_sem, out_sem = take(4)
     width = q_rows.shape[1]
+    hidden = act.shape[1]
     heads = width // HEAD
     pairs = heads // 2
     limit = 2 + CAM_LEN * cameras[0]
     if fast:
-        small_late, part_qkv, part_feat = take(3)
         send, recv, local = refs[-3:]
-        plan = reduce_plan(width, grad_up.shape[-1])
-        parts_of = (grad_down, grad_up, grad_out, part_qkv, part_feat)
+        plan = reduce_plan(width, hidden)
 
         def writer(which, cols):
             def write(value):
@@ -736,23 +802,16 @@
 
             return write
 
-        groups = []
-        for i, (which, cols, direct) in enumerate(plan):
-            bufs = take(4)
-            mine = take(1)[0] if which < 3 else None
-            groups.append(
-                Reduce(
-                    parts_of[which], cols, writer(which, cols), bufs, mine, direct, send, recv, local, i
-                )
-            )
+        groups = [
+            Reduce(parts_of[which], cols, writer(which, cols), take(4), direct, send, recv, i)
+            for i, (which, cols, direct) in enumerate(plan)
+        ]
         groups.append(Total(small, total, take(3), send, recv, len(plan)))
         groups.append(Total(small_late, total_late, take(3), send, recv, len(plan) + 1))
-        greet()
-        turns(groups, *[(0, i) for i in range(5)], (0, 10))
 
     def hook(where):
         if fast:
-            turns(groups, *HOOKS[where])
+            turns(groups, *REDUCE_HOOKS[where])
 
     def pair_hook(pair, spot):
         if fast:
@@ -762,16 +821,77 @@
                 def _():
                     hook((at_pair, spot))
 
+    mixed_low, normed_low = d_cat, joined.at[:, pl.ds(0, width)]
+    grad_branch, grad_att = joined.at[:, pl.ds(width, width)], joined.at[:, pl.ds(2 * width, width)]
+    tail = pl.ds(2 * TAIL, hidden - 2 * TAIL)
+    act_tail = weights.at[2, :, pl.ds(0, hidden - 2 * TAIL)]
+    gin_tail = weights.at[2, :, pl.ds(hidden - 2 * TAIL, hidden - 2 * TAIL)]
+    ends = [
+        (wgrad_in[3], mixed_low),
+        (wgrad_in[2], grad_att),
+        (wgrad_in[0], normed_low),
+        (gin.at[:, tail], gin_tail),
+        (wgrad_in[1], grad_branch),
+        (act.at[:, tail], act_tail),
+        (gin.at[:, pl.ds(0, TAIL)], weights.at[3]),
+        (gin.at[:, pl.ds(TAIL, TAIL)], grad_scores.at[0]),
+        (act.at[:, pl.ds(0, TAIL)], weights.at[0]),
+        (act.at[:, pl.ds(TAIL, TAIL)], weights.at[1]),
+    ]
+    fetch = [
+        pltpu.make_async_copy(source, target, wgrad_sem.at[i])
+        for i, (source, target) in enumerate(ends)
+    ]
+    loads = [
+        pltpu.make_async_copy(source, target, load_sem.at[i])
+        for i, (source, target) in enumerate(zip(inputs, loaded))
+    ]
+    for copy in fetch + loads:
+        copy.start()
+    if fast:
+        greet()
+    hook("start")
+
     def prob_copy(pair, side):
-        slot = 2 * lax.rem(pair, 2) + side
+        slot = 2 * lax.rem(pair + 1, 2) + side
         return pltpu.make_async_copy(
             probs.at[2 * pair + side], weights.at[slot], prob_sem.at[slot]
         )
 
+    def weight_grad(which, left, right, at, size):
+        for cut, wide in chunks(size, 512):
+            grad = dg(left[...], right[:, cut : cut + wide], 0, 0).astype(bf16)
+            put(parts_of[which], pl.ds(at + cut, wide), grad)
+
+    fetch[0].wait()
+    fetch[1].wait()
+    grad = dg(mixed_low[...].reshape(width, ROWS), grad_att[...], 1, 0).astype(bf16)
+    put(parts_of[2], pl.ds(0, width), grad)
+    hook("out")
+    fetch[2].wait()
+    fetch[3].wait()
+    weight_grad(1, normed_low, gin_tail, 2 * TAIL, hidden - 2 * TAIL)
+    fetch[4].wait()
+    fetch[5].wait()
+    weight_grad(0, grad_branch, act_tail, 2 * TAIL, hidden - 2 * TAIL)
+    hook("tails")
+    fetch[6].wait()
+    weight_grad(1, normed_low, weights.at[3], 0, TAIL)
+    hook("up0")
     for side in range(2):
         prob_copy(0, side).start()
-    load = pltpu.make_async_copy(features.at[pl.ds(0, ROWS), :], feats, load_sem)
-    load.start()
+    fetch[7].wait()
+    weight_grad(1, normed_low, grad_scores.at[0], TAIL, TAIL)
+    hook("up1")
+    fetch[8].wait()
+    weight_grad(0, grad_branch, weights.at[0], 0, TAIL)
+    hook("down0")
+    fetch[9].wait()
+    weight_grad(0, grad_branch, weights.at[1], TAIL, TAIL)
+    hook("down1")
+    for load in loads:
+        load.wait()
+
     sums[...] = jnp.zeros_like(sums)
     lane_valid = lax.broadcasted_iota(jnp.int32, (1, ROWS), 1) < limit
     row_valid = lax.broadcasted_iota(jnp.int32, (ROWS, 1), 0) < limit
@@ -801,7 +921,7 @@
         v_cat[:, :128] = values
         v_cat[:, 128:] = values
         k_turned[...] = jnp.where(lane_valid, k_rows[:, lanes].astype(f32).T, 0.0).astype(bf16)
-        base = 2 * lax.rem(pair, 2)
+        base = 2 * lax.rem(pair + 1, 2)
         jobs = [(side, at, size) for side in range(2) for at, size in QBLOCKS]
         parts = chunks(ROWS, STEP)
         turned = {0: [], 1: []}
@@ -846,33 +966,44 @@
         queries(len(jobs) - 1)
         pair_hook(pair, 2)
         first_lane = lax.broadcasted_iota(jnp.int32, (STEP, 128), 1) < HEAD
+        spot = lambda i: pl.ds(pl.multiple_of(pair * 384 + i * 128, 128), 128)
         for part in parts:
             spread(1, part)
             here = slice(part[0], part[0] + part[1])
             keep = row_valid[here]
-            for which, at in ((0, 2), (1, 1)):
+            for which, i in ((0, 2), (1, 1)):
                 value = jnp.where(first_lane, wide[0, part][which], wide[1, part][which])
-                value = jnp.where(keep, value, 0.0).astype(bf16)
-                joined[here, pl.ds(pl.multiple_of(at * width + pair * 128, 128), 128)] = value
-                pair_rows[here, at * 128 : at * 128 + 128] = value
+                joined[here, spot(i)] = jnp.where(keep, value, 0.0).astype(bf16)
         query = jnp.concatenate(
             [jnp.concatenate(turned[0], axis=1), jnp.concatenate(turned[1], axis=1)], axis=0
         )
-        query = (query.astype(bf16).astype(f32).T * 0.125).astype(bf16)
-        joined[:, lanes] = query
-        pair_rows[:, :128] = query
-        grad = dg(start_low[...], pair_rows[...], 0, 0).astype(bf16)
-        if fast:
-            at = pl.ds(pl.multiple_of(pair * 384, 128), 384)
-            part_qkv[:, :, :, :, at] = grad.reshape(part_qkv.shape[:4] + (384,))
-        else:
-            for i in range(3):
-                at = pl.ds(pl.multiple_of(i * width + pair * 128, 128), 128)
-                grad_qkv[:, at] = grad[:, i * 128 : i * 128 + 128]
+        joined[:, spot(0)] = (query.astype(bf16).astype(f32).T * 0.125).astype(bf16)
+        at = pl.ds(pl.multiple_of(pair * 384, 128), 384)
+        put(parts_of[3], at, dg(start_low[...], joined[:, at], 0, 0).astype(bf16))
         return carry
 
     lax.fori_loop(0, pairs, attend_back, 0)
-    load.wait()
+    feats = weights.at[2, :, pl.ds(0, width)]
+    tokens_out = weights.at[2, :, pl.ds(width, width)]
+    features_out = weights.at[3, :, pl.ds(0, width)]
+    grad_memory = grad_scores.at[0, :, pl.ds(0, width)]
+    load = pltpu.make_async_copy(features.at[pl.ds(0, ROWS), :], feats, out_sem.at[0])
+    load.start()
+    blank[...] = jnp.zeros_like(blank)
+    body, rest = pl.ds(0, ROWS), pl.ds(ROWS, SLOTS - ROWS)
+    stores = [
+        pltpu.make_async_copy(source, target, out_sem.at[1 + i])
+        for i, (source, target) in enumerate(
+            (
+                (blank, grad_tokens.at[rest, :]),
+                (blank, grad_features.at[rest, :]),
+                (tokens_out, grad_tokens.at[body, :]),
+                (features_out, grad_features.at[body, :]),
+            )
+        )
+    ]
+    stores[0].start()
+    stores[1].start()
     hook("pairs")
 
     for step in range(4):
@@ -880,43 +1011,74 @@
         ids = step * STEP + lax.broadcasted_iota(jnp.int32, (STEP, 1), 0)
         camera = jnp.logical_and(ids >= 2, ids < limit)
         part = joined[rows, :]
-        sums[0] += fold(part[:, :width].astype(f32))
-        sums[1] += fold(part[:, 2 * width :].astype(f32))
+        for pair in range(pairs):
+            lanes = slice(pair * 128, pair * 128 + 128)
+            sums[0, :, lanes] += fold(part[:, pair * 384 : pair * 384 + 128].astype(f32))
+            sums[1, :, lanes] += fold(part[:, pair * 384 + 256 : pair * 384 + 384].astype(f32))
         grad_start = grad_first[rows, :] + dg(part, w_qkv[...], 1, 1)
-        grad_tokens[rows, :] = grad_start.astype(bf16)
+        tokens_out[rows, :] = grad_start.astype(bf16)
         low = jnp.where(camera, grad_start, 0.0).astype(bf16)
         grad_memory[rows, :] = low
         sums[2] += fold(low.astype(f32))
         if step < 3:
             hook(f"rows{step}")
-    grad = dg(feats[...], grad_memory[...], 0, 0).astype(bf16)
+    stores[2].start()
+    load.wait()
+    put(parts_of[4], pl.ds(0, width), dg(feats[...], grad_memory[...], 0, 0).astype(bf16))
     small_late[...] = jnp.zeros_like(small_late)
     for i in range(3):
         small_late[i : i + 1, :] = jnp.sum(sums[i], axis=0, keepdims=True)
-    if fast:
-        part_feat[...] = grad.reshape(part_feat.shape)
-    else:
-        grad_feat[...] = grad
     hook("feat")
     for step in range(4):
         rows = slice(step * STEP, step * STEP + STEP)
-        grad_features[rows, :] = dg(grad_memory[rows, :], w_feat[...], 1, 1).astype(bf16)
+        features_out[rows, :] = dg(grad_memory[rows, :], w_feat[...], 1, 1).astype(bf16)
         if step == 1:
             hook("half")
-    grad_tokens[ROWS:, :] = jnp.zeros((SLOTS - ROWS, width), bf16)
-    grad_features[ROWS:, :] = jnp.zeros((SLOTS - ROWS, width), bf16)
+    stores[3].start()
     hook("end")
-    if fast:
-        turns(groups, *[(5, i) for i in range(len(groups))])
-
-
-def backward_call(fast, cameras, features, saved, w_qkv, w_feat, grads, small):
-    width = features.shape[1]
-    heads = width // HEAD
+    for copy in stores:
+        copy.wait()
+
+
+def backward_call(fast, cameras, features, saved, small):
+    probs, dots, act, gin, normed_low, grad_branch, grad_att, mixed_low, *inputs = saved
+    width, hidden = features.shape[1], act.shape[1]
     vmem = pl.BlockSpec(memory_space=pltpu.VMEM)
     hbm = pl.BlockSpec(memory_space=pl.ANY)
-    scratch = [
-        pltpu.VMEM((ROWS, width), bf16),
+    rows = width // 32
+    columns = (hidden, hidden, width, 3 * width, width)
+    late = (8, width)
+    outs = (shaped((SLOTS, width), bf16),) * 2
+    scratch = []
+    reduce_scratch = []
+    args = [cameras, features, probs, dots, act, gin, normed_low, grad_branch, grad_att]
+    args += [mixed_low.reshape(2, width // 2, ROWS), *inputs]
+    specs = [pl.BlockSpec(memory_space=pltpu.SMEM), hbm, hbm, vmem] + [hbm] * 15
+    if fast:
+        outs += tuple(shaped((rows, n), f32) for n in columns)
+        outs += (shaped(small.shape, f32), shaped(late, f32))
+        args += [small]
+        specs += [vmem]
+        scratch += [pltpu.VMEM((4, 4, 2, rows, n), bf16) for n in columns] + [pltpu.VMEM(late, f32)]
+        plan = reduce_plan(width, hidden)
+        for which, (_, size), direct in plan:
+            reduce_scratch += [
+                pltpu.VMEM((4, 4, rows, size), bf16),
+                pltpu.VMEM((4, rows, size) if direct else (2, 2, rows, size), bf16),
+                pltpu.VMEM((2, 4, rows, size), bf16),
+                pltpu.VMEM((3, rows, size), bf16),
+            ]
+        for shape in (small.shape, late):
+            reduce_scratch += [pltpu.VMEM((count,) + shape, f32) for count in (4, 4, 2)]
+        reduce_scratch += [
+            pltpu.SemaphoreType.DMA((len(plan) + 2, MESSAGES)),
+            pltpu.SemaphoreType.DMA((len(plan) + 2, MESSAGES)),
+            pltpu.SemaphoreType.DMA((len(plan),)),
+        ]
+    else:
+        outs += tuple(shaped((width, n), bf16) for n in columns) + (shaped(late, f32),)
+    scratch += [pltpu.VMEM(a.shape, a.dtype) for a in inputs]
+    scratch += [
         pltpu.VMEM((4, ROWS, 1280), bf16),
         pltpu.VMEM((2, ROWS, 1280), bf16),
         pltpu.VMEM((ROWS, 3 * width), bf16),
@@ -924,64 +1086,26 @@
         pltpu.VMEM((ROWS, 256), bf16),
         pltpu.VMEM((ROWS, 256), bf16),
         pltpu.VMEM((128, ROWS), bf16),
-        pltpu.VMEM((ROWS, width), bf16),
-        pltpu.VMEM((ROWS, 384), bf16),
+        pltpu.VMEM((SLOTS - ROWS, width), bf16),
         pltpu.VMEM((3, 8, width), f32),
         pltpu.SemaphoreType.DMA((4,)),
-        pltpu.SemaphoreType.DMA(()),
+        pltpu.SemaphoreType.DMA((9,)),
+        pltpu.SemaphoreType.DMA((10,)),
+        pltpu.SemaphoreType.DMA((5,)),
     ]
-    outs = (shaped((SLOTS, width), bf16),) * 2
-    inputs = [cameras, features, *saved, w_qkv, w_feat]
-    specs = [pl.BlockSpec(memory_space=pltpu.SMEM), hbm] + [vmem] * 8 + [hbm] + [vmem] * 2
-    if fast:
-        hidden = grads[0].shape[1]
-        rows = width // 32
-        late = (8, width)
-        outs += tuple(shaped((rows, n), f32) for n in (hidden, hidden, width, 3 * width, width))
-        outs += (shaped(small.shape, f32), shaped(late, f32))
-        inputs += [grad.reshape(4, 4, 2, rows, -1) for grad in grads] + [small]
-        specs += [hbm] * 3 + [vmem]
-        scratch += [
-            pltpu.VMEM(late, f32),
-            pltpu.VMEM((4, 4, 2, rows, 3 * width), bf16),
-            pltpu.VMEM((4, 4, 2, rows, width), bf16),
-        ]
-        plan = reduce_plan(width, hidden)
-        for which, (_, size), direct in plan:
-            scratch += [
-                pltpu.VMEM((4, 4, rows, size), bf16),
-                pltpu.VMEM((4, rows, size) if direct else (2, 2, rows, size), bf16),
-                pltpu.VMEM((2, 4, rows, size), bf16),
-                pltpu.VMEM((3, rows, size), bf16),
-            ]
-            if which < 3:
-                scratch += [pltpu.VMEM((4, 4, rows, size), bf16)]
-        for shape in (small.shape, late):
-            scratch += [pltpu.VMEM((count,) + shape, f32) for count in (4, 4, 2)]
-        scratch += [
-            pltpu.SemaphoreType.DMA((len(plan) + 2, MESSAGES)),
-            pltpu.SemaphoreType.DMA((len(plan) + 2, MESSAGES)),
-            pltpu.SemaphoreType.DMA((len(plan),)),
-        ]
-    else:
-        outs += (
-            shaped((width, 3 * width), bf16),
-            shaped((width, width), bf16),
-            shaped((8, width), f32),
-        )
     return pl.pallas_call(
         functools.partial(backward_kernel, fast),
         out_shape=outs,
         in_specs=specs,
-        out_specs=(vmem,) * len(outs),
-        scratch_shapes=scratch,
+        out_specs=(hbm,) * 2 + (vmem,) * (len(outs) - 2),
+        scratch_shapes=scratch + reduce_scratch,
         compiler_params=pltpu.CompilerParams(
             vmem_limit_bytes=62 * MIB,
             collective_id=1 if fast else None,
             has_side_effects=fast,
         ),
         name="layer_backward",
-    )(*inputs)
+    )(*args)
 
 
 def finish_kernel(*refs):
@@ -1040,30 +1164,34 @@
 ):
     width = tokens.shape[1]
     hidden = w_up.shape[1]
+    pairs = width // 128
     weights = (w_feat, w_qkv, w_out, w_up, w_down)
     if not fast:
-        weights = tuple(lax.all_gather(w, AXES, axis=0, tiled=True) for w in weights)
-    output, start_low, *rest = forward_call(fast, cameras, tokens, features, cotangent, weights, biases)
-    q_rows, k_rows, v_rows, dmix_high, dmix_low, dots, grad_first, probs, *rest = rest
-    grad_down, grad_up, grad_out, small, *wholes = rest
+        weights = [lax.all_gather(w, AXES, axis=0, tiled=True) for w in weights]
+        by_pair = weights[1].reshape(width, 3, pairs, 128).transpose(0, 2, 1, 3)
+        weights[1] = by_pair.reshape(width, 3 * width)
+    output, *kept = forward_call(fast, cameras, tokens, features, cotangent, weights, biases)
+    start_low, q_rows, k_rows, v_rows, dmix_high, dmix_low, grad_first, *kept = kept
+    act, gin, normed_low, grad_branch, grad_att, mixed_low, probs, dots, small, *wholes = kept
     if fast:
         weights = [whole.reshape(width, -1) for whole in wholes]
-    saved = (q_rows, k_rows, v_rows, dmix_high, dmix_low, dots, start_low, grad_first, probs)
-    grads = (grad_down, grad_up, grad_out)
-    grad_tokens, grad_features, *rest = backward_call(
-        fast, cameras, features, saved, weights[1], weights[0], grads, small
-    )
+    saved = (probs, dots, act, gin, normed_low, grad_branch, grad_att, mixed_low)
+    saved += (q_rows, k_rows, v_rows, dmix_high, dmix_low, start_low, grad_first)
+    saved += (weights[1], weights[0])
+    grad_tokens, grad_features, *grads = backward_call(fast, cameras, features, saved, small)
     if fast:
-        *grads, small, late = rest
+        *grads, small, late = grads
     else:
-        grads += tuple(rest[:2])
+        *grads, late = grads
+        by_pair = grads[3].reshape(width, pairs, 3, 128).transpose(0, 2, 1, 3)
+        grads[3] = by_pair.reshape(width, 3 * width)
         grads = [
             lax.psum_scatter(
                 lax.optimization_barrier(grad.astype(f32)), AXES, scatter_dimension=0, tiled=True
             )
             for grad in grads
         ]
-        small, late = lax.psum((small, rest[2]), AXES)
+        small, late = lax.psum((small, late), AXES)
     grad_down, grad_up, grad_out, grad_qkv, grad_feat = grads
     large = (output, grad_tokens, grad_features, grad_qkv, grad_out, grad_up, grad_down, grad_feat)
     return finish_call(large, small, late, hidden)

time: 186 us -> 184 us (0.989); the launches traced: 186 us -> 182 us
  Pallas kernels: 184 us -> 180 us
    pallas_call x1, Pallas kernels: 107 us -> 103 us  [forward_call(): pl.pallas_call(functools.partial(forward_kernel, fast), out_shape=outs, i...]
where the time goes in v4:
time: 184 us; the launch traced here: 182 us
  Pallas kernels  180 us (98%)
    pallas_call x1, Pallas kernels, forward_call(): pl.pallas_call(functools.partial(forward_kernel, fast), out_shape=outs, i...  103 us
    pallas_call x1, Pallas kernels, backward_call(): pl.pallas_call(functools.partial(backward_kernel, fast), out_shape=outs,...  72.4 us
    pallas_call x1, Pallas kernels, finish_call(): pl.pallas_call(finish_kernel, out_shape=tuple((shaped(a.shape, a.dtype) f...  5.02 us

profile of v4, /device:TPU:0, one launch (start us, length us, event | category | flops | bytes accessed | tf_op | source)
XLA Modules:
  0.0 181.9 jit_solution(8598038653490360138)
XLA Ops:
  1.3 102.7 %layer_forward.1 = (bf16[1280,512]{1,0:T(8,128)(2,1)}, bf16[1216,512]{1,0:T(8,128)(2,1)}, bf16[1216,512]{1,0:T(8,128)(2,1)}, bf16[1216,512]{1,0:T(8,128)(2,1)}, ...) custom-call(s32[1]{0:T(128)S(6)} %copy.37.refs_0_, ...), custom_call_target="tpu_custom_call" | custom-call | tf_op jit(solution)/shard_map/layer_forward/pallas_call | solution.py:675
  104.0 72.4 %layer_backward.1 = (bf16[1280,512]{1,0:T(8,128)(2,1)}, bf16[1280,512]{1,0:T(8,128)(2,1)}, f32[16,3200]{1,0:T(8,128)}, f32[16,3200]{1,0:T(8,128)}, f32[16,512]{1...) custom-call(s32[1]{0:T(128)S(6)} %copy.37.refs_0_, ...), custom_call_target="tpu_custom_call" | custom-call | tf_op jit(solution)/shard_map/layer_backward/pallas_call | solution.py:1096
  176.4 5.0 %place_outputs.1 = (bf16[1280,512]{1,0:T(8,128)(2,1)}, bf16[1280,512]{1,0:T(8,128)(2,1)}, bf16[1280,512]{1,0:T(8,128)(2,1)}, f32[16,1536]{1,0:T(8,128)}, f32[16,...) custom-call(bf16[1280,512]{1,0:T(8,128)(2,1)} %get-tuple-element.46., ...), custom_call_target="tpu_custom_call" | custom-call | tf_op jit(solution)/shard_map/place_outputs/pallas_call | solution.py:1138

commit v5 on v4

--- a/solution.py
+++ b/solution.py
@@ -748,11 +748,11 @@
     "pairs": ((0, 10), (2, 9), (3, 7)),
     "rows0": ((1, 10),),
     "rows1": ((3, 8),),
-    "rows2": ((4, 6), (4, 5), (4, 2), (3, 9)),
-    "feat": ((0, 11), (0, 13), (4, 3)),
-    "half": ((1, 11), (1, 13), (3, 10), (4, 4)),
-    "end": ((4, 0), (4, 1), (4, 7), (4, 8), (2, 13), (4, 9), (3, 11), (4, 10), (3, 13), (4, 11))
-    + tuple((5, i) for i in range(14)),
+    "rows2": ((4, 6), (4, 5), (4, 2), (3, 9), (5, 6), (5, 5), (5, 2), (5, 12)),
+    "feat": ((0, 11), (0, 13), (4, 3), (5, 3)),
+    "half": ((1, 11), (1, 13), (3, 10), (4, 4), (4, 0), (4, 1), (5, 4), (5, 0), (5, 1)),
+    "end": ((2, 13), (4, 7), (4, 8), (4, 9), (5, 7), (5, 8), (5, 9), (3, 11), (4, 10), (5, 10))
+    + ((3, 13), (5, 13), (4, 11), (5, 11)),
 }
 
 
@@ -859,7 +859,15 @@
         )
 
     def weight_grad(which, left, right, at, size):
-        for cut, wide in chunks(size, 512):
+        def part(turn, carry):
+            cut = pl.multiple_of(turn * 512, 512)
+            grad = dg(left[...], right[:, pl.ds(cut, 512)], 0, 0).astype(bf16)
+            put(parts_of[which], pl.ds(at + cut, 512), grad)
+            return carry
+
+        lax.fori_loop(0, size // 512, part, 0)
+        if size % 512:
+            cut, wide = size // 512 * 512, size % 512
             grad = dg(left[...], right[:, cut : cut + wide], 0, 0).astype(bf16)
             put(parts_of[which], pl.ds(at + cut, wide), grad)
 
@@ -1006,8 +1014,8 @@
     stores[1].start()
     hook("pairs")
 
-    for step in range(4):
-        rows = slice(step * STEP, step * STEP + STEP)
+    def project_back(step, carry):
+        rows = pl.ds(pl.multiple_of(step * STEP, 16), STEP)
         ids = step * STEP + lax.broadcasted_iota(jnp.int32, (STEP, 1), 0)
         camera = jnp.logical_and(ids >= 2, ids < limit)
         part = joined[rows, :]
@@ -1020,8 +1028,16 @@
         low = jnp.where(camera, grad_start, 0.0).astype(bf16)
         grad_memory[rows, :] = low
         sums[2] += fold(low.astype(f32))
-        if step < 3:
-            hook(f"rows{step}")
+        if fast:
+            for at_step in (0, 1, 2):
+
+                @pl.when(step == at_step)
+                def _():
+                    hook(f"rows{at_step}")
+
+        return carry
+
+    lax.fori_loop(0, 4, project_back, 0)
     stores[2].start()
     load.wait()
     put(parts_of[4], pl.ds(0, width), dg(feats[...], grad_memory[...], 0, 0).astype(bf16))
@@ -1029,11 +1045,14 @@
     for i in range(3):
         small_late[i : i + 1, :] = jnp.sum(sums[i], axis=0, keepdims=True)
     hook("feat")
-    for step in range(4):
-        rows = slice(step * STEP, step * STEP + STEP)
+    hook("half")
+
+    def spread_back(step, carry):
+        rows = pl.ds(pl.multiple_of(step * STEP, 16), STEP)
         features_out[rows, :] = dg(grad_memory[rows, :], w_feat[...], 1, 1).astype(bf16)
-        if step == 1:
-            hook("half")
+        return carry
+
+    lax.fori_loop(0, 4, spread_back, 0)
     stores[3].start()
     hook("end")
     for copy in stores:

time: 184 us -> 172 us (0.935)
  Pallas kernels: 180 us -> 170 us
    pallas_call x1, Pallas kernels: 103 us -> 92.5 us  [forward_call(): pl.pallas_call(functools.partial(forward_kernel, fast), out_shape=outs, i...]
where the time goes in v5:
time: 172 us; the launch traced here: 171 us
  Pallas kernels  170 us (99%)
    pallas_call x1, Pallas kernels, forward_call(): pl.pallas_call(functools.partial(forward_kernel, fast), out_shape=outs, i...  92.5 us
    pallas_call x1, Pallas kernels, backward_call(): pl.pallas_call(functools.partial(backward_kernel, fast), out_shape=outs,...  72.2 us
    pallas_call x1, Pallas kernels, finish_call(): pl.pallas_call(finish_kernel, out_shape=tuple((shaped(a.shape, a.dtype) f...  5.02 us

profile of v5, /device:TPU:0, one launch (start us, length us, event | category | flops | bytes accessed | tf_op | source)
XLA Modules:
  0.0 171.3 jit_solution(142643837784571604)
XLA Ops:
  1.3 92.5 %layer_forward.1 = (bf16[1280,512]{1,0:T(8,128)(2,1)}, bf16[1216,512]{1,0:T(8,128)(2,1)}, bf16[1216,512]{1,0:T(8,128)(2,1)}, bf16[1216,512]{1,0:T(8,128)(2,1)}, ...) custom-call(s32[1]{0:T(128)S(6)} %copy.37.refs_0_, ...), custom_call_target="tpu_custom_call" | custom-call | tf_op jit(solution)/shard_map/layer_forward/pallas_call | solution.py:675
  93.8 72.2 %layer_backward.1 = (bf16[1280,512]{1,0:T(8,128)(2,1)}, bf16[1280,512]{1,0:T(8,128)(2,1)}, f32[16,3200]{1,0:T(8,128)}, f32[16,3200]{1,0:T(8,128)}, f32[16,512]{1...) custom-call(s32[1]{0:T(128)S(6)} %copy.37.refs_0_, ...), custom_call_target="tpu_custom_call" | custom-call | tf_op jit(solution)/shard_map/layer_backward/pallas_call | solution.py:1115
  166.1 5.0 %place_outputs.1 = (bf16[1280,512]{1,0:T(8,128)(2,1)}, bf16[1280,512]{1,0:T(8,128)(2,1)}, bf16[1280,512]{1,0:T(8,128)(2,1)}, f32[16,1536]{1,0:T(8,128)}, f32[16,...) custom-call(bf16[1280,512]{1,0:T(8,128)(2,1)} %get-tuple-element.46., ...), custom_call_target="tpu_custom_call" | custom-call | tf_op jit(solution)/shard_map/place_outputs/pallas_call | solution.py:1157

commit v6 on v5

--- a/solution.py
+++ b/solution.py
@@ -323,24 +323,23 @@
 
 
 GATHER_HOOKS = {
-    "start": ((0, 0), (0, 1)) + tuple((0, i) for i in range(2, 10)),
-    "first": ((1, 0), (1, 1), (1, 2), (2, 0), (2, 1), (1, 3), (3, 0), (3, 1), (4, 0)),
-    0: ((1, 4), (2, 2), (1, 5), (4, 1)),
-    1: ((3, 2), (2, 3), (1, 6), (4, 2)),
-    2: ((3, 3), (2, 4), (2, 5), (1, 7), (4, 3)),
-    3: ((3, 4), (3, 5), (2, 6), (1, 8), (4, 4)),
-    "out": ((2, 7), (3, 6), (1, 9), (4, 5)),
-    "up": ((3, 7), (4, 6), (4, 7)),
-    "up1": ((2, 8),),
-    "up2": ((3, 8), (2, 9)),
-    "down": ((3, 9), (4, 8), (4, 9)) + tuple((5, i) for i in range(10)),
+    "start": tuple((0, i) for i in range(8)),
+    "first": ((1, 0), (1, 1), (1, 2), (2, 0), (2, 1), (3, 0), (3, 1), (4, 0)),
+    0: ((2, 2), (1, 3), (1, 4), (4, 1)),
+    1: ((3, 2), (1, 5), (2, 3), (4, 2)),
+    2: ((2, 4), (3, 3), (1, 6)),
+    3: ((2, 5), (3, 4), (1, 7)),
+    "out": ((2, 6), (3, 5), (4, 3)),
+    "up": ((4, 4), (4, 5)),
+    "up1": ((2, 7), (3, 6)),
+    "up2": (),
+    "down": ((3, 7), (4, 6), (4, 7)) + tuple((5, i) for i in range(8)),
 }
 
 
 def gather_plan(width, hidden):
     half = hidden // 256 * 128
-    plan = [(0, (0, width))] + [(1, (pair * 384, 384)) for pair in range(width // 128)]
-    plan += [(2, (0, width))]
+    plan = [(0, (0, width)), (1, (0, 384)), (1, (384, 3 * width - 384)), (2, (0, width))]
     return plan + [(which, cols) for which in (3, 4) for cols in ((0, half), (half, hidden - half))]
 
 
@@ -720,39 +719,39 @@
     cuts = ((0, TAIL), (TAIL, TAIL), (2 * TAIL, hidden - 2 * TAIL))
     plan = [(which, cols, False) for which in (0, 1) for cols in cuts]
     plan += [(2, (0, width), False)]
-    pairs = width // 128
-    plan += [(3, (pair * 384, 384), pair == pairs - 1) for pair in range(pairs)]
+    last = 3 * width - 384
+    plan += [(3, (0, last - 384), False), (3, (last - 384, 384), False), (3, (last, 384), True)]
     return plan + [(4, (0, width), True)]
 
 
 REDUCE_HOOKS = {
-    "start": ((0, 12),),
+    "start": ((0, 11),),
     "out": ((0, 6),),
     "tails": ((0, 5), (0, 2), (1, 6)),
-    "up0": ((0, 3), (1, 5), (1, 12)),
+    "up0": ((0, 3), (1, 5), (1, 11)),
     "up1": ((0, 4), (1, 2)),
     "down0": ((0, 0), (1, 3), (2, 6)),
     "down1": ((0, 1), (1, 4), (2, 5)),
-    (0, 0): ((2, 2), (2, 12)),
+    (0, 0): ((2, 2), (2, 11)),
     (0, 1): ((1, 0),),
-    (0, 2): ((2, 3), (1, 1), (3, 12)),
-    (1, 0): ((2, 4), (0, 7), (3, 6)),
-    (1, 1): ((1, 7), (3, 5)),
+    (0, 2): ((2, 3), (1, 1), (3, 11)),
+    (1, 0): ((2, 4), (3, 6)),
+    (1, 1): ((3, 5),),
     (1, 2): ((2, 0), (3, 2)),
-    (2, 0): ((0, 8), (2, 1)),
-    (2, 1): ((1, 8), (2, 7), (3, 3)),
+    (2, 0): ((0, 7), (2, 1)),
+    (2, 1): ((1, 7), (3, 3)),
     (2, 2): ((3, 4),),
-    (3, 0): ((0, 9), (2, 8)),
-    (3, 1): ((1, 9), (3, 0)),
+    (3, 0): ((0, 8), (2, 7)),
+    (3, 1): ((1, 8), (3, 0)),
     (3, 2): ((3, 1),),
-    "pairs": ((0, 10), (2, 9), (3, 7)),
-    "rows0": ((1, 10),),
-    "rows1": ((3, 8),),
-    "rows2": ((4, 6), (4, 5), (4, 2), (3, 9), (5, 6), (5, 5), (5, 2), (5, 12)),
-    "feat": ((0, 11), (0, 13), (4, 3), (5, 3)),
-    "half": ((1, 11), (1, 13), (3, 10), (4, 4), (4, 0), (4, 1), (5, 4), (5, 0), (5, 1)),
-    "end": ((2, 13), (4, 7), (4, 8), (4, 9), (5, 7), (5, 8), (5, 9), (3, 11), (4, 10), (5, 10))
-    + ((3, 13), (5, 13), (4, 11), (5, 11)),
+    "pairs": ((0, 9), (2, 8), (3, 7)),
+    "rows0": ((1, 9),),
+    "rows1": (),
+    "rows2": ((4, 6), (4, 5), (4, 2), (3, 8), (5, 6), (5, 5), (5, 2), (5, 11)),
+    "feat": ((0, 10), (0, 12), (4, 3), (5, 3)),
+    "half": ((1, 10), (1, 12), (3, 9), (4, 4), (4, 0), (4, 1), (5, 4), (5, 0), (5, 1)),
+    "end": ((2, 12), (4, 7), (4, 8), (5, 7), (5, 8), (3, 10), (4, 9), (5, 9))
+    + ((3, 12), (5, 12), (4, 10), (5, 10)),
 }
 
 
@@ -793,10 +792,10 @@
         def writer(which, cols):
             def write(value):
                 if which == 3:
-                    pair = cols[0] // 384
-                    for i in range(3):
+                    for here in range(0, cols[1], 128):
+                        pair, i = (cols[0] + here) // 384, (cols[0] + here) // 128 % 3
                         at = i * width + pair * 128
-                        summed[3][:, at : at + 128] = value[:, i * 128 : i * 128 + 128]
+                        summed[3][:, at : at + 128] = value[:, here : here + 128]
                 else:
                     summed[which][:, cols[0] : cols[0] + cols[1]] = value
 
@@ -1131,22 +1130,35 @@
     refs = list(refs)
     take = lambda count: [refs.pop(0) for _ in range(count)]
     sources, (small, late), targets = take(8), take(2), take(8)
-    vectors, sem = take(10), refs[0]
+    vectors, held, (sem_in, sem_out, sem_row) = take(10), take(8), refs
+    loads = [
+        pltpu.make_async_copy(source, hold, sem_in.at[i])
+        for i, (source, hold) in enumerate(zip(sources, held))
+    ]
     copies = [
-        pltpu.make_async_copy(source, target, sem.at[i])
-        for i, (source, target) in enumerate(zip(sources, targets))
+        pltpu.make_async_copy(hold, target, sem_out.at[i])
+        for i, (hold, target) in enumerate(zip(held, targets))
     ]
-    for copy in copies:
-        copy.start()
+    for load in loads:
+        load.start()
     places = ((late, 0), (late, 1), (small, 5), (small, 3), (small, 4), None)
     places += ((small, 2), (small, 0), (small, 1), (late, 2))
-    for vector, spot in zip(vectors, places):
-        if spot is None:
-            for i, (at, size) in enumerate(chunks(vector.shape[0], small.shape[1])):
-                vector[at : at + size] = small[6 + i, :size]
-        else:
-            vector[...] = spot[0][spot[1]]
-    for copy in copies:
+    rows = [(*spot, vector) for vector, spot in zip(vectors, places) if spot is not None]
+    pieces = [(ref.at[row], vector) for ref, row, vector in rows]
+    pieces += [
+        (small.at[6 + i, pl.ds(0, size)], vectors[5].at[pl.ds(at, size)])
+        for i, (at, size) in enumerate(chunks(vectors[5].shape[0], small.shape[1]))
+    ]
+    moves = [
+        pltpu.make_async_copy(source, target, sem_row.at[i])
+        for i, (source, target) in enumerate(pieces)
+    ]
+    for move in moves:
+        move.start()
+    for load, copy in zip(loads, copies):
+        load.wait()
+        copy.start()
+    for copy in moves + copies:
         copy.wait()
 
 
@@ -1158,9 +1170,10 @@
         finish_kernel,
         out_shape=tuple(shaped(a.shape, a.dtype) for a in large)
         + tuple(shaped((hidden if i == 5 else width,), f32) for i in range(10)),
-        in_specs=[vmem] * 10,
-        out_specs=(hbm,) * 8 + (vmem,) * 10,
-        scratch_shapes=[pltpu.SemaphoreType.DMA((8,))],
+        in_specs=[hbm] * 8 + [vmem] * 2,
+        out_specs=(hbm,) * 18,
+        scratch_shapes=[pltpu.VMEM(a.shape, a.dtype) for a in large]
+        + [pltpu.SemaphoreType.DMA((count,)) for count in (8, 8, 9 - (-hidden // width))],
         name="place_outputs",
     )(*large, small, late)
 

time: 172 us -> 169 us (0.983)
  Pallas kernels: 170 us -> 167 us
    pallas_call x1, Pallas kernels: 92.5 us -> 90 us  [forward_call(): pl.pallas_call(functools.partial(forward_kernel, fast), out_shape=outs, i...]
where the time goes in v6:
time: 169 us
  Pallas kernels  167 us (99%)
    pallas_call x1, Pallas kernels, forward_call(): pl.pallas_call(functools.partial(forward_kernel, fast), out_shape=outs, i...  90 us
    pallas_call x1, Pallas kernels, backward_call(): pl.pallas_call(functools.partial(backward_kernel, fast), out_shape=outs,...  72.9 us
    pallas_call x1, Pallas kernels, finish_call(): pl.pallas_call(finish_kernel, out_shape=tuple((shaped(a.shape, a.dtype) f...  4.49 us

profile of v6, /device:TPU:0, one launch (start us, length us, event | category | flops | bytes accessed | tf_op | source)
XLA Modules:
  0.0 168.9 jit_solution(2636422369084556713)
XLA Ops:
  1.3 90.0 %layer_forward.1 = (bf16[1280,512]{1,0:T(8,128)(2,1)}, bf16[1216,512]{1,0:T(8,128)(2,1)}, bf16[1216,512]{1,0:T(8,128)(2,1)}, bf16[1216,512]{1,0:T(8,128)(2,1)}, ...) custom-call(s32[1]{0:T(128)S(6)} %copy.37.refs_0_, ...), custom_call_target="tpu_custom_call" | custom-call | tf_op jit(solution)/shard_map/layer_forward/pallas_call | solution.py:674
  91.3 72.9 %layer_backward.1 = (bf16[1280,512]{1,0:T(8,128)(2,1)}, bf16[1280,512]{1,0:T(8,128)(2,1)}, f32[16,3200]{1,0:T(8,128)}, f32[16,3200]{1,0:T(8,128)}, f32[16,512]{1...) custom-call(s32[1]{0:T(128)S(6)} %copy.37.refs_0_, ...), custom_call_target="tpu_custom_call" | custom-call | tf_op jit(solution)/shard_map/layer_backward/pallas_call | solution.py:1114
  164.2 4.5 %place_outputs.1 = (bf16[1280,512]{1,0:T(8,128)(2,1)}, bf16[1280,512]{1,0:T(8,128)(2,1)}, bf16[1280,512]{1,0:T(8,128)(2,1)}, f32[16,1536]{1,0:T(8,128)}, f32[16,...) custom-call(bf16[1280,512]{1,0:T(8,128)(2,1)} %get-tuple-element.46., ...), custom_call_target="tpu_custom_call" | custom-call | tf_op jit(solution)/shard_map/place_outputs/pallas_call | solution.py:1169
